TPU v7x, 32 devices: a whole 2x2x4 slice. The times are simulated.
32 devices in a mesh: dp: 4 (over x, core), fsdp: 8 (over z, y).
Axes of the slice: x: 2, y: 2, z: 4, core: 2. Of those that a mesh axis runs over, the one named last changes fastest.
Arguments:
- tokens: bfloat16 [32768, 1024], P(('dp', 'fsdp')), may hold values from -6 to 6
- lengths: int32 [32, 16], P(('dp', 'fsdp')), may hold values from 0 to 1024, as said below
- buckets: int32 [32, 16], P(('dp', 'fsdp')), may hold values from 0 to 999
- w_mod: bfloat16 [1024, 4096], P('fsdp'), may hold values from -0.09375 to 0.09375
- b_mod: bfloat16 [4096], P('fsdp'), may hold values from -1.5 to 1.5
- w_qkv: bfloat16 [1024, 3072], P('fsdp'), may hold values from -0.25 to 0.25
- w_out: bfloat16 [1024, 1024], P('fsdp'), may hold values from -0.75 to 0.75
- b_out: bfloat16 [1024], P('fsdp'), may hold values from -1.5 to 1.5
- w_up: bfloat16 [1024, 4096], P('fsdp'), may hold values from -0.1875 to 0.1875
- b_up: bfloat16 [4096], P('fsdp'), may hold values from -2.5 to 2.5
- w_down: bfloat16 [4096, 1024], P('fsdp'), may hold values from -0.125 to 0.125
- b_down: bfloat16 [1024], P('fsdp'), may hold values from -1.5 to 1.5
- cotangent: bfloat16 [32768, 1024], P(('dp', 'fsdp')), may hold values from -6 to 6
Outputs:
- output: bfloat16 [32768, 1024], P(('dp', 'fsdp'))
- grad_tokens: float32 [32768, 1024], P(('dp', 'fsdp'))
- grad_w_mod: float32 [1024, 4096], P('fsdp')
- grad_b_mod: float32 [4096], P('fsdp')
- grad_w_qkv: float32 [1024, 3072], P('fsdp')
- grad_w_out: float32 [1024, 1024], P('fsdp')
- grad_b_out: float32 [1024], P('fsdp')
- grad_w_up: float32 [1024, 4096], P('fsdp')
- grad_b_up: float32 [4096], P('fsdp')
- grad_w_down: float32 [4096, 1024], P('fsdp')
- grad_b_down: float32 [1024], P('fsdp')
Inputs may be any that keep to these rules, and one draw needn't show every extreme that they name: `lengths`: each row lists one device's sequences in order: live entries are multiples of 64, empty slots hold 0 and follow the live ones; a row sums to between 512 and 1024, and the rows of tokens past that sum are padding. In every draw some device holds a single sequence of 1024. `buckets`: entries of empty slots are not used.
All inputs are finite; a program needn't handle non-finite values.
Results may differ from a plain program's by a relative error of at most 0.018.
Values may be sent and summed in bfloat16 or wider, within the bound.
A program may use at most 256 MiB of HBM per device.

v0:
```python
import math

import jax
import jax.numpy as jnp
from jax import lax
from jax.sharding import PartitionSpec as P

D = 1024
HEADS = 16
HEAD_DIM = 64


EPSILON = 1e-05
HIGHEST = lax.Precision.HIGHEST


def layout(lengths, tok_rows):
    seq_ends = jnp.cumsum(lengths, dtype=jnp.int32)
    position = jnp.arange(tok_rows, dtype=jnp.int32)
    segment = jnp.sum(
        (position[:, None] >= seq_ends[None, :]).astype(jnp.int32), axis=1, dtype=jnp.int32
    )
    slot_ids = jnp.arange(lengths.shape[0], dtype=jnp.int32)
    slot_table = (segment[:, None] == slot_ids[None, :]).astype(jnp.float32)
    live_rows = (segment < lengths.shape[0]).astype(jnp.float32)
    return (segment, live_rows, slot_table)


def time_features(buckets):
    half_width = D // 2
    frequency = jnp.exp(-math.log(10000.0) * jnp.arange(half_width, dtype=jnp.float32) / half_width)
    angles = buckets.astype(jnp.float32)[:, None] * frequency[None, :]
    return jnp.concatenate([jnp.sin(angles), jnp.cos(angles)], axis=1)


def normalize(values):
    centred = values - jnp.mean(values, axis=1, keepdims=True)
    inverse = lax.rsqrt(jnp.mean(centred * centred, axis=1, keepdims=True) + EPSILON)
    return (centred * inverse, inverse)


def norm_back(grad_normed, normed, inverse):
    first_mean = jnp.mean(grad_normed, axis=1, keepdims=True)
    second_mean = jnp.mean(grad_normed * normed, axis=1, keepdims=True)
    return inverse * (grad_normed - first_mean - normed * second_mean)


def group_size():
    return min(4, HEADS)


def split_heads(projected, pieces):
    tok_rows = projected.shape[0]
    shaped = projected.reshape(tok_rows, pieces, HEADS // group_size(), group_size(), HEAD_DIM)
    return jnp.transpose(shaped, (1, 2, 0, 3, 4))


def merge_heads(stacked):
    tok_rows = stacked.shape[2]
    return jnp.transpose(stacked, (2, 0, 1, 3, 4)).reshape(tok_rows, stacked.shape[0] * D)


def blocked(array, block_rows):
    return array.reshape((array.shape[0] // block_rows, block_rows) + array.shape[1:])


def masked_scores(query_block, key_rows, seg_block, segment):
    scores = jnp.einsum(
        "qnd,knd->nqk", query_block, key_rows, preferred_element_type=jnp.float32
    ) * HEAD_DIM ** (-0.5)
    allowed = seg_block[:, None] == segment[None, :]
    return jnp.where(allowed[None], scores, -1e30)


def attend_group(queries, key_rows, value_rows, segment):
    block_rows = min(512, queries.shape[0])

    def one_block(packed):
        query_block, seg_block = packed
        scores = masked_scores(query_block, key_rows, seg_block, segment)
        row_max = jnp.max(scores, axis=2, keepdims=True)
        exponent = jnp.exp(scores - row_max)
        row_total = jnp.sum(exponent, axis=2, keepdims=True)
        attn_probs = (exponent / row_total).astype(jnp.bfloat16)
        mixed = jnp.einsum(
            "nqk,knd->qnd", attn_probs, value_rows, preferred_element_type=jnp.float32
        )
        return (mixed, (row_max + jnp.log(row_total))[:, :, 0])

    mixed, log_total = lax.map(
        one_block, (blocked(queries, block_rows), blocked(segment, block_rows))
    )
    return (mixed.reshape(queries.shape), log_total)


def attend_back(queries, key_rows, value_rows, segment, log_total, grad_mixed):
    block_rows = min(512, queries.shape[0])
    scale_qk = HEAD_DIM ** (-0.5)

    def one_block(carry, packed):
        grad_keys, grad_values = carry
        query_block, seg_block, total_block, grad_block = packed
        scores = masked_scores(query_block, key_rows, seg_block, segment)
        attn_probs = jnp.exp(scores - total_block[:, :, None])
        grad_probs = jnp.einsum(
            "qnd,knd->nqk", grad_block, value_rows, preferred_element_type=jnp.float32
        )
        row_delta = jnp.sum(attn_probs * grad_probs, axis=2, keepdims=True)
        grad_scores = (attn_probs * (grad_probs - row_delta)).astype(jnp.bfloat16)
        grad_query = scale_qk * jnp.einsum(
            "nqk,knd->qnd", grad_scores, key_rows, preferred_element_type=jnp.float32
        )
        grad_keys = grad_keys + scale_qk * jnp.einsum(
            "nqk,qnd->knd", grad_scores, query_block, preferred_element_type=jnp.float32
        )
        grad_values = grad_values + jnp.einsum(
            "nqk,qnd->knd",
            attn_probs.astype(jnp.bfloat16),
            grad_block,
            preferred_element_type=jnp.float32,
        )
        return ((grad_keys, grad_values), grad_query)

    zero_rows = jnp.zeros(key_rows.shape, jnp.float32)
    carried, grad_query = lax.scan(
        one_block,
        (zero_rows, zero_rows),
        (
            blocked(queries, block_rows),
            blocked(segment, block_rows),
            log_total,
            blocked(grad_mixed, block_rows),
        ),
    )
    return (grad_query.reshape(queries.shape), carried[0], carried[1])


def local(
    tokens,
    lengths,
    buckets,
    w_mod,
    b_mod,
    w_qkv,
    w_out,
    b_out,
    w_up,
    b_up,
    w_down,
    b_down,
    cotangent,
):
    tok_rows = tokens.shape[0]
    full_mod, full_bmod, full_qkv, full_out, full_bout = (
        lax.all_gather(w_mod, "fsdp", axis=0, tiled=True),
        lax.all_gather(b_mod, "fsdp", axis=0, tiled=True),
        lax.all_gather(w_qkv, "fsdp", axis=0, tiled=True),
        lax.all_gather(w_out, "fsdp", axis=0, tiled=True),
        lax.all_gather(b_out, "fsdp", axis=0, tiled=True),
    )
    full_up, full_bup, full_down, full_bdown = (
        lax.all_gather(w_up, "fsdp", axis=0, tiled=True),
        lax.all_gather(b_up, "fsdp", axis=0, tiled=True),
        lax.all_gather(w_down, "fsdp", axis=0, tiled=True),
        lax.all_gather(b_down, "fsdp", axis=0, tiled=True),
    )
    segment, live_rows, slot_table = layout(lengths[0], tok_rows)
    live_col = live_rows[:, None]
    time_feats = time_features(buckets[0]).astype(jnp.bfloat16)
    modulation = jnp.dot(time_feats, full_mod, preferred_element_type=jnp.float32) + full_bmod
    per_row = jnp.dot(slot_table, modulation, precision=HIGHEST)
    scale_one = per_row[:, :D]
    shift_one = per_row[:, D : 2 * D]
    scale_two = per_row[:, 2 * D : 3 * D]
    shift_two = per_row[:, 3 * D :]
    inputs = tokens.astype(jnp.float32)
    normed_one, inverse_one = normalize(inputs)
    hidden_attn = (normed_one * (1.0 + scale_one) + shift_one).astype(jnp.bfloat16)
    projected = jnp.dot(hidden_attn, full_qkv, preferred_element_type=jnp.float32).astype(
        jnp.bfloat16
    )
    grouped = split_heads(projected, 3)
    attn_mixed, log_total = lax.map(
        lambda packed: attend_group(packed[0], packed[1], packed[2], segment),
        (grouped[0], grouped[1], grouped[2]),
    )
    attn_out = merge_heads(attn_mixed[None]).astype(jnp.bfloat16)
    branch_one = jnp.dot(attn_out, full_out, preferred_element_type=jnp.float32) + full_bout
    middle = inputs + live_col * branch_one
    normed_two, inverse_two = normalize(middle)
    hidden_mlp = (normed_two * (1.0 + scale_two) + shift_two).astype(jnp.bfloat16)
    up_pre = jnp.dot(hidden_mlp, full_up, preferred_element_type=jnp.float32) + full_bup
    up_act = jax.nn.gelu(up_pre).astype(jnp.bfloat16)
    branch_two = jnp.dot(up_act, full_down, preferred_element_type=jnp.float32) + full_bdown
    output = (middle + live_col * branch_two).astype(jnp.bfloat16)
    grad_res = cotangent.astype(jnp.float32)
    back_up, back_down = (
        lax.all_gather(w_up, "fsdp", axis=0, tiled=True),
        lax.all_gather(w_down, "fsdp", axis=0, tiled=True),
    )
    grad_two = (live_col * grad_res).astype(jnp.bfloat16)
    grad_w_down = jnp.einsum("rf,rd->fd", up_act, grad_two, preferred_element_type=jnp.float32)
    grad_b_down = jnp.sum(grad_two, axis=0, dtype=jnp.float32)
    grad_act = jnp.einsum("rd,fd->rf", grad_two, back_down, preferred_element_type=jnp.float32)
    gelu_value, gelu_back = jax.vjp(jax.nn.gelu, up_pre)
    grad_pre = gelu_back(grad_act)[0].astype(jnp.bfloat16)
    grad_w_up = jnp.einsum("rd,rf->df", hidden_mlp, grad_pre, preferred_element_type=jnp.float32)
    grad_b_up = jnp.sum(grad_pre, axis=0, dtype=jnp.float32)
    mlp_sums = (
        lax.psum_scatter(grad_w_up, "fsdp", scatter_dimension=0, tiled=True),
        lax.psum_scatter(grad_b_up, "fsdp", scatter_dimension=0, tiled=True),
        lax.psum_scatter(grad_w_down, "fsdp", scatter_dimension=0, tiled=True),
        lax.psum_scatter(grad_b_down, "fsdp", scatter_dimension=0, tiled=True),
    )
    grad_hidden_two = jnp.einsum("rf,df->rd", grad_pre, back_up, preferred_element_type=jnp.float32)
    grad_mid = grad_res + norm_back(grad_hidden_two * (1.0 + scale_two), normed_two, inverse_two)
    back_qkv, back_out = (
        lax.all_gather(w_qkv, "fsdp", axis=0, tiled=True),
        lax.all_gather(w_out, "fsdp", axis=0, tiled=True),
    )
    grad_one = (live_col * grad_mid).astype(jnp.bfloat16)
    grad_w_out = jnp.einsum("rd,re->de", attn_out, grad_one, preferred_element_type=jnp.float32)
    grad_b_out = jnp.sum(grad_one, axis=0, dtype=jnp.float32)
    grad_attn = jnp.einsum(
        "re,de->rd", grad_one, back_out, preferred_element_type=jnp.float32
    ).astype(jnp.bfloat16)
    grad_heads = split_heads(grad_attn, 1)[0]
    grad_query, grad_keys, grad_values = lax.map(
        lambda packed: attend_back(packed[0], packed[1], packed[2], segment, packed[3], packed[4]),
        (grouped[0], grouped[1], grouped[2], log_total, grad_heads),
    )
    grad_proj = merge_heads(jnp.stack([grad_query, grad_keys, grad_values])).astype(jnp.bfloat16)
    grad_w_qkv = jnp.einsum("rd,re->de", hidden_attn, grad_proj, preferred_element_type=jnp.float32)
    grad_hidden_one = jnp.einsum(
        "re,de->rd", grad_proj, back_qkv, preferred_element_type=jnp.float32
    )
    grad_tokens = grad_mid + norm_back(grad_hidden_one * (1.0 + scale_one), normed_one, inverse_one)
    row_terms = jnp.concatenate(
        [
            grad_hidden_one * normed_one,
            grad_hidden_one,
            grad_hidden_two * normed_two,
            grad_hidden_two,
        ],
        axis=1,
    )
    grad_mod = jnp.einsum("rs,rc->sc", slot_table, row_terms, precision=HIGHEST).astype(
        jnp.bfloat16
    )
    grad_w_mod = jnp.einsum("sd,sc->dc", time_feats, grad_mod, preferred_element_type=jnp.float32)
    grad_b_mod = jnp.sum(grad_mod, axis=0, dtype=jnp.float32)
    attn_sums = (
        lax.psum_scatter(grad_w_mod, "fsdp", scatter_dimension=0, tiled=True),
        lax.psum_scatter(grad_b_mod, "fsdp", scatter_dimension=0, tiled=True),
        lax.psum_scatter(grad_w_qkv, "fsdp", scatter_dimension=0, tiled=True),
        lax.psum_scatter(grad_w_out, "fsdp", scatter_dimension=0, tiled=True),
        lax.psum_scatter(grad_b_out, "fsdp", scatter_dimension=0, tiled=True),
    )
    totals = lax.psum(
        (
            attn_sums[0],
            attn_sums[1],
            attn_sums[2],
            attn_sums[3],
            attn_sums[4],
            mlp_sums[0],
            mlp_sums[1],
            mlp_sums[2],
            mlp_sums[3],
        ),
        "dp",
    )
    return (
        output,
        grad_tokens,
        totals[0],
        totals[1],
        totals[2],
        totals[3],
        totals[4],
        totals[5],
        totals[6],
        totals[7],
        totals[8],
    )


def solution(mesh):
    return jax.shard_map(
        local,
        mesh=mesh,
        in_specs=(
            P(("dp", "fsdp"), None),
            P(("dp", "fsdp"), None),
            P(("dp", "fsdp"), None),
            P("fsdp", None),
            P("fsdp"),
            P("fsdp", None),
            P("fsdp", None),
            P("fsdp"),
            P("fsdp", None),
            P("fsdp"),
            P("fsdp", None),
            P("fsdp"),
            P(("dp", "fsdp"), None),
        ),
        out_specs=(
            P(("dp", "fsdp"), None),
            P(("dp", "fsdp"), None),
            P("fsdp", None),
            P("fsdp"),
            P("fsdp", None),
            P("fsdp", None),
            P("fsdp"),
            P("fsdp", None),
            P("fsdp"),
            P("fsdp", None),
            P("fsdp"),
        ),
        check_vma=False,
    )
```

profile of v0, /device:TPU:0, one launch (start us, length us, event | category | flops | bytes accessed | tf_op | source)
XLA Modules:
  0.0 1998.6 jit_solution(8403924340936433734)
XLA Ops:
  12.3 22.3 %all-gather.1 = bf16[8,1,128]{2,1,0:T(2,128)(2,1)S(1)} all-gather(bf16[1,1,128]{2,1,0:T(2,128)(2,1)S(1)} %bitcast.228), channel_id=1, replica_groups=mesh['dp'=4,'fsdp'=8] {'fsdp'}, dimensions={0}, use_global_device_ids=true | all-gather | bytes 2304 | tf_op jit(solution)/shard_map/all_gather | solution.py:159
  36.3 26.4 %all-gather.2 = bf16[8,1,512]{2,1,0:T(2,128)(2,1)S(1)} all-gather(bf16[1,1,512]{2,1,0:T(2,128)(2,1)S(1)} %reshape.233), channel_id=1, replica_groups=mesh['dp'=4,'fsdp'=8] {'fsdp'}, dimensions={0}, use_global_device_ids=true | all-gather | bytes 9216 | tf_op jit(solution)/shard_map/all_gather | solution.py:163
  63.3 26.6 %all-gather = bf16[8,1,512]{2,1,0:T(2,128)(2,1)S(1)} all-gather(bf16[1,1,512]{2,1,0:T(2,128)(2,1)S(1)} %reshape.229), channel_id=1, replica_groups=mesh['dp'=4,'fsdp'=8] {'fsdp'}, dimensions={0}, use_global_device_ids=true | all-gather | bytes 9216 | tf_op jit(solution)/shard_map/all_gather | solution.py:156
  90.2 48.2 %all-gather.10.cloned.1.call-done = bf16[1024,4096]{1,0:T(8,128)(2,1)} async-done(((bf16[128,4096]{1,0:T(8,128)(2,1)}), bf16[1024,4096]{1,0:T(8,128)(2,1)}) %all-gather.10.cloned.1.call-update) | async-done | bytes 8388624 | tf_op jit(solution)/shard_map/all_gather | solution.py:155
  138.3 4.6 convolution_add_fusion
  142.9 6.9 fusion.77
  149.9 5.7 copy-done
  158.4 79.4 %all-gather.12.cloned.1.call-done = bf16[1024,3072]{1,0:T(8,128)(2,1)} async-done(((bf16[128,3072]{1,0:T(8,128)(2,1)}), bf16[1024,3072]{1,0:T(8,128)(2,1)}) %all-gather.12.cloned.1.call-update) | async-done | bytes 6291472 | tf_op jit(solution)/shard_map/all_gather | solution.py:157
  237.8 11.2 convolution_convert_fusion
  249.0 8.7 copy.81
  257.6 5.8 slice_bitcast_fusion
  265.0 81.9 %while.58 = (s32[]{:T(128)}, bf16[4,1024,4,64]{1,3,2,0:T(8,128)(2,1)}, f32[4,2,4,512]{3,2,1,0:T(4,128)S(1)}, bf16[4,1024,4,64]{1,3,2,0:T(8,128)(2,1)}, s32[1024]...) while((s32[]{:T(128)}, ...), condition=%wide.wide.region_9.10_spmd, body=%wide.wide.region_4.9_spmd.sunk | while | flops 562558976 | bytes 37595464 | solution.py:183
  267.9 15.4 while.61
  288.4 15.4 while.61
  308.9 15.4 while.61
  329.3 15.4 while.61
  347.0 5.8 fusion.94
  357.5 55.6 %all-gather.16.cloned.1.call-done = bf16[1024,4096]{1,0:T(8,128)(2,1)} async-done(((bf16[128,4096]{1,0:T(8,128)(2,1)}), bf16[1024,4096]{1,0:T(8,128)(2,1)}) %all-gather.16.cloned.1.call-update) | async-done | bytes 8388624 | tf_op jit(solution)/shard_map/all_gather | solution.py:162
  413.0 14.4 fusion.95
  427.4 110.7 %all-gather.18.cloned.1.call-done = bf16[4096,1024]{1,0:T(8,128)(2,1)} async-done(((bf16[512,1024]{1,0:T(8,128)(2,1)}), bf16[4096,1024]{1,0:T(8,128)(2,1)}) %all-gather.18.cloned.1.call-update) | async-done | bytes 8388624 | tf_op jit(solution)/shard_map/all_gather | solution.py:164
  538.1 26.9 %convert_reduce_fusion = (f32[4096]{0:T(1024)}, bf16[1024,4096]{1,0:T(8,128)(2,1)}) fusion(f32[1024,4096]{1,0:T(8,128)} %fusion.95, f32[4096]{0:T(1024)S(1)} %bitcast.222, bf16[4096,1024]{1,0:T(8,128)(2,1)} %all-gather.18.cloned.1.call-done, bf16[1024,1024]{1,0:T(8,128)(2,1)} %param.33, f32[1024]{0:T(1024)S(1)} %copy-done.40), kind=kOutput, calls=%fused_computation.80 | convolution fusion | flops 8689545216 | bytes 35688448 | tf_op jit(solution)/shard_map/rd,fd->rf/dot_general | solution.py:204
  565.0 15.5 fusion.92
  580.6 8.2 convert_reduce_fusion.3
  590.2 4.3 fusion.97
  596.1 5.3 convolution_convert_fusion.1
  606.1 142.4 %while.60 = (s32[]{:T(128)}, bf16[4,1024,4,64]{1,3,2,0:T(8,128)(2,1)}, bf16[4,1024,4,64]{1,3,2,0:T(8,128)(2,1)}, bf16[4,1024,4,64]{1,3,2,0:T(8,128)(2,1)}, bf16[...) while((s32[]{:T(128)}, ...), condition=%wide.wide.region_18.19_spmd, body=%wide.wide.region_14.18_spmd.sunk | while | flops 1375598592 | bytes 100764216 | solution.py:228
  611.8 24.7 %while.62 = (s32[]{:T(128)}, f32[1024,4,64]{0,2,1:T(8,128)S(1)}, f32[1024,4,64]{0,2,1:T(8,128)}, bf16[2,512,4,64]{1,3,2,0:T(8,128)(2,1)}, bf16[2,512,4,64]{1,3,2...) while((s32[]{:T(128)}, f32[1024,4,64]{0,2,1:T(8,128)S(1)}, ...), condition=%wide.region_17.17_spmd.clone, body=%wide.region_15.16_spmd.clone.sunk | while | flops 1375598592 | bytes 85002520 | solution.py:125
  647.3 24.8 %while.62 = (s32[]{:T(128)}, f32[1024,4,64]{0,2,1:T(8,128)S(1)}, f32[1024,4,64]{0,2,1:T(8,128)}, bf16[2,512,4,64]{1,3,2,0:T(8,128)(2,1)}, bf16[2,512,4,64]{1,3,2...) while((s32[]{:T(128)}, f32[1024,4,64]{0,2,1:T(8,128)S(1)}, ...), condition=%wide.region_17.17_spmd.clone, body=%wide.region_15.16_spmd.clone.sunk | while | flops 1375598592 | bytes 85002520 | solution.py:125
  682.9 24.7 %while.62 = (s32[]{:T(128)}, f32[1024,4,64]{0,2,1:T(8,128)S(1)}, f32[1024,4,64]{0,2,1:T(8,128)}, bf16[2,512,4,64]{1,3,2,0:T(8,128)(2,1)}, bf16[2,512,4,64]{1,3,2...) while((s32[]{:T(128)}, f32[1024,4,64]{0,2,1:T(8,128)S(1)}, ...), condition=%wide.region_17.17_spmd.clone, body=%wide.region_15.16_spmd.clone.sunk | while | flops 1375598592 | bytes 85002520 | solution.py:125
  718.4 24.7 %while.62 = (s32[]{:T(128)}, f32[1024,4,64]{0,2,1:T(8,128)S(1)}, f32[1024,4,64]{0,2,1:T(8,128)}, bf16[2,512,4,64]{1,3,2,0:T(8,128)(2,1)}, bf16[2,512,4,64]{1,3,2...) while((s32[]{:T(128)}, f32[1024,4,64]{0,2,1:T(8,128)S(1)}, ...), condition=%wide.region_17.17_spmd.clone, body=%wide.region_15.16_spmd.clone.sunk | while | flops 1375598592 | bytes 85002520 | solution.py:125
  748.6 3.7 pad_maximum_fusion
  754.9 9.3 fusion.96
  765.8 20.3 %fusion.86 = f32[4096,1024]{1,0:T(8,128)} fusion(bf16[1024,1024]{1,0:T(8,128)(2,1)S(1)} %copy-done.21, f32[1024]{0:T(1024)S(1)} %copy-done.41, f32[1024,4096]{1,0:T(8,128)} %fusion.95, f32[4096]{0:T(1024)S(1)} %bitcast.223), kind=kOutput, calls=%fused_computation.153 | convolution fusion | flops 8635023360 | bytes 35672064 | tf_op jit(solution)/shard_map/rf,rd->fd/dot_general | solution.py:202
  787.8 14.6 fusion.98
  804.0 13.6 fusion.93
  817.7 4.9 fusion.58
  822.5 7.6 convert_reduce_fusion.4
  830.2 8.1 fusion.82
  838.4 131.4 %reduce-scatter.8.cloned.1.call-done = f32[128,3072]{1,0:T(8,128)} async-done(((f32[1024,3072]{1,0:T(8,128)}), f32[128,3072]{1,0:T(8,128)}) %reduce-scatter.8.cloned.1.call-update) | async-done | bytes 1572880 | tf_op jit(solution)/shard_map/reduce_scatter | solution.py:255
  969.7 286.0 %reduce-scatter.14.cloned.1.call-done = f32[512,1024]{1,0:T(8,128)} async-done(((f32[4096,1024]{1,0:T(8,128)}), f32[512,1024]{1,0:T(8,128)}) %reduce-scatter.14.cloned.1.call-update) | async-done | bytes 2097168 | tf_op jit(solution)/shard_map/reduce_scatter | solution.py:212
  1255.8 285.5 %reduce-scatter.12.cloned.1.call-done = f32[128,4096]{1,0:T(8,128)} async-done(((f32[1024,4096]{1,0:T(8,128)}), f32[128,4096]{1,0:T(8,128)}) %reduce-scatter.12.cloned.1.call-update) | async-done | bytes 2097168 | tf_op jit(solution)/shard_map/reduce_scatter | solution.py:210
  1541.3 285.9 %reduce-scatter.6.cloned.1.call-done = f32[128,4096]{1,0:T(8,128)} async-done(((f32[1024,4096]{1,0:T(8,128)}), f32[128,4096]{1,0:T(8,128)}) %reduce-scatter.6.cloned.1.call-update) | async-done | bytes 2097168 | tf_op jit(solution)/shard_map/reduce_scatter | solution.py:253
  1829.8 18.5 all-gather.3
  1848.3 33.4 %all-reduce.4 = (f32[4096]{0:T(1024)S(1)}, f32[1024]{0:T(1024)S(1)}, f32[4096]{0:T(1024)S(1)}, f32[1024]{0:T(1024)S(1)}) all-reduce(f32[4096]{0:T(1024)S(1)} %get-tuple-element.456, f32[1024]{0:T(1024)S(1)} %copy-done.38, f32[4096]{0:T(1024)S(1)} %copy-done.37, f32[1024]{0:T(1024)S(1)} %copy-done.39), channel_id=3, replica_groups=mesh['dp'=4,'fsdp'=8] {'fsdp'}, use_global_device_ids=true, to_apply=%region_24.25.clone | all-reduce | flops 10240 | bytes 81920
  1882.0 7.6 all-reduce.5
  1889.6 18.4 add_convert_fusion
  1908.0 75.8 %all-reduce.9.cloned.1.call-done = (f32[128,4096]{1,0:T(8,128)}, f32[128,3072]{1,0:T(8,128)}, f32[128,1024]{1,0:T(8,128)}, f32[128,4096]{1,0:T(8,128)}, f32[512,1024]{1,0:T(8,128)}) async-done(((f32[128,4096]{1,0:T(8,128)}, f32[128,3072]{1,0:T(8,128)}, f32[128,1024]{1,0:T(8,128)}, f32[128,4096]{1,0:T(8,128)}, f32[512,1024]{1,0:T(8,128)}), (f32[128,4096]{1,0:T(8,128)}, f32[128,3072]{1,0:T(8,128)}, ...) | async-done | bytes 8388624 | tf_op jit(solution)/shard_map/psum | solution.py:259
  1983.8 3.3 copy.192
  (445 shorter events, 259.7 us)
Async XLA Ops:
  7.2 3.5 copy-start.45
  7.2 5.0 copy-start.48
  7.2 5.0 copy-start.43
  7.2 5.0 copy-start.44
  7.2 5.1 copy-start.46
  7.2 28.0 %copy-start.4 = (bf16[1024,1024]{1,0:T(8,128)(2,1)S(1)}, bf16[1024,1024]{1,0:T(8,128)(2,1)}, u32[]{:S(2)}) copy-start(bf16[1024,1024]{1,0:T(8,128)(2,1)} %param.21) | copy-start | bytes 6291460
  7.2 131.1 %all-gather.10.cloned.1.call-start = ((), (), s32[]{:S(2)}) async-start(), calls=%async_computation.5 | async-start | bytes 9437184 | tf_op jit(solution)/shard_map/all_gather | solution.py:155
  8.0 229.8 %all-gather.12.cloned.1.call-start = ((), (), s32[]{:S(2)}) async-start(), calls=%async_computation.6 | async-start | bytes 7077888 | tf_op jit(solution)/shard_map/all_gather | solution.py:157
  8.7 338.2 %all-gather.14.cloned.1.call-start = ((), (), s32[]{:S(2)}) async-start(), calls=%async_computation.7 | async-start | bytes 2359296 | tf_op jit(solution)/shard_map/all_gather | solution.py:158
  9.5 403.6 %all-gather.16.cloned.1.call-start = ((), (), s32[]{:S(2)}) async-start(), calls=%async_computation.8 | async-start | bytes 9437184 | tf_op jit(solution)/shard_map/all_gather | solution.py:162
  10.0 528.1 %all-gather.18.cloned.1.call-start = ((), (), s32[]{:S(2)}) async-start(), calls=%async_computation.9 | async-start | bytes 9437184 | tf_op jit(solution)/shard_map/all_gather | solution.py:164
  10.6 827.8 %reduce-scatter.10.cloned.1.call-start = ((), (), s32[]{:S(2)}) async-start(), calls=%async_computation.12 | async-start | bytes 4718592 | tf_op jit(solution)/shard_map/reduce_scatter | solution.py:256
  35.6 114.3 %copy-start.31 = (f32[1024]{0:T(1024)}, f32[1024]{0:T(1024)S(1)}, u32[]{:S(2)}) copy-start(f32[1024]{0:T(1024)S(1)} %broadcast_multiply_fusion.5) | copy-start | bytes 12292
  36.3 113.6 %copy-start.33 = (f32[1024]{0:T(1024)}, f32[1024]{0:T(1024)S(1)}, u32[]{:S(2)}) copy-start(f32[1024]{0:T(1024)S(1)} %add_rsqrt_fusion.1) | copy-start | bytes 12292
  90.1 52.8 %copy-start.27 = (bf16[16,512]{1,0:T(8,128)(2,1)}, bf16[16,512]{1,0:T(8,128)(2,1)S(1)}, u32[]{:S(2)}) copy-start(bf16[16,512]{1,0:T(8,128)(2,1)S(1)} %get-tuple-element.450) | copy-start | bytes 49156
  90.2 52.8 %copy-start.29 = (bf16[16,512]{1,0:T(8,128)(2,1)}, bf16[16,512]{1,0:T(8,128)(2,1)S(1)}, u32[]{:S(2)}) copy-start(bf16[16,512]{1,0:T(8,128)(2,1)S(1)} %get-tuple-element.451) | copy-start | bytes 49156
  149.9 5.7 copy-start
  265.0 81.9 %copy-start.40 = (f32[1024]{0:T(1024)S(1)}, f32[1024]{0:T(1024)}, u32[]{:S(2)}) copy-start(f32[1024]{0:T(1024)} %compare_convert_fusion) | copy-start | bytes 12292
  265.0 81.9 %copy-start.42 = (f32[8,1,128]{2,1,0:T(1,128)S(1)}, f32[8,1,128]{2,1,0:T(1,128)}, u32[]{:S(2)}) copy-start(f32[8,1,128]{2,1,0:T(1,128)} %convert_element_type.141) | copy-start | bytes 12292
  347.0 9.2 copy-start.1
  357.5 70.0 %copy-start.14 = (bf16[1024,1024]{1,0:T(8,128)(2,1)}, bf16[1024,1024]{1,0:T(8,128)(2,1)S(1)}, u32[]{:S(2)}) copy-start(bf16[1024,1024]{1,0:T(8,128)(2,1)S(1)} %fusion.73) | copy-start | bytes 6291460
  357.5 180.7 %copy-start.35 = (f32[8,1,512]{2,1,0:T(1,128)S(1)}, f32[8,1,512]{2,1,0:T(1,128)}, u32[]{:S(2)}) copy-start(f32[8,1,512]{2,1,0:T(1,128)} %convert_element_type.142) | copy-start | bytes 49156
  538.1 26.9 %copy-start.3 = (f32[1024,1024]{1,0:T(8,128)S(1)}, f32[1024,1024]{1,0:T(8,128)}, u32[]{:S(2)}) copy-start(f32[1024,1024]{1,0:T(8,128)} %copy-done.2) | copy-start | bytes 12582916
  565.0 15.5 copy-start.20
  580.5 8.3 copy-start.12
  580.6 9.6 copy-start.16
  594.5 375.2 %reduce-scatter.8.cloned.1.call-start = ((), (), s32[]{:S(2)}) async-start(), calls=%async_computation.11 | async-start | bytes 14155776 | tf_op jit(solution)/shard_map/reduce_scatter | solution.py:255
  601.4 4.7 copy-start.25
  616.1 3.2 copy-start.7
  628.5 3.2 copy-start.7
  651.6 3.2 copy-start.7
  664.1 3.2 copy-start.7
  748.6 6.4 copy-start.19
  764.3 491.5 %reduce-scatter.14.cloned.1.call-start = ((), (), s32[]{:S(2)}) async-start(), calls=%async_computation.14 | async-start | bytes 18874368 | tf_op jit(solution)/shard_map/reduce_scatter | solution.py:212
  786.2 755.1 %reduce-scatter.12.cloned.1.call-start = ((), (), s32[]{:S(2)}) async-start(), calls=%async_computation.13 | async-start | bytes 18874368 | tf_op jit(solution)/shard_map/reduce_scatter | solution.py:210
  802.4 1024.9 %reduce-scatter.6.cloned.1.call-start = ((), (), s32[]{:S(2)}) async-start(), calls=%async_computation.10 | async-start | bytes 18874368 | tf_op jit(solution)/shard_map/reduce_scatter | solution.py:253
  804.0 13.7 copy-start.8
  817.6 4.9 copy-start.13
  822.5 7.6 copy-start.28
  822.5 7.7 copy-start.30
  838.3 1145.5 %all-reduce.9.cloned.1.call-start = ((), (), s32[]{:S(2)}) async-start(), calls=%async_computation.15 | async-start | bytes 16777216 | tf_op jit(solution)/shard_map/psum | solution.py:259
  1827.3 21.0 %copy-start.37 = (f32[4096]{0:T(1024)S(1)}, f32[4096]{0:T(1024)}, u32[]{:S(2)}) copy-start(f32[4096]{0:T(1024)} %get-tuple-element.458) | copy-start | bytes 49156
  1827.3 21.0 %copy-start.38 = (f32[1024]{0:T(1024)S(1)}, f32[1024]{0:T(1024)}, u32[]{:S(2)}) copy-start(f32[1024]{0:T(1024)} %get-tuple-element.432) | copy-start | bytes 12292
  1827.3 21.1 %copy-start.39 = (f32[1024]{0:T(1024)S(1)}, f32[1024]{0:T(1024)}, u32[]{:S(2)}) copy-start(f32[1024]{0:T(1024)} %get-tuple-element.449) | copy-start | bytes 12292
  1983.8 3.3 copy-start.24
  1983.8 4.4 copy-start.26
  1983.8 5.2 copy-start.18
  1987.1 3.3 copy-start.17
  (41 other events, 72.6 us)
Sparse Core Ops, SparseCore 0:
  10.2 128.0 all-gather.9
  140.5 97.2 all-gather.11
  239.9 47.6 all-gather.13
  289.5 123.4 all-gather.15
  415.0 123.0 all-gather.17
  594.7 86.2 reduce-scatter.9
  764.4 205.3 reduce-scatter.7
  974.0 281.7 reduce-scatter.13
  1259.6 281.7 reduce-scatter.11
  1545.4 281.7 reduce-scatter.5
  1830.2 153.5 all-reduce.8
where the time goes:
time: 2010 us; the launch traced here: 2000 us
  waiting for transfers between devices  1360 us (68%)
  matrix products  301 us (15%)
  blocking collectives  135 us (7%)
  local copies, waits for them, and re-layouts  113 us (6%)
  other arithmetic  69 us (3%)
    reduce_scatter x1, waiting for transfers between devices, local(): lax.psum_scatter(grad_w_down, 'fsdp', scatter_dimension=0, tiled=True)  286 us
    reduce_scatter x1, waiting for transfers between devices, local(): lax.psum_scatter(grad_w_mod, 'fsdp', scatter_dimension=0, tiled=True)  286 us
    reduce_scatter x1, waiting for transfers between devices, local(): lax.psum_scatter(grad_w_up, 'fsdp', scatter_dimension=0, tiled=True)  286 us
    reduce_scatter x1, waiting for transfers between devices, local(): lax.psum_scatter(grad_w_qkv, 'fsdp', scatter_dimension=0, tiled=True)  131 us
    all_gather x1, waiting for transfers between devices, local(): lax.all_gather(w_down, 'fsdp', axis=0, tiled=True)  111 us
    all_gather x1, waiting for transfers between devices, local(): lax.all_gather(w_qkv, 'fsdp', axis=0, tiled=True)  79.4 us
    psum x1, waiting for transfers between devices, local(): lax.psum((attn_sums[0], attn_sums[1], attn_sums[2], attn_sums[3], attn_su...  75.8 us
    all_gather x1, waiting for transfers between devices, local(): lax.all_gather(w_up, 'fsdp', axis=0, tiled=True)  55.6 us
  transfers between devices with their start and end apart: 11, of which 9 were waited for; matrix products, arithmetic and copies ran while one was open for 20% of the time, Pallas kernels for 0%

commit v1 on v0

v1 whole, which is shorter than its diff:
```python
import functools
import math

import jax
import jax.numpy as jnp
from jax import lax
from jax.experimental import pallas as pl
from jax.experimental.pallas import tpu as pltpu
from jax.sharding import PartitionSpec as P

D = 1024
HEADS = 16
HEAD_DIM = 64
EPSILON = 1e-05
UNIT = 64
ROWS = 512
ROWS_F = 512
ROWS_B = 512
FF_BLOCK = 512
LSE_LANE = 24
VMEM_LIMIT = 62 * 2**20
HIGHEST = lax.Precision.HIGHEST
MESH = pl.DeviceIdType.MESH


def layout(lengths, tok_rows):
    slots = lengths.shape[0]
    upto = jnp.arange(slots)[:, None] <= jnp.arange(slots)[None, :]
    seq_ends = jnp.sum(jnp.where(upto, lengths[:, None], 0), axis=0, dtype=jnp.int32)
    position = jnp.arange(0, tok_rows, UNIT, dtype=jnp.int32)
    segment = jnp.sum((position[:, None] >= seq_ends[None, :]).astype(jnp.int32), axis=1, dtype=jnp.int32)
    unit_table = (segment[:, None] == jnp.arange(slots, dtype=jnp.int32)[None, :]).astype(jnp.float32)
    return segment, (segment < slots).astype(jnp.float32), unit_table


def time_features(buckets):
    half_width = D // 2
    frequency = jnp.exp(-math.log(10000.0) * jnp.arange(half_width, dtype=jnp.float32) / half_width)
    angles = buckets.astype(jnp.float32)[:, None] * frequency[None, :]
    return jnp.concatenate([jnp.sin(angles), jnp.cos(angles)], axis=1)


def place():
    dp, fsdp = lax.axis_index("dp"), lax.axis_index("fsdp")
    return dp // 2, dp % 2, fsdp // 2, fsdp % 2


def device(x, core, z, y):
    return (x * 2 + core, z * 2 + y)


class Links:
    def __init__(self, send_sems, recv_sems):
        self.send_sems, self.recv_sems, self.used, self.begun = send_sems, recv_sems, 0, []

    def copy(self, src, dst, target):
        slot = self.used
        self.used += 1
        made = pltpu.make_async_remote_copy(
            src_ref=src,
            dst_ref=dst,
            send_sem=self.send_sems.at[slot],
            recv_sem=self.recv_sems.at[slot],
            device_id=target,
            device_id_type=MESH,
        )
        made.start()
        self.begun.append(made)
        return made

    def drain(self):
        for made in self.begun:
            made.wait_send()


def split(extent, unit, share):
    half = extent // 2
    outer = int(half * share / 2) // unit * unit
    return half, outer, half - 2 * outer


def cut(ref, block, rows, axis, start, width):
    if axis == 0:
        first = pl.multiple_of(block * rows + start, 16)
        return ref.at[pl.ds(first, width), :]
    return ref.at[pl.ds(pl.multiple_of(block * rows, 16), rows), pl.ds(pl.multiple_of(start, 128), width)]


def gather_one(shard, whole, links, me, base, extent):
    x, core, z, y = me
    rows = shard.shape[0]
    axis = 1 if shard.shape[1] > rows * 2 else 0
    half, outer, inner = split(extent, 128 if axis else 16, 0.75)
    own = (base + core * half + x * outer, outer + inner)
    crossing = (base + core * half + x * (outer + inner), outer)
    full = (base + core * half, half)
    mine = z * 2 + y

    def part(block, piece):
        return cut(whole, block, rows, axis, *piece)

    first = cut(shard, 0, rows, axis, *own)
    along_z = [None] + [
        links.copy(first, part(mine, own), device(x, core, (z + k) % 4, y)) for k in (1, 2, 3)
    ]
    along_y = [links.copy(first, part(mine, own), device(x, core, z, 1 - y))]
    yield
    order = [("z", 1), ("y", 0), ("z", 2), ("y", 1), ("z", 3), ("y", 2), ("y", 3)]
    crossed, handed = [], []

    def hand_on(j):
        crossed[j][1].wait_recv()
        block = crossed[j][0]
        handed.append(links.copy(part(block, full), part(block, full), device(x, 1 - core, z, y)))

    for j, (way, k) in enumerate(order):
        source_z = (z - k + 4) % 4
        if way == "z":
            block = source_z * 2 + y
            along_z[k].wait_recv()
            along_y.append(links.copy(part(block, own), part(block, own), device(x, core, z, 1 - y)))
        else:
            block = source_z * 2 + 1 - y
            along_y[k].wait_recv()
        crossed.append((block, links.copy(part(block, crossing), part(block, crossing), device(1 - x, core, z, y))))
        if j >= 2:
            hand_on(j - 2)
        yield
    hand_on(5)
    yield
    hand_on(6)
    yield
    for made in handed:
        made.wait_recv()
    yield


GATHER_COPIES = 21


def take_turns(parts):
    parts = list(parts)
    while parts:
        left = []
        for one in parts:
            try:
                next(one)
                left.append(one)
            except StopIteration:
                pass
        parts = left


def staggered(parts, every):
    parts = list(parts)
    turn, active = 0, []
    while parts or active:
        if parts and turn % every == 0:
            active.append(parts.pop(0))
        left = []
        for one in active:
            try:
                next(one)
                left.append(one)
            except StopIteration:
                pass
        active = left
        turn += 1


EVERY = 3


def pieces_of(shape):
    along = shape[1] if shape[1] > shape[0] * 2 else shape[0]
    count = 2 if shape[0] * shape[1] > 2**18 else 1
    return [(i * along // count, along // count) for i in range(count)]


def exchange_small(small, small_all, links, local_sem, me):
    x, core, z, y = me
    number = (x * 2 + core) * 8 + z * 2 + y
    keep = pltpu.make_async_copy(small.at[z * 2 + y], small_all.at[number], local_sem)
    keep.start()
    few = []
    for k in range(1, 32):
        to = (number + k) % 32
        few.append(links.copy(small.at[to % 8], small_all.at[number], (to // 8, to % 8)))
    return keep, few


def gather_kernel(count, *refs):
    small, shards, small_all, wholes = refs[0], refs[1 : 1 + count], refs[1 + count], refs[2 + count : 2 + 2 * count]
    send_sems, recv_sems, local_sems = refs[2 + 2 * count :]
    me = place()
    x, core, z, y = me
    links = Links(send_sems, recv_sems)
    mine = z * 2 + y
    keep, few = exchange_small(small, small_all, links, local_sems.at[count], me)
    kept = []
    for i in range(count):
        rows = shards[i].shape[0]
        kept.append(pltpu.make_async_copy(shards[i], wholes[i].at[pl.ds(pl.multiple_of(mine * rows, 16), rows), :], local_sems.at[i]))
    parts = [
        gather_one(shards[i], wholes[i], links, me, base, extent) for i in range(count) for base, extent in pieces_of(shards[i].shape)
    ]
    for made in kept:
        made.start()
    staggered(parts, EVERY)
    for made in kept:
        made.wait()
    for made in few:
        made.wait_recv()
    keep.wait()
    links.drain()


def gather_all(small, shards):
    count = len(shards)
    copies = 31 + GATHER_COPIES * sum(len(pieces_of(s.shape)) for s in shards)
    out = pl.pallas_call(
        functools.partial(gather_kernel, count),
        out_shape=[jax.ShapeDtypeStruct((32,) + small.shape[1:], small.dtype)]
        + [jax.ShapeDtypeStruct((8 * s.shape[0], s.shape[1]), s.dtype) for s in shards],
        in_specs=[pl.BlockSpec(memory_space=pl.ANY)] * (1 + count),
        out_specs=[pl.BlockSpec(memory_space=pl.ANY)] * (1 + count),
        scratch_shapes=[
            pltpu.SemaphoreType.DMA((copies,)),
            pltpu.SemaphoreType.DMA((copies,)),
            pltpu.SemaphoreType.DMA((count + 1,)),
        ],
        compiler_params=pltpu.CompilerParams(has_side_effects=True),
    )(small, *shards)
    return out[0], out[1:]


def reduce_buffers(shape):
    rows, width = shape[0] // 8, shape[1]
    axis = 1 if width > rows * 2 else 0
    half, outer, inner = split((rows, width)[axis], 128 if axis else 16, 0.5)

    def sized(extent):
        return (extent, width) if axis == 0 else (rows, extent)

    return [
        (8,) + sized(half),
        (8,) + sized(outer),
        (4,) + sized(outer + inner),
        (4,) + sized(outer + inner),
        sized(outer + inner),
    ]


def reduce_one(local, result, lands, links, me):
    x, core, z, y = me
    from_core, from_x, from_y, from_z, from_last = lands
    rows, width = local.shape[0] // 8, local.shape[1]
    axis = 1 if width > rows * 2 else 0
    half, outer, inner = split((rows, width)[axis], 128 if axis else 16, 0.5)
    own = (core * half + x * outer, outer + inner)
    crossing = (core * half + (1 - x) * (outer + inner), outer)
    kept = (core * half + x * (outer + inner), outer)

    def part(block, piece):
        return cut(local, block, rows, axis, *piece)

    def add(block, piece, landed):
        ref = part(block, piece)
        ref[...] = (ref[...].astype(jnp.float32) + landed[...].astype(jnp.float32)).astype(local.dtype)

    blocks = [((z + k) % 4) * 2 for k in (1, 2, 3, 0)]
    by_core = [
        [links.copy(part(b + o, ((1 - core) * half, half)), from_core.at[2 * t + o], device(x, 1 - core, z, y)) for o in (0, 1)]
        for t, b in enumerate(blocks)
    ]
    yield
    by_x, by_y, by_z = [], [], []
    for t in range(7):
        if t < 4:
            for o in (0, 1):
                by_core[t][o].wait_recv()
                add(blocks[t] + o, (core * half, half), from_core.at[2 * t + o])
            by_x.append([
                links.copy(part(blocks[t] + o, crossing), from_x.at[2 * t + o], device(1 - x, core, z, y)) for o in (0, 1)
            ])
        if 1 <= t < 5:
            for o in (0, 1):
                by_x[t - 1][o].wait_recv()
                add(blocks[t - 1] + o, kept, from_x.at[2 * (t - 1) + o])
            by_y.append(links.copy(part(blocks[t - 1] + 1 - y, own), from_y.at[t - 1], device(x, core, z, 1 - y)))
        if 2 <= t < 6:
            by_y[t - 2].wait_recv()
            add(blocks[t - 2] + y, own, from_y.at[t - 2])
            if t - 2 < 3:
                by_z.append(links.copy(part(blocks[t - 2] + y, own), from_z.at[t - 2], device(x, core, (z + t - 1) % 4, y)))
        yield
    mine = part(z * 2 + y, own)
    total = mine[...].astype(jnp.float32)
    for k in range(3):
        by_z[k].wait_recv()
        total = total + from_z[k].astype(jnp.float32)
    mine[...] = total.astype(local.dtype)
    last = links.copy(mine, from_last, device(1 - x, core, z, y))
    yield
    last.wait_recv()

    def place_in(start, size):
        if axis == 0:
            return result.at[pl.ds(pl.multiple_of(core * half + start, 16), size), :]
        return result.at[:, pl.ds(pl.multiple_of(core * half + start, 128), size)]

    def inside(ref, start, size):
        return ref.at[pl.ds(start, size), :] if axis == 0 else ref.at[:, pl.ds(start, size)]

    whole_own = cut(local, z * 2 + y, rows, axis, core * half, half)
    for plane in (0, 1):

        @pl.when(x == plane)
        def _():
            if plane == 0:
                a_mine, b_mine = inside(whole_own, 0, outer), inside(whole_own, outer, inner)
                b_other, a_other = inside(from_last, 0, inner), inside(from_last, inner, outer)
            else:
                b_mine, a_mine = inside(whole_own, outer, inner), inside(whole_own, outer + inner, outer)
                a_other, b_other = inside(from_last, 0, outer), inside(from_last, outer, inner)
            place_in(plane * (outer + inner), outer)[...] = a_mine[...]
            place_in((1 - plane) * (outer + inner), outer)[...] = a_other[...]
            place_in(outer, inner)[...] = (
                b_mine[...].astype(jnp.float32) + b_other[...].astype(jnp.float32)
            ).astype(result.dtype)

    final = links.copy(place_in(0, half), place_in(0, half), device(x, 1 - core, z, y))
    yield
    final.wait_recv()
    yield


REDUCE_COPIES = 8 + 8 + 4 + 3 + 1 + 1


def reduce_kernel(count, smalls, *refs):
    locals_, refs = refs[:count], refs[count:]
    small, refs = refs[:smalls], refs[smalls:]
    results, refs = refs[:count], refs[count:]
    small_all, refs = refs[:smalls], refs[smalls:]
    lands = refs[: 5 * count]
    send_sems, recv_sems, local_sems = refs[5 * count :]
    me = place()
    links = Links(send_sems, recv_sems)
    waiting = [exchange_small(small[i], small_all[i], links, local_sems.at[i], me) for i in range(smalls)]
    parts = [reduce_one(locals_[i], results[i], lands[5 * i : 5 * i + 5], links, me) for i in range(count)]
    take_turns(parts)
    for keep, few in waiting:
        for made in few:
            made.wait_recv()
        keep.wait()
    links.drain()


def reduce_all(grads, small=()):
    count, smalls = len(grads), len(small)
    lands = [pltpu.VMEM(s, jnp.bfloat16) for g in grads for s in reduce_buffers(g.shape)]
    copies = REDUCE_COPIES * count + 31 * smalls
    out = pl.pallas_call(
        functools.partial(reduce_kernel, count, smalls),
        out_shape=[jax.ShapeDtypeStruct((g.shape[0] // 8, g.shape[1]), g.dtype) for g in grads]
        + [jax.ShapeDtypeStruct((32,) + s.shape[1:], s.dtype) for s in small],
        in_specs=[pl.BlockSpec(memory_space=pltpu.VMEM)] * (count + smalls),
        out_specs=[pl.BlockSpec(memory_space=pltpu.VMEM)] * (count + smalls),
        scratch_shapes=lands
        + [pltpu.SemaphoreType.DMA((copies,)), pltpu.SemaphoreType.DMA((copies,)), pltpu.SemaphoreType.DMA((max(smalls, 1),))],
        compiler_params=pltpu.CompilerParams(has_side_effects=True, vmem_limit_bytes=VMEM_LIMIT),
    )(*grads, *small)
    return out[:count], out[count:]


def nt(a, b):
    return lax.dot_general(a, b, (((1,), (1,)), ((), ())), preferred_element_type=jnp.float32)


def tn(a, b):
    return lax.dot_general(a, b, (((0,), (0,)), ((), ())), preferred_element_type=jnp.float32)


def nn(a, b):
    return jnp.dot(a, b, preferred_element_type=jnp.float32)


def normalize(values):
    centred = values - jnp.mean(values, axis=1, keepdims=True)
    inverse = lax.rsqrt(jnp.mean(centred * centred, axis=1, keepdims=True) + EPSILON)
    return (centred * inverse, inverse)


def norm_back(grad_normed, normed, inverse):
    first_mean = jnp.mean(grad_normed, axis=1, keepdims=True)
    second_mean = jnp.mean(grad_normed * normed, axis=1, keepdims=True)
    return inverse * (grad_normed - first_mean - normed * second_mean)


def gelu_both(u):
    c = math.sqrt(2 / math.pi)
    square = u * u
    t = jnp.tanh(u * (c + (c * 0.044715) * square))
    half = 0.5 + 0.5 * t
    value = u * half
    return value, half + value * (1.0 - t) * (c + (3 * c * 0.044715) * square)


def loop(count, body):
    def step(i, carry):
        body(i)
        return carry

    lax.fori_loop(0, count, step, 0)


def mlp_kernel(
    attn_ref, tok_ref, cot_ref, wout_ref, bout_ref, scale_ref, shift_ref, live_ref, up_ref, bup_ref, down_ref, bdown_ref,
    out_ref, mid_grad_ref, attn_grad_ref, gout_ref, gbout_ref, gup_ref, gbup_ref, gdown_ref, gbdown_ref, gscale_ref, gshift_ref,
    middle, hidden, two, acc, back, act, pre,
):
    j = pl.program_id(0)
    rows = tok_ref.shape[0]
    blocks, units = rows // ROWS, ROWS // UNIT

    @pl.when(j == 0)
    def _():
        gbdown_ref[...] = jnp.zeros_like(gbdown_ref)

        def block(r):
            here = pl.ds(pl.multiple_of(r * ROWS, ROWS), ROWS)
            middle[here, :] = nn(attn_ref[here, :], wout_ref[...]) + bout_ref[...].astype(jnp.float32)

            for i in range(units):
                u = r * units + i
                at = pl.ds(pl.multiple_of(u * UNIT, UNIT), UNIT)
                live = live_ref[pl.ds(u, 1), :]
                value = tok_ref[at, :].astype(jnp.float32) + live * middle[at, :]
                middle[at, :] = value
                normed, _ = normalize(value)
                hidden[at, :] = (normed * (1.0 + scale_ref[pl.ds(u, 1), :]) + shift_ref[pl.ds(u, 1), :]).astype(jnp.bfloat16)
                grad = (live * cot_ref[at, :].astype(jnp.float32)).astype(jnp.bfloat16)
                two[at, :] = grad
                gbdown_ref[...] += jnp.sum(grad.astype(jnp.float32), axis=0, keepdims=True)

        loop(blocks, block)

    gbup_ref[...] = jnp.zeros_like(gbup_ref)

    def block(r):
        here = pl.ds(pl.multiple_of(r * ROWS, ROWS), ROWS)
        value, slope = gelu_both(nn(hidden[here, :], up_ref[...]) + bup_ref[...].astype(jnp.float32))
        value = value.astype(jnp.bfloat16)
        grad = (nt(two[here, :], down_ref[...]) * slope).astype(jnp.bfloat16)
        act[here, :] = value
        pre[here, :] = grad
        gbup_ref[...] += jnp.sum(grad.astype(jnp.float32), axis=0, keepdims=True)
        forward, backward = nn(value, down_ref[...]), nt(grad, up_ref[...])

        @pl.when(j == 0)
        def _():
            acc[here, :] = forward
            back[here, :] = backward

        @pl.when(j > 0)
        def _():
            acc[here, :] += forward
            back[here, :] += backward

    loop(blocks, block)
    gdown_ref[...] = tn(act[...], two[...]).astype(jnp.bfloat16)
    gup_ref[...] = tn(hidden[...], pre[...]).astype(jnp.bfloat16)

    @pl.when(j == pl.num_programs(0) - 1)
    def _():
        gbout_ref[...] = jnp.zeros_like(gbout_ref)

        def block(r):
            for i in range(units):
                u = r * units + i
                at = pl.ds(pl.multiple_of(u * UNIT, UNIT), UNIT)
                live = live_ref[pl.ds(u, 1), :]
                value = middle[at, :]
                out_ref[at, :] = (value + live * (acc[at, :] + bdown_ref[...].astype(jnp.float32))).astype(jnp.bfloat16)
                normed, inverse = normalize(value)
                grad = back[at, :]
                gshift_ref[pl.ds(u, 1), :] = jnp.sum(grad, axis=0, keepdims=True)
                gscale_ref[pl.ds(u, 1), :] = jnp.sum(grad * normed, axis=0, keepdims=True)
                passed = cot_ref[at, :].astype(jnp.float32) + norm_back(grad * (1.0 + scale_ref[pl.ds(u, 1), :]), normed, inverse)
                mid_grad_ref[at, :] = passed
                one = (live * passed).astype(jnp.bfloat16)
                two[at, :] = one
                gbout_ref[...] += jnp.sum(one.astype(jnp.float32), axis=0, keepdims=True)
            here = pl.ds(pl.multiple_of(r * ROWS, ROWS), ROWS)
            attn_grad_ref[here, :] = nt(two[here, :], wout_ref[...]).astype(jnp.bfloat16)

        loop(blocks, block)

        def part(r):
            here = pl.ds(pl.multiple_of(r * ROWS, ROWS), ROWS)
            gout_ref[here, :] = tn(attn_ref[:, here], two[...]).astype(jnp.bfloat16)

        loop(D // ROWS, part)


def feed_forward(attn_out, tokens, cotangent, w_out, b_out, scale, shift, live, w_up, b_up, w_down, b_down):
    rows, ff = tokens.shape[0], w_up.shape[1]
    once = lambda shape: pl.BlockSpec(shape, lambda j: (0, 0), pipeline_mode=pl.Buffered(1))
    wide = pl.BlockSpec((D, FF_BLOCK), lambda j: (0, j))
    tall = pl.BlockSpec((FF_BLOCK, D), lambda j: (j, 0))
    narrow = pl.BlockSpec((1, FF_BLOCK), lambda j: (0, j))
    row, whole, units = once((1, D)), once((rows, D)), once((rows // UNIT, D))
    f32, b16 = jnp.float32, jnp.bfloat16
    return pl.pallas_call(
        mlp_kernel,
        grid=(ff // FF_BLOCK,),
        out_shape=[
            jax.ShapeDtypeStruct((rows, D), b16), jax.ShapeDtypeStruct((rows, D), f32), jax.ShapeDtypeStruct((rows, D), b16),
            jax.ShapeDtypeStruct((D, D), b16), jax.ShapeDtypeStruct((1, D), f32),
            jax.ShapeDtypeStruct((D, ff), b16), jax.ShapeDtypeStruct((1, ff), f32),
            jax.ShapeDtypeStruct((ff, D), b16), jax.ShapeDtypeStruct((1, D), f32),
            jax.ShapeDtypeStruct((rows // UNIT, D), f32), jax.ShapeDtypeStruct((rows // UNIT, D), f32),
        ],
        in_specs=[whole, whole, whole, once((D, D)), row, units, units, units, wide, narrow, tall, row],
        out_specs=[whole, whole, whole, once((D, D)), row, wide, narrow, tall, row, units, units],
        scratch_shapes=[
            pltpu.VMEM((rows, D), f32), pltpu.VMEM((rows, D), b16), pltpu.VMEM((rows, D), b16),
            pltpu.VMEM((rows, D), f32), pltpu.VMEM((rows, D), f32),
            pltpu.VMEM((rows, FF_BLOCK), b16), pltpu.VMEM((rows, FF_BLOCK), b16),
        ],
        compiler_params=pltpu.CompilerParams(vmem_limit_bytes=VMEM_LIMIT),
    )(attn_out, tokens, cotangent, w_out, b_out, scale, shift, live, w_up, b_up, w_down, b_down)


def attention_lanes(segment, slots):
    lane = jnp.arange(128) % 64
    hot = segment[:, None] == lane[None, :]
    listed = lane[None, :] <= slots
    query_lanes = (hot & listed).astype(jnp.bfloat16)
    ones = (lane >= LSE_LANE) & (lane < LSE_LANE + 3)
    key_lanes = jnp.where(listed & ~hot, -1e30, jnp.where(ones[None, :], 1.0, 0.0)).astype(jnp.bfloat16)
    return query_lanes, key_lanes


def attend_pair(q_ref, k_ref, v_ref, ql_ref, kl_ref, out_ref, qa_ref):
    rows = q_ref.shape[0]
    block = min(ROWS_F, rows)
    low = lax.broadcasted_iota(jnp.int32, (1, 128), 1) < HEAD_DIM
    lane = lax.broadcasted_iota(jnp.int32, (1, 128), 1) % HEAD_DIM
    keys, vals = [], []
    for own in (low, ~low):
        keys.append(jnp.where(own, k_ref[...], kl_ref[...]))
        vals.append(jnp.where(own, v_ref[...], jnp.bfloat16(1)))
    for first in range(0, rows, block):
        here = pl.ds(first, block)
        queries = q_ref[here, :] * jnp.bfloat16(HEAD_DIM**-0.5)
        mixed = []
        for head, own in enumerate((low, ~low)):
            asked = jnp.where(own, queries, ql_ref[here, :])
            scores = nt(asked, keys[head])
            top = jnp.max(scores, axis=1, keepdims=True)
            weight = jnp.exp(scores - top).astype(jnp.bfloat16)
            both = nn(weight, vals[head])
            mixed.append(both)
            log_total = -(top + jnp.log(both))
            first_part = log_total.astype(jnp.bfloat16)
            rest = log_total - first_part.astype(jnp.float32)
            second = rest.astype(jnp.bfloat16)
            third = (rest - second.astype(jnp.float32)).astype(jnp.bfloat16)
            for at, part in enumerate((first_part, second, third)):
                asked = jnp.where(~own & (lane == LSE_LANE + at), part, asked)
            qa_ref[head, here, :] = asked
        total = pltpu.roll(jnp.where(low, mixed[1], mixed[0]), HEAD_DIM, 1)
        out_ref[here, :] = (jnp.where(low, mixed[0], mixed[1]) / total).astype(jnp.bfloat16)


def attend_back_pair(k_ref, v_ref, kl_ref, qa_ref, out_ref, go_ref, grad_ref, kt_ref, dqt_ref):
    rows = k_ref.shape[0]
    block = min(ROWS_B, rows)
    low = lax.broadcasted_iota(jnp.int32, (1, 128), 1) < HEAD_DIM
    grads = go_ref[...]
    product = pltpu.roll(-(grads.astype(jnp.float32) * out_ref[...].astype(jnp.float32)), HEAD_DIM, 1).astype(jnp.bfloat16)
    kt_ref[...] = k_ref[...].astype(jnp.float32).T.astype(jnp.bfloat16)
    given = [jnp.where(own, grads, product) for own in (low, ~low)]
    for first in range(0, rows, block):
        here = pl.ds(first, block)
        dks, dvs = [], []
        for head, own in enumerate((low, ~low)):
            keys = jnp.where(own, k_ref[here, :], kl_ref[here, :])
            vals = jnp.where(own, v_ref[here, :], jnp.bfloat16(1))
            probs = jnp.exp(nt(keys, qa_ref[head]))
            slopes = nt(vals, given[head])
            moved = (probs * slopes).astype(jnp.bfloat16)
            dvs.append(nn(probs.astype(jnp.bfloat16), grads))
            dks.append(nn(moved, qa_ref[head]))
            part = nn(kt_ref[head * HEAD_DIM : (head + 1) * HEAD_DIM, here], moved)
            where = pl.ds(head * HEAD_DIM, HEAD_DIM)
            if first == 0:
                dqt_ref[where, :] = part
            else:
                dqt_ref[where, :] += part
        grad_ref[1, here, :] = jnp.where(low, dks[0], dks[1]).astype(jnp.bfloat16)
        grad_ref[2, here, :] = jnp.where(low, dvs[0], dvs[1]).astype(jnp.bfloat16)
    grad_ref[0] = (dqt_ref[...].T * HEAD_DIM**-0.5).astype(jnp.bfloat16)


def attend(projected, query_lanes, key_lanes):
    rows = projected.shape[0]
    pairs = D // 128
    spec = lambda shift: pl.BlockSpec((rows, 128), lambda i: (0, i + shift))
    lanes = pl.BlockSpec((rows, 128), lambda i: (0, 0))
    return pl.pallas_call(
        attend_pair,
        grid=(pairs,),
        out_shape=[jax.ShapeDtypeStruct((rows, D), jnp.bfloat16), jax.ShapeDtypeStruct((HEADS, rows, 128), jnp.bfloat16)],
        in_specs=[spec(0), spec(pairs), spec(2 * pairs), lanes, lanes],
        out_specs=[spec(0), pl.BlockSpec((2, rows, 128), lambda i: (i, 0, 0))],
        compiler_params=pltpu.CompilerParams(vmem_limit_bytes=VMEM_LIMIT),
    )(projected, projected, projected, query_lanes, key_lanes)


def attend_back(projected, key_lanes, asked, attn_out, grad_attn):
    rows = projected.shape[0]
    pairs = D // 128
    spec = lambda shift: pl.BlockSpec((rows, 128), lambda i: (0, i + shift))
    lanes = pl.BlockSpec((rows, 128), lambda i: (0, 0))
    return pl.pallas_call(
        attend_back_pair,
        grid=(pairs,),
        out_shape=jax.ShapeDtypeStruct((3, rows, D), jnp.bfloat16),
        in_specs=[spec(pairs), spec(2 * pairs), lanes, pl.BlockSpec((2, rows, 128), lambda i: (i, 0, 0)), spec(0), spec(0)],
        out_specs=pl.BlockSpec((3, rows, 128), lambda i: (0, 0, i)),
        scratch_shapes=[pltpu.VMEM((128, rows), jnp.bfloat16), pltpu.VMEM((128, rows), jnp.float32)],
        compiler_params=pltpu.CompilerParams(vmem_limit_bytes=VMEM_LIMIT),
    )(projected, projected, key_lanes, asked, attn_out, grad_attn)


def head_kernel(tok_ref, scale_ref, shift_ref, w_ref, hidden_ref, out_ref):
    rows = tok_ref.shape[0]

    @pl.when(pl.program_id(0) == 0)
    def _():
        def unit(u):
            at = pl.ds(pl.multiple_of(u * UNIT, UNIT), UNIT)
            normed, _ = normalize(tok_ref[at, :].astype(jnp.float32))
            hidden_ref[at, :] = (normed * (1.0 + scale_ref[pl.ds(u, 1), :]) + shift_ref[pl.ds(u, 1), :]).astype(jnp.bfloat16)

        loop(rows // UNIT, unit)

    def block(r):
        here = pl.ds(pl.multiple_of(r * ROWS, ROWS), ROWS)
        out_ref[here, :] = nn(hidden_ref[here, :], w_ref[...]).astype(jnp.bfloat16)

    loop(rows // ROWS, block)


def project_in(tokens, scale, shift, w_qkv):
    rows = tokens.shape[0]
    whole = lambda shape: pl.BlockSpec(shape, lambda j: (0, 0))
    return pl.pallas_call(
        head_kernel,
        grid=(3,),
        out_shape=[jax.ShapeDtypeStruct((rows, D), jnp.bfloat16), jax.ShapeDtypeStruct((rows, 3 * D), jnp.bfloat16)],
        in_specs=[whole((rows, D)), whole((rows // UNIT, D)), whole((rows // UNIT, D)), pl.BlockSpec((D, D), lambda j: (0, j))],
        out_specs=[whole((rows, D)), pl.BlockSpec((rows, D), lambda j: (0, j))],
        compiler_params=pltpu.CompilerParams(vmem_limit_bytes=VMEM_LIMIT),
    )(tokens, scale, shift, w_qkv)


def tail_kernel(grad_ref, hidden_ref, w_ref, tok_ref, mid_ref, scale_ref, gw_ref, gtok_ref, gscale_ref, gshift_ref, back):
    p = pl.program_id(0)
    rows = tok_ref.shape[0]

    def block(r):
        here = pl.ds(pl.multiple_of(r * ROWS, ROWS), ROWS)
        part = nt(grad_ref[0, here, :], w_ref[...])

        @pl.when(p == 0)
        def _():
            back[here, :] = part

        @pl.when(p > 0)
        def _():
            back[here, :] += part

    loop(rows // ROWS, block)

    def columns(r):
        here = pl.ds(pl.multiple_of(r * ROWS, ROWS), ROWS)
        gw_ref[here, :] = tn(hidden_ref[:, here], grad_ref[0]).astype(jnp.bfloat16)

    loop(D // ROWS, columns)

    @pl.when(p == pl.num_programs(0) - 1)
    def _():
        def unit(u):
            at = pl.ds(pl.multiple_of(u * UNIT, UNIT), UNIT)
            normed, inverse = normalize(tok_ref[at, :].astype(jnp.float32))
            grad = back[at, :]
            gshift_ref[pl.ds(u, 1), :] = jnp.sum(grad, axis=0, keepdims=True)
            gscale_ref[pl.ds(u, 1), :] = jnp.sum(grad * normed, axis=0, keepdims=True)
            gtok_ref[at, :] = mid_ref[at, :] + norm_back(grad * (1.0 + scale_ref[pl.ds(u, 1), :]), normed, inverse)

        loop(rows // UNIT, unit)


def project_back(grad_proj, hidden, w_qkv, tokens, grad_mid, scale):
    rows = tokens.shape[0]
    once = lambda shape: pl.BlockSpec(shape, lambda p: (0, 0), pipeline_mode=pl.Buffered(1))
    units, whole = once((rows // UNIT, D)), once((rows, D))
    f32 = jnp.float32
    return pl.pallas_call(
        tail_kernel,
        grid=(3,),
        out_shape=[
            jax.ShapeDtypeStruct((D, 3 * D), jnp.bfloat16), jax.ShapeDtypeStruct((rows, D), f32),
            jax.ShapeDtypeStruct((rows // UNIT, D), f32), jax.ShapeDtypeStruct((rows // UNIT, D), f32),
        ],
        in_specs=[
            pl.BlockSpec((1, rows, D), lambda p: (p, 0, 0)), whole, pl.BlockSpec((D, D), lambda p: (0, p)), whole, whole, units,
        ],
        out_specs=[pl.BlockSpec((D, D), lambda p: (0, p)), whole, units, units],
        scratch_shapes=[pltpu.VMEM((rows, D), f32)],
        compiler_params=pltpu.CompilerParams(vmem_limit_bytes=VMEM_LIMIT),
    )(grad_proj, hidden, w_qkv, tokens, grad_mid, scale)


def tuned(sizes):
    return sizes == (4, 8)


def gathered(sizes, shards, biases, feats):
    n = sizes[1]
    if not tuned(sizes):
        every = lax.all_gather(feats, ("dp", "fsdp"), axis=0, tiled=True)
        return (
            [lax.all_gather(w, "fsdp", axis=0, tiled=True) for w in shards],
            [lax.all_gather(b, "fsdp", axis=0, tiled=True) for b in biases],
            lax.dynamic_slice(every, (0, lax.axis_index("fsdp") * (D // n)), (every.shape[0], D // n)),
        )
    slots = feats.shape[0]
    packed = jnp.concatenate(biases).reshape(-1, 128)
    packed = jnp.pad(packed, ((0, 16 - packed.shape[0]), (0, 0)))
    by_owner = feats.reshape(slots, n, 128).transpose(1, 0, 2)
    small = jnp.concatenate([jnp.broadcast_to(packed, (n, 16, 128)), by_owner], axis=1)
    small_all, weights = gather_all(small, shards)
    of_group = lax.dynamic_slice(small_all, (lax.axis_index("dp") * n, 0, 0), (n, 16, 128))
    wholes, first = [], 0
    for b in biases:
        count = b.shape[0] // 128
        wholes.append(of_group[:, first : first + count].reshape(-1))
        first += count
    return weights, wholes, small_all[:, 16:].reshape(-1, 128)


def reduced(sizes, grads, sums=None):
    n = sizes[1]
    if tuned(sizes):
        if sums is None:
            totals, _ = reduce_all(grads)
            shares = None
        else:
            packed = jnp.concatenate([s.reshape(n, -1, 128) for s in sums], axis=1)
            totals, [every] = reduce_all(grads, [jnp.pad(packed, ((0, 0), (0, 16 - packed.shape[1]), (0, 0)))])
            total, shares, first = jnp.sum(every, axis=0), [], 0
            for s in sums:
                count = s.shape[0] // n // 128
                shares.append(total[first : first + count].reshape(-1))
                first += count
    else:
        totals = [lax.psum(lax.psum_scatter(g, "fsdp", scatter_dimension=0, tiled=True), "dp") for g in grads]
        shares = sums
        if sums is not None:
            shares = [lax.psum(lax.psum_scatter(s, "fsdp", scatter_dimension=0, tiled=True), "dp") for s in sums]
    return [t.astype(jnp.float32) for t in totals], shares


def local(
    sizes, tokens, lengths, buckets, w_mod, b_mod, w_qkv, w_out, b_out, w_up, b_up, w_down, b_down, cotangent,
):
    rows, slots = tokens.shape[0], lengths.shape[1]
    segment, live, unit_table = layout(lengths[0], rows)
    feats = time_features(buckets[0]).astype(jnp.bfloat16)
    weights, biases, every_feats = gathered(sizes, (w_mod, w_qkv, w_out, w_up, w_down), (b_mod, b_out, b_up, b_down), feats)
    full_mod, full_qkv, full_out, full_up, full_down = weights
    full_bmod, full_bout, full_bup, full_bdown = biases
    modulation = jnp.dot(feats, full_mod, preferred_element_type=jnp.float32) + full_bmod
    per_unit = jnp.dot(unit_table, modulation, precision=HIGHEST)
    scale_one, shift_one, scale_two, shift_two = [per_unit[:, i * D : (i + 1) * D] for i in range(4)]
    live_units = jnp.broadcast_to(live[:, None], (rows // UNIT, D))
    hidden_attn, projected = project_in(tokens, scale_one, shift_one, full_qkv)
    query_lanes, key_lanes = attention_lanes(jnp.repeat(segment, UNIT), slots)
    attn_out, asked = attend(projected, query_lanes, key_lanes)
    (
        output, grad_mid, grad_attn, grad_w_out, grad_b_out, grad_w_up, grad_b_up, grad_w_down, grad_b_down, grad_scale_two, grad_shift_two,
    ) = feed_forward(
        attn_out, tokens, cotangent, full_out, full_bout[None], scale_two, shift_two, live_units,
        full_up, full_bup[None], full_down, full_bdown[None],
    )
    (sum_up, sum_down), _ = reduced(sizes, (grad_w_up, grad_w_down))
    grad_proj = attend_back(projected, key_lanes, asked, attn_out, grad_attn)
    grad_w_qkv, grad_tokens, grad_scale_one, grad_shift_one = project_back(
        grad_proj, hidden_attn, full_qkv, tokens, grad_mid, scale_one
    )
    by_unit = jnp.concatenate([grad_scale_one, grad_shift_one, grad_scale_two, grad_shift_two], axis=1)
    grad_mod = jnp.dot(unit_table.T, by_unit, precision=HIGHEST).astype(jnp.bfloat16)
    every_mod = lax.all_gather(grad_mod, ("dp", "fsdp"), axis=0, tiled=True)
    sum_mod = jnp.einsum("sd,sc->dc", every_feats, every_mod, preferred_element_type=jnp.float32)
    grad_b_mod = jnp.sum(grad_mod, axis=0, dtype=jnp.float32)
    (sum_qkv, sum_out), (sum_bmod, sum_bout, sum_bup, sum_bdown) = reduced(
        sizes, (grad_w_qkv, grad_w_out), (grad_b_mod, grad_b_out[0], grad_b_up[0], grad_b_down[0])
    )
    return output, grad_tokens, sum_mod, sum_bmod, sum_qkv, sum_out, sum_bout, sum_up, sum_bup, sum_down, sum_bdown


def solution(mesh):
    sizes = (mesh.shape["dp"], mesh.shape["fsdp"])
    rows, cut_rows, vector = P(("dp", "fsdp"), None), P("fsdp", None), P("fsdp")
    return jax.shard_map(
        functools.partial(local, sizes),
        mesh=mesh,
        in_specs=(rows, rows, rows, cut_rows, vector, cut_rows, cut_rows, vector, cut_rows, vector, cut_rows, vector, rows),
        out_specs=(rows, rows, cut_rows, vector, cut_rows, cut_rows, vector, cut_rows, vector, cut_rows, vector),
        check_vma=False,
    )
```

time: 2010 us -> 630 us (0.31)
  waiting for transfers between devices: 1360 us -> 0.02 us
  Pallas kernels: 0 us -> 573 us
  matrix products: 301 us -> 11.1 us
  blocking collectives: 135 us -> 0 us
  local copies, waits for them, and re-layouts: 113 us -> 4.73 us
  other arithmetic: 69 us -> 15.7 us
    reduce_scatter x5 -> x0, waiting for transfers between devices: 989 us -> none  [the longest x1 286 us: local(): lax.psum_scatter(grad_w_down, 'fsdp', scatter_dimension=0, tiled=True)]
    pallas_call x0 -> x8, Pallas kernels: none -> 573 us  [the longest x2 203 us: reduce_all(): pl.pallas_call(functools.partial(reduce_kernel, count, smalls), out_shape...]
    all_gather x5 -> x1, waiting for transfers between devices: 294 us -> 0.01 us  [local(): every_mod = lax.all_gather(grad_mod, ('dp', 'fsdp'), axis=0, tiled=True)]
    dot_general x72 -> x4, matrix products: 301 us -> 11.1 us  [the longest x1 4.63 us: local(): jnp.dot(feats, full_mod, preferred_element_type=jnp.float32) + full_bmod]
    all_gather x4 -> x0, blocking collectives: 93.8 us -> none  [the longest x1 26.6 us: local(): lax.all_gather(b_mod, 'fsdp', axis=0, tiled=True)]
    psum x1 -> x0, waiting for transfers between devices: 75.8 us -> none  [local(): lax.psum((attn_sums[0], attn_sums[1], attn_sums[2], attn_sums[3], attn_su...]
    unnamed x1 -> x0, blocking collectives: 33.4 us -> none
    reduce_sum x12 -> x2, other arithmetic: 29.3 us -> 0.78 us  [the longest x1 0.74 us: layout(): jnp.sum(jnp.where(upto, lengths[:, None], 0), axis=0, dtype=jnp.int32)]
  transfers between devices with their start and end apart: 11 -> 1, of which waited for: 9 -> 0; matrix products, arithmetic and copies ran while one was open for 20% -> 2% of each run, Pallas kernels for 0% -> 33%
where the time goes in v1:
time: 630 us; the launch traced here: 619 us
  Pallas kernels  573 us (91%)
  other arithmetic  15.7 us (2%)
  between operations  14.7 us (2%)
  matrix products  11.1 us (2%)
    pallas_call x2, Pallas kernels, reduce_all(): pl.pallas_call(functools.partial(reduce_kernel, count, smalls), out_shape...  203 us
    pallas_call x1, Pallas kernels, gather_all(): pl.pallas_call(functools.partial(gather_kernel, count), out_shape=[jax.Sh...  160 us
    pallas_call x1, Pallas kernels, feed_forward(): pl.pallas_call(mlp_kernel, grid=(ff // FF_BLOCK,), out_shape=[jax.ShapeDt...  88.7 us
    pallas_call x1, Pallas kernels, attend_back(): pl.pallas_call(attend_back_pair, grid=(pairs,), out_shape=jax.ShapeDtypeS...  46.4 us
    pallas_call x1, Pallas kernels, attend(): pl.pallas_call(attend_pair, grid=(pairs,), out_shape=[jax.ShapeDtypeStruc...  29.9 us
    pallas_call x1, Pallas kernels, project_back(): pl.pallas_call(tail_kernel, grid=(3,), out_shape=[jax.ShapeDtypeStruct((D...  29.1 us
    pallas_call x1, Pallas kernels, project_in(): pl.pallas_call(head_kernel, grid=(3,), out_shape=[jax.ShapeDtypeStruct((r...  15.4 us
  transfers between devices with their start and end apart: 1, of which 0 were waited for; matrix products, arithmetic and copies ran while one was open for 2% of the time, Pallas kernels for 33%

profile of v1, /device:TPU:0, one launch (start us, length us, event | category | flops | bytes accessed | tf_op | source)
XLA Modules:
  0.0 619.2 jit_solution(8936627354767227278)
XLA Ops:
  7.2 0.0 all-gather.2.cloned.1.call-start
  7.3 0.7 convert_bitcast_fusion
  8.0 0.7 select_reduce_fusion
  8.7 0.2 convert_reduce_fusion.1
  8.9 0.1 broadcast_in_dim.62
  9.0 0.1 eq.30
  9.0 0.2 fusion.11
  9.2 0.2 fusion.9
  9.4 0.9 fusion.ql_ref
  10.4 0.9 select_convert_fusion.kl_ref
  11.3 0.7 maximum_bitcast_fusion.1
  12.0 0.6 pad_maximum_fusion.refs_0_
  12.7 160.2 %shard_map.212 = (bf16[32,32,128]{2,1,0:T(8,128)(2,1)}, bf16[1024,4096]{1,0:T(8,128)(2,1)}, bf16[1024,3072]{1,0:T(8,128)(2,1)}, bf16[1024,1024]{1,0:T(8,128)(2,1...) custom-call(bf16[8,32,128]{2,1,0:T(8,128)(2,1)} %pad_maximum_fusion.refs_0_, bf16[128,4096]{1,0:T(8,128)(2,1)} %refs_1_.1, ...), custom_call_target="tpu_custom_call" | custom-call | tf_op jit(solution)/shard_map/pallas_call | solution.py:221
  172.9 0.8 constant_dynamic-slice_fusion
  173.8 0.0 copy-start.1
  173.8 4.6 convolution_add_fusion
  178.4 0.3 fusion.16
  178.7 0.7 fusion.21
  179.4 0.6 broadcast_in_dim_reshape.11.bup_ref
  180.0 0.0 copy-done.1
  180.0 0.6 dynamic-slice_bitcast_fusion
  180.6 15.4 %shard_map.213 = (bf16[1024,1024]{1,0:T(8,128)(2,1)}, bf16[1024,3072]{1,0:T(8,128)(2,1)}) custom-call(bf16[1024,1024]{1,0:T(8,128)(2,1)} %tok_ref.5, f32[16,1024]{1,0:T(8,128)} %get-tuple-element.78.scale_ref, f32[16,1024]{1,0:T(8,128)} %get-tuple-element.77.shift_ref, bf16[1024,3072]{1,0:T(8,128)(2,1)} %get-tuple-element.43.w_ref), custom_call_target="tpu_custom_call" | custom-call | tf_op jit(solution)/shard_map/pallas_call | solution.py:661
  196.0 29.9 %shard_map.214 = (bf16[1024,1024]{1,0:T(8,128)(2,1)}, bf16[16,1024,128]{2,1,0:T(8,128)(2,1)}) custom-call(bf16[1024,3072]{1,0:T(8,128)(2,1)} %get-tuple-element.44.q_ref.k_ref.v_ref, bf16[1024,3072]{1,0:T(8,128)(2,1)} %get-tuple-element.44.q_ref.k_ref.v_ref, bf16[1024,3072]{1,0:T(8,128)(2,1)} %get-tuple-element.44.q_ref.k_ref.v_ref, ...), custom_call_target="tpu_custom_call" | custom-call | tf_op jit(solution)/shard_map/pallas_call | solution.py:613
  225.9 0.7 broadcast_in_dim.67.live_ref
  226.6 88.7 %shard_map.215 = (bf16[1024,1024]{1,0:T(8,128)(2,1)}, f32[1024,1024]{1,0:T(8,128)}, bf16[1024,1024]{1,0:T(8,128)(2,1)}, bf16[1024,1024]{1,0:T(8,128)(2,1)}, f32[...) custom-call(bf16[1024,1024]{1,0:T(8,128)(2,1)} %get-tuple-element.45, ...), custom_call_target="tpu_custom_call" | custom-call | tf_op jit(solution)/shard_map/pallas_call | solution.py:515
  315.3 46.4 %shard_map.216.grad_ref = bf16[3,1024,1024]{2,1,0:T(8,128)(2,1)} custom-call(bf16[1024,3072]{1,0:T(8,128)(2,1)} %get-tuple-element.44.q_ref.k_ref.v_ref, bf16[1024,3072]{1,0:T(8,128)(2,1)} %get-tuple-element.44.q_ref.k_ref.v_ref, bf16[1024,128]{1,0:T(8,128)(2,1)} %select_convert_fusion.kl_ref, bf16[16,1024,128]{2,1,0:T(8,128)(2,1)} %get-tuple-element.50.qa_ref, ...), custom_call_target="tpu_custom_call" | custom-call | tf_op jit(solution)/shard_map/pallas_call | solution.py:628
  361.7 0.0 copy-start.2
  361.7 0.0 copy-start.3
  361.7 0.0 copy-start.4
  361.7 29.1 %shard_map.217 = (bf16[1024,3072]{1,0:T(8,128)(2,1)}, f32[1024,1024]{1,0:T(8,128)}, f32[16,1024]{1,0:T(8,128)}, f32[16,1024]{1,0:T(8,128)}) custom-call(bf16[3,1024,1024]{2,1,0:T(8,128)(2,1)} %shard_map.216.grad_ref, bf16[1024,1024]{1,0:T(8,128)(2,1)} %get-tuple-element.52.hidden_ref, bf16[1024,3072]{1,0:T(8,128)(2,1)} %get-tuple-element.43.w_ref, ...), custom_call_target="tpu_custom_call" | custom-call | tf_op jit(solution)/shard_map/pallas_call | solution.py:713
  390.8 0.0 copy-done.5
  390.8 0.0 copy-done.6
  390.8 1.9 convert_reduce_fusion
  392.8 0.0 all-gather.2.cloned.1.call-update
  392.8 0.0 copy-done.2
  392.8 0.0 copy-done.3
  392.8 0.0 copy-done.4
  392.8 0.7 select_maximum_fusion.refs_2_
  393.5 81.0 %shard_map.218 = (bf16[128,3072]{1,0:T(8,128)(2,1)}, bf16[128,1024]{1,0:T(8,128)(2,1)}, f32[32,16,128]{2,1,0:T(8,128)}) custom-call(bf16[1024,3072]{1,0:T(8,128)(2,1)} %get-tuple-element.59.refs_0_, bf16[1024,1024]{1,0:T(8,128)(2,1)} %get-tuple-element.60.refs_1_, f32[8,16,128]{2,1,0:T(8,128)} %select_maximum_fusion.refs_2_), custom_call_target="tpu_custom_call" | custom-call | tf_op jit(solution)/shard_map/pallas_call | solution.py:364
  474.5 1.8 convert_element_type.72
  476.3 2.4 convert_element_type.71
  478.7 122.2 %shard_map.219 = (bf16[128,4096]{1,0:T(8,128)(2,1)}, bf16[512,1024]{1,0:T(8,128)(2,1)}) custom-call(bf16[1024,4096]{1,0:T(8,128)(2,1)} %get-tuple-element.67.refs_0_, bf16[4096,1024]{1,0:T(8,128)(2,1)} %get-tuple-element.68.refs_1_), custom_call_target="tpu_custom_call" | custom-call | tf_op jit(solution)/shard_map/pallas_call | solution.py:364
  600.9 0.0 copy-start
  600.9 2.8 convert_element_type.73
  603.7 2.8 convert_element_type.74
  606.5 0.5 slice_bitcast_fusion.2
  607.1 0.6 slice_bitcast_fusion
  607.7 4.2 fusion.22
  (17 shorter events, 0.1 us)
Async XLA Ops:
  7.2 600.5 %all-gather.2.cloned.1.call-start = ((), (), s32[]{:S(2)}) async-start(), calls=%async_computation | async-start | bytes 4325376 | tf_op jit(solution)/shard_map/all_gather | solution.py:808
  173.8 6.3 %copy-start.1 = (bf16[32,32,128]{2,1,0:T(8,128)(2,1)S(1)}, bf16[32,32,128]{2,1,0:T(8,128)(2,1)}, u32[]{:S(2)}) copy-start(bf16[32,32,128]{2,1,0:T(8,128)(2,1)} %get-tuple-element.42) | copy-start | bytes 786436
  361.7 29.2 %copy-start.5 = (f32[16,1024]{1,0:T(8,128)S(1)}, f32[16,1024]{1,0:T(8,128)}, u32[]{:S(2)}) copy-start(f32[16,1024]{1,0:T(8,128)} %get-tuple-element.57) | copy-start | bytes 196612
  361.7 29.2 %copy-start.6 = (f32[16,1024]{1,0:T(8,128)S(1)}, f32[16,1024]{1,0:T(8,128)}, u32[]{:S(2)}) copy-start(f32[16,1024]{1,0:T(8,128)} %get-tuple-element.58) | copy-start | bytes 196612
  361.7 31.1 %copy-start.2 = (f32[1,4096]{1,0:T(1,128)S(1)}, f32[1,4096]{1,0:T(1,128)}, u32[]{:S(2)}) copy-start(f32[1,4096]{1,0:T(1,128)} %get-tuple-element.62) | copy-start | bytes 49156
  361.7 31.1 %copy-start.3 = (f32[1,1024]{1,0:T(1,128)S(1)}, f32[1,1024]{1,0:T(1,128)}, u32[]{:S(2)}) copy-start(f32[1,1024]{1,0:T(1,128)} %get-tuple-element.61) | copy-start | bytes 12292
  361.7 31.1 %copy-start.4 = (f32[1,1024]{1,0:T(1,128)S(1)}, f32[1,1024]{1,0:T(1,128)}, u32[]{:S(2)}) copy-start(f32[1,1024]{1,0:T(1,128)} %get-tuple-element.63) | copy-start | bytes 12292
  600.9 5.6 copy-start
Sparse Core Ops, SparseCore 0:
  392.9 83.9 all-gather.1

commit v2 on v0

v2 whole, which is shorter than its diff:
```python
import functools
import math

import jax
import jax.numpy as jnp
from jax import lax
from jax.experimental import pallas as pl
from jax.experimental.pallas import tpu as pltpu
from jax.sharding import PartitionSpec as P

D = 1024
HEADS = 16
HEAD_DIM = 64
EPSILON = 1e-05
UNIT = 64
ROWS = 512
ATTENTION_ROWS = 512
FF_BLOCKS = 4
EARLY = 2
LSE_LANE = 24
GATHER_EVERY = 1
REDUCE_EVERY = 1
GATHER_START, GATHER_LAGS = 3, (0, 5, 10, 15, 18)
REDUCE_START, REDUCE_LAGS = 3, (0, 3, 9, 16, 22, 26, 28)
VMEM_LIMIT = 62 * 2**20
HIGHEST = lax.Precision.HIGHEST
MESH = pl.DeviceIdType.MESH


def layout(lengths, tok_rows):
    slots = lengths.shape[0]
    upto = jnp.arange(slots)[:, None] <= jnp.arange(slots)[None, :]
    seq_ends = jnp.sum(jnp.where(upto, lengths[:, None], 0), axis=0, dtype=jnp.int32)
    position = jnp.arange(0, tok_rows, UNIT, dtype=jnp.int32)
    segment = jnp.sum((position[:, None] >= seq_ends[None, :]).astype(jnp.int32), axis=1, dtype=jnp.int32)
    unit_table = (segment[:, None] == jnp.arange(slots, dtype=jnp.int32)[None, :]).astype(jnp.float32)
    return segment, (segment < slots).astype(jnp.float32), unit_table


def time_features(buckets):
    half_width = D // 2
    frequency = jnp.exp(-math.log(10000.0) * jnp.arange(half_width, dtype=jnp.float32) / half_width)
    angles = buckets.astype(jnp.float32)[:, None] * frequency[None, :]
    return jnp.concatenate([jnp.sin(angles), jnp.cos(angles)], axis=1)


def place():
    dp, fsdp = lax.axis_index("dp"), lax.axis_index("fsdp")
    return dp // 2, dp % 2, fsdp // 2, fsdp % 2


def device(x, core, z, y):
    return (x * 2 + core, z * 2 + y)


class Hop:
    def __init__(self, links, src, dst, target):
        self.links, self.src, self.dst, self.target, self.gone = links, src, dst, target, False
        self.slot = links.used
        links.used += 1
        links.hops.append(self)

    def made(self):
        return pltpu.make_async_remote_copy(
            src_ref=self.src(),
            dst_ref=self.dst(),
            send_sem=self.links.send_sems.at[self.slot],
            recv_sem=self.links.recv_sems.at[self.slot],
            device_id=self.target(),
            device_id_type=MESH,
        )

    def start(self):
        self.made().start()

    def arrived(self):
        self.made().wait_recv()

    def left(self):
        self.gone = True
        self.made().wait_send()


class Near:
    def __init__(self, links, src, dst):
        self.links, self.src, self.dst = links, src, dst
        self.slot = links.used_near
        links.used_near += 1

    def made(self):
        return pltpu.make_async_copy(self.src(), self.dst(), self.links.near_sems.at[self.slot])

    def start(self):
        self.made().start()

    def arrived(self):
        self.made().wait()


class Links:
    def __init__(self, send_sems, recv_sems, near_sems):
        self.send_sems, self.recv_sems, self.near_sems = send_sems, recv_sems, near_sems
        self.used, self.used_near, self.hops, self.ends = 0, 0, [], []

    def drain(self):
        for hop in self.hops:
            if not hop.gone:
                hop.left()
        for near in self.ends:
            near.arrived()


def lanes(at, size):
    return pl.ds(pl.multiple_of(at, 128), size)


def lines(at, size):
    return pl.ds(pl.multiple_of(at, 16), size)


HALVES = (pl.ds(0, 64), pl.ds(64, 64))


def gather_turns(links, me, shard, whole, outer, at=None):
    x, core, z, y = me
    rows, width = shard.shape
    half = width // 2
    inner = half - 2 * outer

    def own():
        return lanes(core * half + x * outer, outer + inner)

    def crossing():
        return lanes(core * half + x * (outer + inner), outer)

    def full():
        return lanes(core * half, half)

    def block(way, k):
        return ((z - k + 4) % 4) * 2 + (y if way == "z" else 1 - y)

    def place_of(index):
        return lines(index * rows, rows) if at is None else lines(index * 128 + at, rows)

    def part(index, columns):
        return whole.at[place_of(index), columns]

    def mine():
        return z * 2 + y

    def from_shard(target):
        return Hop(links, lambda: shard.at[:, own()], lambda: part(mine(), own()), target)

    def pass_on(way, k, columns, target):
        def at():
            return part(block(way, k), columns())

        return Hop(links, at, at, target)

    to_y = lambda: device(x, core, z, 1 - y)
    keep = Near(links, lambda: shard, lambda: whole.at[place_of(mine()), :])
    along_z = {k: from_shard(lambda k=k: device(x, core, (z + k) % 4, y)) for k in (1, 2, 3)}
    along_y = {0: from_shard(to_y)}
    for k in (1, 2, 3):
        along_y[k] = pass_on("z", k, own, to_y)
    order = [("z", 1), ("y", 0), ("z", 2), ("y", 1), ("z", 3), ("y", 2), ("y", 3)]
    crossed = [pass_on(way, k, crossing, lambda: device(1 - x, core, z, y)) for way, k in order] if outer else None
    handed = [pass_on(way, k, full, lambda: device(x, 1 - core, z, y)) for way, k in order]

    def first():
        for k in (1, 2, 3):
            along_z[k].start()
        along_y[0].start()
        keep.start()

    def arrive(j):
        way, k = order[j]
        (along_z if way == "z" else along_y)[k].arrived()
        if way == "z":
            along_y[k].start()
        (crossed if outer else handed)[j].start()

    def hand_on(j):
        if outer:
            crossed[j].arrived()
            handed[j].start()

    def last():
        for hop in handed:
            hop.arrived()
        keep.arrived()

    return [
        first,
        lambda: [arrive(j) for j in (1, 0, 2, 4)],
        lambda: [arrive(j) for j in (3, 5, 6)] + [hand_on(j) for j in (1, 0, 2, 4)],
        lambda: [hand_on(j) for j in (3, 5, 6)],
        last,
    ]


GATHER_HOPS, GATHER_NEAR = 3 + 4 + 7 + 7, 1


def reduce_lands(rows, width=1024, far=True):
    half = width // 2
    outer = half // 4
    shapes = [
        (4, 2, rows, half), (4, 2, rows, outer), (4, rows, half - outer), (3, rows, half - outer), (rows, half - outer),
    ]
    if far:
        shapes.append((4, 2, rows, half))
    return [pltpu.VMEM(s, jnp.bfloat16) for s in shapes]


def reduce_turns(links, me, local, at, result, out, lands):
    x, core, z, y = me
    total, from_x, from_y, from_z, from_last = lands[:5]
    far = lands[5] if len(lands) > 5 else None
    rows, width = result.shape
    half = width // 2
    outer = half // 4
    wide = half - outer

    def own():
        return lanes(x * outer, wide)

    def kept():
        return lanes(x * wide, outer)

    def given():
        return lanes((1 - x) * wide, outer)

    def owners(t, side):
        return local.at[pl.ds(((z + t + 1) % 4) * 2, 2), pl.ds(at, rows), lanes(side * half, half)]

    turns4 = range(4)
    load = [Near(links, lambda t=t: owners(t, core), lambda t=t: far.at[t]) for t in turns4] if far is not None else []
    to_core = [Hop(links, lambda t=t: owners(t, 1 - core), lambda t=t: total.at[t], lambda: device(x, 1 - core, z, y)) for t in turns4]
    to_x = [
        Hop(links, lambda t=t: total.at[t, :, :, given()], lambda t=t: from_x.at[t], lambda: device(1 - x, core, z, y)) for t in turns4
    ]
    to_y = [
        Hop(links, lambda t=t: total.at[t, 1 - y, :, own()], lambda t=t: from_y.at[t], lambda: device(x, core, z, 1 - y)) for t in turns4
    ]
    to_z = [
        Hop(links, lambda t=t: total.at[t, y, :, own()], lambda t=t: from_z.at[t], lambda t=t: device(x, core, (z + t + 1) % 4, y))
        for t in range(3)
    ]
    to_last = Hop(links, lambda: total.at[3, y, :, own()], lambda: from_last, lambda: device(1 - x, core, z, y))
    mine = lambda: result.at[:, lanes(core * half, half)]
    to_final = Hop(links, mine, mine, lambda: device(x, 1 - core, z, y))
    store = Near(links, lambda: result, lambda: out)
    links.ends.append(store)

    def add(index, landed):
        total[index] = (total[index].astype(jnp.float32) + landed.astype(jnp.float32)).astype(total.dtype)

    def first():
        for t in turns4:
            to_core[t].start()
        for near in load:
            near.start()

    def core_turn():
        for t in turns4:
            to_core[t].arrived()
            if far is None:
                to_core[t].left()
                add(t, owners(t, core)[...])
            else:
                load[t].arrived()
                add(t, far[t])
            to_x[t].start()

    def x_turn():
        for t in turns4:
            to_x[t].arrived()
            add((t, slice(None), slice(None), kept()), from_x[t])
            to_y[t].start()

    def y_turn():
        for t in range(3):
            to_y[t].arrived()
            add((t, y, slice(None), own()), from_y[t])
            to_z[t].start()

    def z_turn():
        to_y[3].arrived()
        everything = total[3, y, :, own()].astype(jnp.float32) + from_y[3].astype(jnp.float32)
        for t in range(3):
            to_z[t].arrived()
            everything = everything + from_z[t].astype(jnp.float32)
        total[3, y, :, own()] = everything.astype(total.dtype)
        to_last.start()

    def last_turn():
        to_last.arrived()
        middle = half - 2 * outer
        shared = total[3, y, :, lanes(outer, middle)].astype(jnp.float32) + from_last[:, lanes(x * outer, middle)].astype(jnp.float32)
        result[:, lanes(core * half + outer, middle)] = shared.astype(result.dtype)
        result[:, lanes(core * half + x * wide, outer)] = total[3, y, :, kept()]
        result[:, lanes(core * half + (1 - x) * wide, outer)] = from_last[:, lanes((1 - x) * middle, outer)]
        to_final.start()

    def end():
        to_final.arrived()
        store.start()

    return [first, core_turn, x_turn, y_turn, z_turn, last_turn, end]


REDUCE_HOPS, REDUCE_NEAR = 4 + 4 + 4 + 3 + 2, 5


def merged(units, every, lag=1):
    turns = []
    for i, unit in enumerate(units):
        for k, turn in enumerate(unit):
            at = i * every + k * lag
            turns += [[] for _ in range(at + 1 - len(turns))]
            turns[at].insert(0, turn)
    return turns


def run(turn):
    for action in turn:
        action()


def semaphores(hops, near):
    return [pltpu.SemaphoreType.DMA((hops,)), pltpu.SemaphoreType.DMA((hops,)), pltpu.SemaphoreType.DMA((max(near, 1),))]


def exchange_small(small, small_all, links, me):
    x, core, z, y = me
    number = lambda: (x * 2 + core) * 8 + z * 2 + y
    keep = Near(links, lambda: small.at[z * 2 + y], lambda: small_all.at[number()])
    few = [
        Hop(
            links,
            lambda k=k: small.at[(number() + k) % 8],
            lambda: small_all.at[number()],
            lambda k=k: (((number() + k) % 32) // 8, (number() + k) % 8),
        )
        for k in range(1, 32)
    ]

    def begin():
        keep.start()
        for hop in few:
            hop.start()

    def end():
        keep.arrived()
        for hop in few:
            hop.arrived()

    return begin, end


def factors_turns(links, me, factors, group, whole):
    x, core, z, y = me
    slots = factors.shape[0]
    mine = lambda: group.at[lines((x * 2 + core) * slots, slots), :]
    keep = Near(links, lambda: factors, mine)
    peers = [
        Hop(links, lambda: factors, mine, lambda i=i, j=j: device((x + i) % 2, (core + j) % 2, z, y)) for i, j in ((0, 1), (1, 0), (1, 1))
    ]

    def first():
        keep.start()
        for hop in peers:
            hop.start()

    def second():
        keep.arrived()
        for hop in peers:
            hop.arrived()

    turns = gather_turns(links, me, group, whole, 256)
    return [first, lambda: (second(), turns[0]())] + turns[1:]


FACTOR_HOPS, FACTOR_NEAR = 3 + GATHER_HOPS, 1 + GATHER_NEAR


def nt(a, b):
    return lax.dot_general(a, b, (((1,), (1,)), ((), ())), preferred_element_type=jnp.float32)


def tn(a, b):
    return lax.dot_general(a, b, (((0,), (0,)), ((), ())), preferred_element_type=jnp.float32)


def nn(a, b):
    return jnp.dot(a, b, preferred_element_type=jnp.float32)


def normalize(values):
    centred = values - jnp.mean(values, axis=1, keepdims=True)
    inverse = lax.rsqrt(jnp.mean(centred * centred, axis=1, keepdims=True) + EPSILON)
    return (centred * inverse, inverse)


def norm_back(grad_normed, normed, inverse):
    first_mean = jnp.mean(grad_normed, axis=1, keepdims=True)
    second_mean = jnp.mean(grad_normed * normed, axis=1, keepdims=True)
    return inverse * (grad_normed - first_mean - normed * second_mean)


def gelu_both(u):
    c = math.sqrt(2 / math.pi)
    square = u * u
    t = jnp.tanh(u * (c + (c * 0.044715) * square))
    half = 0.5 + 0.5 * t
    value = u * half
    return value, half + value * (1.0 - t) * (c + (3 * c * 0.044715) * square)


def loop(count, body):
    def step(i, carry):
        body(i)
        return carry

    lax.fori_loop(0, count, step, 0)


def attention_lanes(segment, slots):
    lane = jnp.arange(128) % 64
    hot = segment[:, None] == lane[None, :]
    listed = lane[None, :] <= slots
    query_lanes = (hot & listed).astype(jnp.bfloat16)
    ones = (lane >= LSE_LANE) & (lane < LSE_LANE + 3)
    key_lanes = jnp.where(listed & ~hot, -1e30, jnp.where(ones[None, :], 1.0, 0.0)).astype(jnp.bfloat16)
    return query_lanes, key_lanes


class Host:
    def __init__(self, links, turns, steps, per_step):
        self.links, self.turns, self.steps, self.per_step = links, turns, steps, per_step
        self.step = pl.program_id(0)

    def turn(self, index):
        for hook, turn in sorted(self.turns.items()):
            if hook < self.steps * self.per_step and hook % self.per_step == index:
                pl.when(self.step == hook // self.per_step)(functools.partial(run, turn))

    def finish(self):
        @pl.when(self.step == self.steps - 1)
        def _():
            for hook, turn in sorted(self.turns.items()):
                if hook >= self.steps * self.per_step:
                    run(turn)
            self.links.drain()


def even(turns, hooks):
    placed = {}
    for t, turn in enumerate(turns):
        placed.setdefault(t * hooks // len(turns), []).extend(turn)
    return placed


def placed(schedule):
    turns = {}
    for hook, turn in schedule:
        turns.setdefault(hook, []).insert(0, turn)
    return turns


class Idle:
    def turn(self, index):
        pass

    def finish(self):
        pass


ANY = pl.BlockSpec(memory_space=pl.ANY)


def call(kernel, grid, inputs, outputs, scratch=()):
    made = pl.pallas_call(
        kernel,
        grid=grid,
        out_shape=[jax.ShapeDtypeStruct(shape, kind) for shape, kind, _ in outputs],
        in_specs=[spec for _, spec in inputs],
        out_specs=[spec for _, _, spec in outputs],
        scratch_shapes=list(scratch),
        compiler_params=pltpu.CompilerParams(has_side_effects=True, vmem_limit_bytes=VMEM_LIMIT),
    )
    return made(*[array for array, _ in inputs])


def gather_kernel(widths, *refs):
    count = len(widths)
    small, shards, refs = refs[0], refs[1 : 1 + count], refs[1 + count :]
    small_all, wholes, sems = refs[0], refs[1 : 1 + count], refs[1 + count :]
    me, links = place(), Links(*sems)
    begin, end = exchange_small(small, small_all, links, me)
    units = []
    for shard, whole, width in zip(shards, wholes, widths):
        for first in range(0, width, 1024):
            columns = pl.ds(first, 1024)
            units.append(gather_turns(links, me, shard.at[:, columns], whole.at[:, columns], 128 if len(units) % 2 else 256))
    begin()
    for turn in merged(units, GATHER_EVERY):
        run(turn)
    end()
    links.drain()


def gather_all(small, shards):
    widths = [s.shape[1] for s in shards]
    units = sum(widths) // 1024
    out = call(
        functools.partial(gather_kernel, widths),
        (),
        [(small, ANY)] + [(s, ANY) for s in shards],
        [((32,) + small.shape[1:], small.dtype, ANY)] + [((8 * s.shape[0], s.shape[1]), s.dtype, ANY) for s in shards],
        semaphores(31 + GATHER_HOPS * units, 1 + GATHER_NEAR * units),
    )
    return out[0], out[1:]


def attend_kernel(shared, q_ref, k_ref, v_ref, ql_ref, kl_ref, *refs):
    if shared:
        shards, out_ref, qa_ref, wholes, *sems = refs
        me, links = place(), Links(*sems)
        units = [
            gather_turns(links, me, shards.at[i, half], wholes.at[i], 128 if half.start else 256, half.start)
            for i in range(shared)
            for half in HALVES
        ]
        host = Host(links, even(merged(units, GATHER_EVERY), D // 32), D // 128, 4)
    else:
        (out_ref, qa_ref), host = refs, Idle()
    rows = q_ref.shape[0]
    block = min(ATTENTION_ROWS, rows)
    low = lax.broadcasted_iota(jnp.int32, (1, 128), 1) < HEAD_DIM
    lane = lax.broadcasted_iota(jnp.int32, (1, 128), 1) % HEAD_DIM
    keys, vals = [], []
    for own in (low, ~low):
        keys.append(jnp.where(own, k_ref[...], kl_ref[...]))
        vals.append(jnp.where(own, v_ref[...], jnp.bfloat16(1)))
    for at, first in enumerate(range(0, rows, block)):
        here = pl.ds(first, block)
        queries = q_ref[here, :] * jnp.bfloat16(HEAD_DIM**-0.5)
        mixed = []
        for head, own in enumerate((low, ~low)):
            host.turn(2 * at + head)
            asked = jnp.where(own, queries, ql_ref[here, :])
            scores = nt(asked, keys[head])
            top = jnp.max(scores, axis=1, keepdims=True)
            weight = jnp.exp(scores - top).astype(jnp.bfloat16)
            both = nn(weight, vals[head])
            mixed.append(both)
            log_total = -(top + jnp.log(both))
            first_part = log_total.astype(jnp.bfloat16)
            rest = log_total - first_part.astype(jnp.float32)
            second = rest.astype(jnp.bfloat16)
            third = (rest - second.astype(jnp.float32)).astype(jnp.bfloat16)
            for i, part in enumerate((first_part, second, third)):
                asked = jnp.where(~own & (lane == LSE_LANE + i), part, asked)
            qa_ref[head, here, :] = asked
        total = pltpu.roll(jnp.where(low, mixed[1], mixed[0]), HEAD_DIM, 1)
        out_ref[here, :] = (jnp.where(low, mixed[0], mixed[1]) / total).astype(jnp.bfloat16)
    host.finish()


def attend(projected, query_lanes, key_lanes, shards=None):
    rows, pairs = projected.shape[0], D // 128
    spec = lambda shift: pl.BlockSpec((rows, 128), lambda i: (0, i + shift))
    same = pl.BlockSpec((rows, 128), lambda i: (0, 0))
    inputs = [(projected, spec(0)), (projected, spec(pairs)), (projected, spec(2 * pairs)), (query_lanes, same), (key_lanes, same)]
    outputs = [((rows, D), jnp.bfloat16, spec(0)), ((HEADS, rows, 128), jnp.bfloat16, pl.BlockSpec((2, rows, 128), lambda i: (i, 0, 0)))]
    if shards is None:
        return call(functools.partial(attend_kernel, 0), (pairs,), inputs, outputs)
    units, depth, width = shards.shape
    return call(
        functools.partial(attend_kernel, units),
        (pairs,),
        inputs + [(shards, ANY)],
        outputs + [((units, 8 * depth, width), shards.dtype, ANY)],
        semaphores(2 * GATHER_HOPS * units, 2 * GATHER_NEAR * units),
    )


def attend_back_kernel(counts, k_ref, v_ref, kl_ref, qa_ref, out_ref, go_ref, *refs):
    units = sum(counts)
    if units:
        groups, refs = refs[: len(counts)], refs[len(counts) :]
        small, factors, grad_ref, results, small_all, factor_group, factor_all, kt_ref, dqt_ref, *refs = refs
        summed, lands, sems = refs[0], refs[1 : 1 + 12 * units], refs[1 + 12 * units :]
        me, links = place(), Links(*sems)
        begin, end = exchange_small(small, small_all, links, me)
        locals_ = [group.at[i] for group, count in zip(groups, counts) for i in range(count)]
        plans = [
            reduce_turns(
                links, me, locals_[i // 2], i % 2 * 64, summed.at[i // 2, HALVES[i % 2]], results.at[i // 2, HALVES[i % 2]], lands[6 * i : 6 * i + 6]
            )
            for i in range(2 * units)
        ]
        plans.append(factors_turns(links, me, factors, factor_group, factor_all))
        turns = merged(plans, REDUCE_EVERY, 2)
        turns[0].append(begin)
        turns[-1].append(end)
        host = Host(links, even(turns, D // 32), D // 128, 4)
    else:
        (grad_ref, kt_ref, dqt_ref), host = refs, Idle()
    rows = k_ref.shape[0]
    block = min(ATTENTION_ROWS, rows)
    low = lax.broadcasted_iota(jnp.int32, (1, 128), 1) < HEAD_DIM
    grads = go_ref[...]
    product = pltpu.roll(-(grads.astype(jnp.float32) * out_ref[...].astype(jnp.float32)), HEAD_DIM, 1).astype(jnp.bfloat16)
    kt_ref[...] = k_ref[...].astype(jnp.float32).T.astype(jnp.bfloat16)
    given = [jnp.where(own, grads, product) for own in (low, ~low)]
    for at, first in enumerate(range(0, rows, block)):
        here = pl.ds(first, block)
        dks, dvs = [], []
        for head, own in enumerate((low, ~low)):
            host.turn(2 * at + head)
            keys = jnp.where(own, k_ref[here, :], kl_ref[here, :])
            vals = jnp.where(own, v_ref[here, :], jnp.bfloat16(1))
            probs = jnp.exp(nt(keys, qa_ref[head]))
            slopes = nt(vals, given[head])
            moved = (probs * slopes).astype(jnp.bfloat16)
            dvs.append(nn(probs.astype(jnp.bfloat16), grads))
            dks.append(nn(moved, qa_ref[head]))
            part = nn(kt_ref[head * HEAD_DIM : (head + 1) * HEAD_DIM, here], moved)
            where = pl.ds(head * HEAD_DIM, HEAD_DIM)
            if first == 0:
                dqt_ref[where, :] = part
            else:
                dqt_ref[where, :] += part
        grad_ref[1, here, :] = jnp.where(low, dks[0], dks[1]).astype(jnp.bfloat16)
        grad_ref[2, here, :] = jnp.where(low, dvs[0], dvs[1]).astype(jnp.bfloat16)
    grad_ref[0] = (dqt_ref[...].T * HEAD_DIM**-0.5).astype(jnp.bfloat16)
    host.finish()


VMEM = pl.BlockSpec(memory_space=pltpu.VMEM)


def attend_back(projected, key_lanes, asked, attn_out, grad_attn, groups=(), small=None, factors=None):
    rows, pairs = projected.shape[0], D // 128
    spec = lambda shift: pl.BlockSpec((rows, 128), lambda i: (0, i + shift))
    same = pl.BlockSpec((rows, 128), lambda i: (0, 0))
    two = pl.BlockSpec((2, rows, 128), lambda i: (i, 0, 0))
    inputs = [(projected, spec(pairs)), (projected, spec(2 * pairs)), (key_lanes, same), (asked, two), (attn_out, spec(0)), (grad_attn, spec(0))]
    outputs = [((3, rows, D), jnp.bfloat16, pl.BlockSpec((3, rows, 128), lambda i: (0, 0, i)))]
    scratch = [pltpu.VMEM((128, rows), jnp.bfloat16), pltpu.VMEM((128, rows), jnp.float32)]
    counts = [g.shape[0] for g in groups]
    units = sum(counts)
    if units:
        inputs += [(g, ANY) for g in groups] + [(small, ANY), (factors, ANY)]
        slots, width = factors.shape
        outputs += [((units, 128, D), jnp.bfloat16, ANY), ((32,) + small.shape[1:], small.dtype, ANY)]
        outputs += [((4 * slots, width), factors.dtype, ANY), ((32 * slots, width), factors.dtype, ANY)]
        scratch += [pltpu.VMEM((units, 128, D), jnp.bfloat16)] + [land for _ in range(2 * units) for land in reduce_lands(64)]
        scratch += semaphores(31 + FACTOR_HOPS + 2 * REDUCE_HOPS * units, 1 + FACTOR_NEAR + 2 * REDUCE_NEAR * units)
    return call(functools.partial(attend_back_kernel, counts), (pairs,), inputs, outputs, scratch)


def before_kernel(attn_ref, tok_ref, cot_ref, wout_ref, bout_ref, scale_ref, shift_ref, live_ref, middle_ref, hidden_ref, two_ref, gbdown_ref):
    r = pl.program_id(0)
    rows = tok_ref.shape[0]
    units = rows // UNIT

    @pl.when(r == 0)
    def _():
        gbdown_ref[...] = jnp.zeros_like(gbdown_ref)

    middle_ref[...] = nn(attn_ref[...], wout_ref[0]) + bout_ref[...].astype(jnp.float32)
    for i in range(units):
        u = r * units + i
        at = pl.ds(i * UNIT, UNIT)
        live = live_ref[pl.ds(u, 1), :]
        value = tok_ref[at, :].astype(jnp.float32) + live * middle_ref[at, :]
        middle_ref[at, :] = value
        normed, _ = normalize(value)
        hidden_ref[at, :] = (normed * (1.0 + scale_ref[pl.ds(u, 1), :]) + shift_ref[pl.ds(u, 1), :]).astype(jnp.bfloat16)
        grad = (live * cot_ref[at, :].astype(jnp.float32)).astype(jnp.bfloat16)
        two_ref[at, :] = grad
        gbdown_ref[...] += jnp.sum(grad.astype(jnp.float32), axis=0, keepdims=True)


def before_mlp(attn_out, tokens, cotangent, weights, b_out, scale, shift, live):
    rows = tokens.shape[0]
    block = pl.BlockSpec((256, D), lambda r: (r, 0))
    once = lambda shape: pl.BlockSpec(shape, lambda r: (0,) * len(shape))
    units = once((rows // UNIT, D))
    return call(
        before_kernel,
        (rows // 256,),
        [(attn_out, block), (tokens, block), (cotangent, block), (weights, once((1, D, D))), (b_out, once((1, D))), (scale, units), (shift, units), (live, units)],
        [((rows, D), jnp.float32, block), ((rows, D), jnp.bfloat16, block), ((rows, D), jnp.bfloat16, block), ((1, D), jnp.float32, once((1, D)))],
    )


def mlp_kernel(early, hidden, two, bup_ref, weights, *refs):
    j = pl.program_id(0)
    rows = hidden.shape[0]
    late = FF_BLOCKS - early
    if late:
        shards, acc, back, gbup_ref, grads_ref, results, act, pre, held, made, summed, *refs = refs
        lands, sems = refs[: 20 * early], refs[20 * early :]
    else:
        acc, back, gbup_ref, grads_ref, act, pre, held, made, *sems = refs
    slots = made.shape[0]
    me, links = place(), Links(*sems)
    fetch = [[Near(links, lambda b=b, w=w: weights.at[1 + 2 * b + w], lambda b=b, w=w: held.at[b, w]) for w in (0, 1)] for b in range(early)]
    store = [Near(links, lambda b=b: made.at[b % slots], lambda b=b: grads_ref.at[b - FF_BLOCKS + grads_ref.shape[0]]) for b in range(FF_BLOCKS)]
    kept_blocks = range(FF_BLOCKS - grads_ref.shape[0], FF_BLOCKS)
    if late:
        schedule = []
        for i in range(4 * late):
            b, w, half = early + i // 4, i // 2 % 2, HALVES[i % 2]
            unit = gather_turns(links, me, shards.at[i // 2, half], held.at[b, w], 128 if i % 2 else 256, half.start)
            schedule += [(GATHER_START * i + at, turn) for at, turn in zip(GATHER_LAGS, unit)]
        for i in range(4 * early):
            b, w, half = i // 4, i // 2 % 2, HALVES[i % 2]
            unit = reduce_turns(
                links, me, made.at[b % slots, w], half.start, summed.at[2 * b + w, half], results.at[2 * b + w, half], lands[5 * i : 5 * i + 5]
            )
            schedule += [(16 * (b + 1) + REDUCE_START * (i % 4) + at, turn) for at, turn in zip(REDUCE_LAGS, unit)]
        host = Host(links, placed(schedule), FF_BLOCKS, 16)
    else:
        host = Idle()

    @pl.when(j == 0)
    def _():
        for pair in fetch:
            for near in pair:
                near.start()

    host.turn(0)
    for b in range(early):

        @pl.when(j == b)
        def _():
            for near in fetch[b]:
                near.arrived()

    gbup_ref[...] = jnp.zeros_like(gbup_ref)
    up, down = held.at[j, 0], held.at[j, 1]
    block = rows // 4
    for r in range(4):
        if r:
            host.turn(2 * r)
        here = pl.ds(r * block, block)
        value, slope = gelu_both(nn(hidden[here, :], up[...]) + bup_ref[0].astype(jnp.float32))
        value = value.astype(jnp.bfloat16)
        grad = (nt(two[here, :], down[...]) * slope).astype(jnp.bfloat16)
        act[here, :] = value
        pre[here, :] = grad
        gbup_ref[0] += jnp.sum(grad.astype(jnp.float32), axis=0, keepdims=True)
        host.turn(2 * r + 1)
        forward, backward = nn(value, down[...]), nt(grad, up[...])

        @pl.when(j == 0)
        def _():
            acc[here, :] = forward
            back[here, :] = backward

        @pl.when(j > 0)
        def _():
            acc[here, :] += forward
            back[here, :] += backward

    slot = lax.rem(j, slots)
    for r in range(4):
        here = pl.ds(r * 256, 256)
        for w, (left, right) in enumerate(((hidden, pre), (act, two))):
            host.turn(8 + 2 * r + w)
            value = tn(left[:, here], right[...]).astype(jnp.bfloat16)
            for half in (0, 1):
                made[slot, w, 2 * r + half] = value[half * 128 : half * 128 + 128]
    for b in kept_blocks:
        pl.when(j == b)(store[b].start)

    @pl.when(j == FF_BLOCKS - 1)
    def _():
        for b in kept_blocks:
            store[b].arrived()

    host.finish()


def feed_forward(hidden, two, weights, b_up, shards=None):
    rows = hidden.shape[0]
    once = lambda shape: pl.BlockSpec(shape, lambda j: (0, 0), pipeline_mode=pl.Buffered(1))
    whole = once((rows, D))
    row = pl.BlockSpec((1, 1, D), lambda j: (j, 0, 0))
    f32, b16 = jnp.float32, jnp.bfloat16
    early = FF_BLOCKS if shards is None else EARLY
    late = FF_BLOCKS - early
    kept = late or FF_BLOCKS
    inputs = [(hidden, whole), (two, whole), (b_up, row), (weights, ANY)]
    outputs = [((rows, D), f32, whole), ((rows, D), f32, whole), ((FF_BLOCKS, 1, D), f32, row), ((kept, 2, 8, 128, D), b16, ANY)]
    slots = 2 if late else FF_BLOCKS
    scratch = [
        pltpu.VMEM((rows, D), b16), pltpu.VMEM((rows, D), b16), pltpu.VMEM((FF_BLOCKS, 2, D, D), b16), pltpu.VMEM((slots, 2, 8, 128, D), b16),
    ]
    hops, near = 1, 2 * early + FF_BLOCKS
    if late:
        inputs += [(shards, ANY)]
        outputs += [((2 * early, 128, D), b16, ANY)]
        scratch += [pltpu.VMEM((2 * early, 128, D), b16)] + [land for _ in range(4 * early) for land in reduce_lands(64, far=False)]
        hops = 4 * late * GATHER_HOPS + 4 * early * REDUCE_HOPS
        near += 4 * late * GATHER_NEAR + 4 * early * REDUCE_NEAR
    return call(functools.partial(mlp_kernel, early), (FF_BLOCKS,), inputs, outputs, scratch + semaphores(hops, near))


def after_kernel(
    middle_ref, acc_ref, back_ref, cot_ref, attn_ref, wout_ref, bdown_ref, scale_ref, live_ref,
    out_ref, mid_grad_ref, attn_grad_ref, gout_ref, gbout_ref, gscale_ref, gshift_ref, one_ref, total_ref,
):
    r = pl.program_id(0)
    rows = cot_ref.shape[0]
    units = rows // UNIT

    @pl.when(r == 0)
    def _():
        gbout_ref[...] = jnp.zeros_like(gbout_ref)
        total_ref[...] = jnp.zeros_like(total_ref)

    for i in range(units):
        u = r * units + i
        at = pl.ds(i * UNIT, UNIT)
        live = live_ref[pl.ds(u, 1), :]
        value = middle_ref[at, :]
        out_ref[at, :] = (value + live * (acc_ref[at, :] + bdown_ref[...].astype(jnp.float32))).astype(jnp.bfloat16)
        normed, inverse = normalize(value)
        grad = back_ref[at, :]
        gshift_ref[pl.ds(u, 1), :] = jnp.sum(grad, axis=0, keepdims=True)
        gscale_ref[pl.ds(u, 1), :] = jnp.sum(grad * normed, axis=0, keepdims=True)
        passed = cot_ref[at, :].astype(jnp.float32) + norm_back(grad * (1.0 + scale_ref[pl.ds(u, 1), :]), normed, inverse)
        mid_grad_ref[at, :] = passed
        one = (live * passed).astype(jnp.bfloat16)
        one_ref[at, :] = one
        gbout_ref[...] += jnp.sum(one.astype(jnp.float32), axis=0, keepdims=True)
    attn_grad_ref[...] = nt(one_ref[...], wout_ref[0]).astype(jnp.bfloat16)
    total_ref[...] += tn(attn_ref[...], one_ref[...])

    @pl.when(r == pl.num_programs(0) - 1)
    def _():
        for i in range(8):
            gout_ref[0, i] = total_ref[i * 128 : i * 128 + 128, :].astype(jnp.bfloat16)


def after_mlp(middle, acc, back, cotangent, attn_out, weights, b_down, scale, live):
    rows = middle.shape[0]
    block = pl.BlockSpec((256, D), lambda r: (r, 0))
    once = lambda shape: pl.BlockSpec(shape, lambda r: (0,) * len(shape))
    units, row = once((rows // UNIT, D)), once((1, D))
    f32, b16 = jnp.float32, jnp.bfloat16
    return call(
        after_kernel,
        (rows // 256,),
        [
            (middle, block), (acc, block), (back, block), (cotangent, block), (attn_out, block), (weights, once((1, D, D))),
            (b_down, row), (scale, units), (live, units),
        ],
        [
            ((rows, D), b16, block), ((rows, D), f32, block), ((rows, D), b16, block), ((1, 8, 128, D), b16, once((1, 8, 128, D))), ((1, D), f32, row),
            ((rows // UNIT, D), f32, units), ((rows // UNIT, D), f32, units),
        ],
        [pltpu.VMEM((256, D), b16), pltpu.VMEM((D, D), f32)],
    )


def head_kernel(tok_ref, scale_ref, shift_ref, w_ref, hidden_ref, out_ref):
    rows = tok_ref.shape[0]

    @pl.when(pl.program_id(0) == 0)
    def _():
        def unit(u):
            at = pl.ds(pl.multiple_of(u * UNIT, UNIT), UNIT)
            normed, _ = normalize(tok_ref[at, :].astype(jnp.float32))
            hidden_ref[at, :] = (normed * (1.0 + scale_ref[pl.ds(u, 1), :]) + shift_ref[pl.ds(u, 1), :]).astype(jnp.bfloat16)

        loop(rows // UNIT, unit)

    def block(r):
        here = pl.ds(pl.multiple_of(r * ROWS, ROWS), ROWS)
        out_ref[here, :] = nn(hidden_ref[here, :], w_ref[...]).astype(jnp.bfloat16)

    loop(rows // ROWS, block)


def project_in(tokens, scale, shift, w_qkv):
    rows = tokens.shape[0]
    whole = lambda shape: pl.BlockSpec(shape, lambda j: (0, 0))
    return pl.pallas_call(
        head_kernel,
        grid=(3,),
        out_shape=[jax.ShapeDtypeStruct((rows, D), jnp.bfloat16), jax.ShapeDtypeStruct((rows, 3 * D), jnp.bfloat16)],
        in_specs=[whole((rows, D)), whole((rows // UNIT, D)), whole((rows // UNIT, D)), pl.BlockSpec((D, D), lambda j: (0, j))],
        out_specs=[whole((rows, D)), pl.BlockSpec((rows, D), lambda j: (0, j))],
        compiler_params=pltpu.CompilerParams(vmem_limit_bytes=VMEM_LIMIT),
    )(tokens, scale, shift, w_qkv)


def tail_kernel(shared, grad_ref, hidden_ref, w_ref, tok_ref, mid_ref, scale_ref, *refs):
    p = pl.program_id(0)
    rows = tok_ref.shape[0]
    if shared:
        table_ref, results, gtok_ref, gscale_ref, gshift_ref, factor_group, factor_all, back, gw, summed, factors, *refs = refs
        lands, sems = refs[:30], refs[30:]
        me, links = place(), Links(*sems)
        schedule = []
        for i in range(6):
            half = HALVES[i % 2]
            unit = reduce_turns(
                links, me, gw.at[i // 2], half.start, summed.at[i // 2, half], results.at[i // 2, half], lands[5 * i : 5 * i + 5]
            )
            schedule += [(2 * (i // 2) + 1 + i % 2 + k, turn) for k, turn in enumerate(unit)]
        turns = placed(schedule)
        host = Host(links, {h: t for h, t in turns.items() if h < 12}, 6, 2)
        rest = [turns[h] for h in sorted(turns) if h >= 12]
        spread = factors_turns(links, me, factors, factor_group, factor_all)
    else:
        gw, gtok_ref, gscale_ref, gshift_ref, back = refs
        host = Idle()

    host.turn(0)

    @pl.when(p < 3)
    def _():
        for r in range(D // 256):
            value = tn(hidden_ref[:, r * 256 : r * 256 + 256], grad_ref[0]).astype(jnp.bfloat16)
            for half in (0, 1):
                gw[p if shared else 0, 2 * r + half] = value[half * 128 : half * 128 + 128]

    def way_back(first):
        for r in range(2):
            here = pl.ds(first + r * (rows // 4), rows // 4)
            part = nt(grad_ref[0, here, :], w_ref[...])

            @pl.when(p == 3)
            def _():
                back[here, :] = part

            @pl.when(p > 3)
            def _():
                back[here, :] += part

    pl.when(p >= 3)(functools.partial(way_back, 0))
    host.turn(1)
    pl.when(p >= 3)(functools.partial(way_back, rows // 2))

    @pl.when(p == pl.num_programs(0) - 1)
    def _():
        def unit(u):
            at = pl.ds(pl.multiple_of(u * UNIT, UNIT), UNIT)
            normed, inverse = normalize(tok_ref[at, :].astype(jnp.float32))
            grad = back[at, :]
            gshift_ref[pl.ds(u, 1), :] = jnp.sum(grad, axis=0, keepdims=True)
            gscale_ref[pl.ds(u, 1), :] = jnp.sum(grad * normed, axis=0, keepdims=True)
            gtok_ref[at, :] = mid_ref[at, :] + norm_back(grad * (1.0 + scale_ref[pl.ds(u, 1), :]), normed, inverse)

        loop(rows // UNIT, unit)
        if shared:
            table = table_ref[...].astype(jnp.bfloat16)
            for i, ref in enumerate((gscale_ref, gshift_ref)):
                whole, sums = ref[...], None
                for _ in range(3):
                    part = whole.astype(jnp.bfloat16)
                    whole = whole - part.astype(jnp.float32)
                    sums = nn(table, part) if sums is None else sums + nn(table, part)
                factors[:, i * D : (i + 1) * D] = sums.astype(jnp.bfloat16)
            for i in range(max(len(rest), len(spread))):
                if i < len(spread):
                    spread[i]()
                if i < len(rest):
                    run(rest[i])

    host.finish()


def project_back(grad_proj, hidden, w_qkv, tokens, grad_mid, scale, table=None):
    rows = tokens.shape[0]
    once = lambda shape: pl.BlockSpec(shape, lambda p: (0, 0), pipeline_mode=pl.Buffered(1))
    units, whole = once((rows // UNIT, D)), once((rows, D))
    f32, b16 = jnp.float32, jnp.bfloat16
    block = pl.BlockSpec((1, rows, D), lambda p: (lax.rem(p, 3), 0, 0))
    inputs = [
        (grad_proj, block), (hidden, whole), (w_qkv, pl.BlockSpec((D, D), lambda p: (0, jnp.maximum(p - 3, 0)))), (tokens, whole), (grad_mid, whole), (scale, units),
    ]
    outputs = [((rows, D), f32, whole), ((rows // UNIT, D), f32, units), ((rows // UNIT, D), f32, units)]
    scratch = [pltpu.VMEM((rows, D), f32)]
    shared = table is not None
    if shared:
        slots = table.shape[0]
        inputs += [(table, once(table.shape))]
        outputs = [((3, 128, D), b16, ANY)] + outputs
        outputs += [((4 * slots, 2 * D), b16, ANY), ((32 * slots, 2 * D), b16, ANY)]
        scratch += [pltpu.VMEM((3, 8, 128, D), b16), pltpu.VMEM((3, 128, D), b16), pltpu.VMEM((slots, 2 * D), b16)] + [land for _ in range(6) for land in reduce_lands(64, far=False)]
        scratch += semaphores(6 * REDUCE_HOPS + FACTOR_HOPS, 6 * REDUCE_NEAR + FACTOR_NEAR)
    else:
        outputs = [((3, 8, 128, D), b16, pl.BlockSpec((1, 8, 128, D), lambda p: (jnp.minimum(p, 2), 0, 0, 0)))] + outputs
    return call(functools.partial(tail_kernel, shared), (6,), inputs, outputs, scratch)


def tuned(sizes):
    return sizes == (4, 8)


def blocks_of(columns):
    return columns.reshape(columns.shape[0], FF_BLOCKS, -1).transpose(1, 0, 2)


def local(
    sizes, tokens, lengths, buckets, w_mod, b_mod, w_qkv, w_out, b_out, w_up, b_up, w_down, b_down, cotangent,
):
    rows, slots, n = tokens.shape[0], lengths.shape[1], sizes[1]
    own = tuned(sizes)
    segment, live, unit_table = layout(lengths[0], rows)
    feats = time_features(buckets[0]).astype(jnp.bfloat16)
    whole = lambda array: lax.all_gather(array, "fsdp", axis=0, tiled=True)
    if own:
        packed = jnp.concatenate([b_mod, b_out, b_up, b_down]).reshape(-1, 128)
        packed = jnp.pad(packed, ((0, 16 - packed.shape[0]), (0, 0)))
        by_owner = feats.reshape(slots, n, 128).transpose(1, 0, 2)
        small = jnp.concatenate([jnp.broadcast_to(packed, (n, 16, 128)), by_owner], axis=1)
        small_all, (full_mod, full_qkv) = gather_all(small, (w_mod, w_qkv))
        of_group = lax.dynamic_slice(small_all, (lax.axis_index("dp") * n, 0, 0), (n, 16, 128))
        full_bmod, full_bout, full_bdown = of_group[:, :4].reshape(-1), of_group[:, 4].reshape(1, -1), of_group[:, 9].reshape(1, -1)
        full_bup = of_group[:, 5:9].transpose(1, 0, 2).reshape(FF_BLOCKS, 1, -1)
        every_feats = small_all[:, 16:].reshape(sizes[0], n, slots, 128).transpose(1, 0, 2, 3).reshape(-1, 128)
    else:
        full_mod, full_qkv, full_bmod, full_bout, full_bup, full_bdown = [whole(a) for a in (w_mod, w_qkv, b_mod, b_out, b_up, b_down)]
        full_bout, full_bdown, full_bup = full_bout[None], full_bdown[None], full_bup.reshape(FF_BLOCKS, 1, -1)
        every_feats = lax.all_gather(feats, ("dp", "fsdp"), axis=0, tiled=True)
        every_feats = lax.dynamic_slice(every_feats, (0, lax.axis_index("fsdp") * (D // n)), (every_feats.shape[0], D // n))
    modulation = jnp.dot(feats, full_mod, preferred_element_type=jnp.float32) + full_bmod
    per_unit = jnp.dot(unit_table, modulation, precision=HIGHEST)
    scale_one, shift_one, scale_two, shift_two = [per_unit[:, i * D : (i + 1) * D] for i in range(4)]
    live_units = jnp.broadcast_to(live[:, None], (rows // UNIT, D))
    hidden_attn, projected = project_in(tokens, scale_one, shift_one, full_qkv)
    query_lanes, key_lanes = attention_lanes(jnp.repeat(segment, UNIT), slots)
    if own:
        ups = w_up.reshape(-1, n, FF_BLOCKS, 128).transpose(2, 0, 1, 3).reshape(FF_BLOCKS, 1, -1, D)
        downs = w_down.reshape(FF_BLOCKS, 1, -1, D)
        pairs = jnp.concatenate([ups, downs], axis=1).reshape(2 * FF_BLOCKS, -1, D)
        attn_out, asked, weights = attend(projected, query_lanes, key_lanes, jnp.concatenate([w_out[None], pairs[: 2 * EARLY]]))
        late = pairs[2 * EARLY :]
    else:
        attn_out, asked = attend(projected, query_lanes, key_lanes)
        pairs = jnp.stack([blocks_of(whole(w_up)), whole(w_down).reshape(FF_BLOCKS, D, D)], axis=1)
        weights, late = jnp.concatenate([whole(w_out)[None], pairs.reshape(2 * FF_BLOCKS, D, D)]), None
    middle, hidden_mlp, grad_two, grad_b_down = before_mlp(
        attn_out, tokens, cotangent, weights, full_bout, scale_two, shift_two, live_units
    )
    forward, backward, grad_b_up, grad_pairs, *totals_early = feed_forward(hidden_mlp, grad_two, weights, full_bup, late)
    output, grad_mid, grad_attn, grad_w_out, grad_b_out, grad_scale_two, grad_shift_two = after_mlp(
        middle, forward, backward, cotangent, attn_out, weights, full_bdown, scale_two, live_units
    )

    def factors_of(first, second):
        return jnp.dot(unit_table.T, jnp.concatenate([first, second], axis=1), precision=HIGHEST).astype(jnp.bfloat16)

    mod_two = factors_of(grad_scale_two, grad_shift_two)
    if own:
        sums = [grad_b_out.reshape(n, 1, 128), grad_b_up.reshape(FF_BLOCKS, n, 128).transpose(1, 0, 2), grad_b_down.reshape(n, 1, 128)]
        small = jnp.pad(jnp.concatenate(sums, axis=1), ((0, 0), (0, 2), (0, 0)))
        grad_proj, totals, small_all, _, mod_two = attend_back(
            projected, key_lanes, asked, attn_out, grad_attn, (grad_pairs.reshape(-1, 8, 128, D), grad_w_out), small, mod_two
        )
        total = jnp.sum(small_all, axis=0)
        sum_bout, sum_bup, sum_bdown = total[0], total[1:5].reshape(-1), total[5]
    else:
        grad_proj = attend_back(projected, key_lanes, asked, attn_out, grad_attn)[0]
    qkv_grads, grad_tokens, grad_scale_one, grad_shift_one, *factors = project_back(
        grad_proj, hidden_attn, full_qkv, tokens, grad_mid, scale_one, unit_table.T if own else None
    )
    if own:
        mod_one = factors[1]
    else:
        mod_one = factors_of(grad_scale_one, grad_shift_one)
        mod_one, mod_two = [lax.all_gather(m, ("dp", "fsdp"), axis=0, tiled=True) for m in (mod_one, mod_two)]
    sum_mod = jnp.concatenate(
        [jnp.einsum("sd,sc->dc", every_feats, m, preferred_element_type=jnp.float32) for m in (mod_one, mod_two)], axis=1
    )
    position, share = lax.axis_index("fsdp"), 4 * D // n
    chosen = jnp.where(position < n // 2, mod_one, mod_two)
    sum_bmod = jnp.sum(
        lax.dynamic_slice(chosen, (0, position % (n // 2) * share), (chosen.shape[0], share)), axis=0, dtype=jnp.float32
    )
    if own:
        totals, qkv_grads = totals.astype(jnp.float32), qkv_grads.astype(jnp.float32)
        pairs = jnp.concatenate([totals_early[0].astype(jnp.float32), totals[:-1]]).reshape(FF_BLOCKS, 2, 128, D)
        sum_up = pairs[:, 0].reshape(FF_BLOCKS, -1, n, 128).transpose(1, 2, 0, 3).reshape(w_up.shape)
        sum_down = pairs[:, 1].reshape(w_down.shape)
        sum_out = totals[-1]
        sum_qkv = qkv_grads.transpose(1, 0, 2).reshape(w_qkv.shape)
    else:
        summed = lambda a: lax.psum(lax.psum_scatter(a, "fsdp", scatter_dimension=0, tiled=True), "dp").astype(jnp.float32)
        sum_up = summed(grad_pairs[:, 0].reshape(FF_BLOCKS, D, D).transpose(1, 0, 2).reshape(D, -1))
        sum_down = summed(grad_pairs[:, 1].reshape(-1, D))
        sum_out, sum_qkv = summed(grad_w_out.reshape(D, D)), summed(qkv_grads.reshape(3, D, D).transpose(1, 0, 2).reshape(D, -1))
        sum_bout, sum_bup, sum_bdown = [summed(a.reshape(-1)) for a in (grad_b_out, grad_b_up, grad_b_down)]
    return output, grad_tokens, sum_mod, sum_bmod, sum_qkv, sum_out, sum_bout, sum_up, sum_bup, sum_down, sum_bdown


def solution(mesh):
    sizes = (mesh.shape["dp"], mesh.shape["fsdp"])
    rows, cut_rows, vector = P(("dp", "fsdp"), None), P("fsdp", None), P("fsdp")
    return jax.shard_map(
        functools.partial(local, sizes),
        mesh=mesh,
        in_specs=(rows, rows, rows, cut_rows, vector, cut_rows, cut_rows, vector, cut_rows, vector, cut_rows, vector, rows),
        out_specs=(rows, rows, cut_rows, vector, cut_rows, cut_rows, vector, cut_rows, vector, cut_rows, vector),
        check_vma=False,
    )
```

time: 2010 us -> 553 us (0.28)
  waiting for transfers between devices: 1360 us -> 0 us
  Pallas kernels: 0 us -> 499 us
  matrix products: 301 us -> 9.26 us
  blocking collectives: 135 us -> 0 us
  local copies, waits for them, and re-layouts: 113 us -> 22.8 us
  other arithmetic: 69 us -> 14.4 us
    reduce_scatter x5 -> x0, waiting for transfers between devices: 989 us -> none  [the longest x1 286 us: local(): lax.psum_scatter(grad_w_down, 'fsdp', scatter_dimension=0, tiled=True)]
    pallas_call x0 -> x8, Pallas kernels: none -> 499 us  [the longest x7 483 us: call(): return made(*[array for array, _ in inputs])]
    all_gather x5 -> x0, waiting for transfers between devices: 294 us -> none  [the longest x1 111 us: local(): lax.all_gather(w_down, 'fsdp', axis=0, tiled=True)]
    dot_general x72 -> x5, matrix products: 301 us -> 9.26 us  [the longest x1 4.58 us: local(): jnp.dot(feats, full_mod, preferred_element_type=jnp.float32) + full_bmod]
    all_gather x4 -> x0, blocking collectives: 93.8 us -> none  [the longest x1 26.6 us: local(): lax.all_gather(b_mod, 'fsdp', axis=0, tiled=True)]
    psum x1 -> x0, waiting for transfers between devices: 75.8 us -> none  [local(): lax.psum((attn_sums[0], attn_sums[1], attn_sums[2], attn_sums[3], attn_su...]
    unnamed x1 -> x0, blocking collectives: 33.4 us -> none
    reduce_sum x12 -> x3, other arithmetic: 29.3 us -> 2.89 us  [the longest x1 2.11 us: local(): jnp.sum(lax.dynamic_slice(chosen, (0, position % (n // 2) * share), (chos...]
  transfers between devices with their start and end apart: 11 -> 0, of which waited for: 9 -> 0; matrix products, arithmetic and copies ran while one was open for 20% -> 0% of each run, Pallas kernels for 0% -> 0%
where the time goes in v2:
time: 553 us; the launch traced here: 547 us
  Pallas kernels  499 us (90%)
  local copies, waits for them, and re-layouts  22.8 us (4%)
  other arithmetic  14.4 us (3%)
  matrix products  9.26 us (2%)
    pallas_call x7, Pallas kernels, call(): return made(*[array for array, _ in inputs])  483 us
    pallas_call x1, Pallas kernels, project_in(): pl.pallas_call(head_kernel, grid=(3,), out_shape=[jax.ShapeDtypeStruct((r...  15.5 us

profile of v2, /device:TPU:0, one launch (start us, length us, event | category | flops | bytes accessed | tf_op | source)
XLA Modules:
  0.0 546.8 jit_solution(12011253482690158489)
XLA Ops:
  0.7 0.7 convert_bitcast_fusion.1
  1.3 0.7 select_reduce_fusion
  2.3 0.7 maximum_bitcast_fusion.1
  3.1 0.6 fusion.14.refs_0_
  4.0 0.6 pad_maximum_fusion.4.refs_0_
  4.9 0.7 broadcast_in_dim.71.live_ref
  5.5 0.9 select_convert_fusion.kl_ref
  6.5 0.9 fusion.1.ql_ref
  7.4 1.8 reshape.145
  9.3 0.5 reshape.146
  9.8 0.6 copy-done.3
  10.4 1.2 pad_maximum_fusion.3
  11.6 1.2 pad_maximum_fusion.2.refs_0_
  12.7 82.8 %shard_map.212 = (bf16[32,32,128]{2,1,0:T(8,128)(2,1)}, bf16[1024,4096]{1,0:T(8,128)(2,1)}, bf16[1024,3072]{1,0:T(8,128)(2,1)}) custom-call(bf16[8,32,128]{2,1,0:T(8,128)(2,1)} %pad_maximum_fusion.4.refs_0_, bf16[128,4096]{1,0:T(8,128)(2,1)} %refs_1_.1, bf16[128,3072]{1,0:T(8,128)(2,1)} %refs_2_.1), custom_call_target="tpu_custom_call" | custom-call | tf_op jit(solution)/shard_map/pallas_call | solution.py:493
  95.5 1.3 dynamic-slice_bitcast_fusion.1
  96.9 0.8 dynamic-slice_bitcast_fusion
  97.7 0.9 slice.72
  98.6 4.6 convolution_add_fusion
  103.2 0.3 fusion.13
  103.5 0.7 fusion.20
  104.2 0.6 copy.38.bup_ref
  104.8 15.5 %shard_map.213 = (bf16[1024,1024]{1,0:T(8,128)(2,1)}, bf16[1024,3072]{1,0:T(8,128)(2,1)}) custom-call(bf16[1024,1024]{1,0:T(8,128)(2,1)} %tok_ref.5, f32[16,1024]{1,0:T(8,128)} %get-tuple-element.106.scale_ref, f32[16,1024]{1,0:T(8,128)} %get-tuple-element.105.shift_ref, bf16[1024,3072]{1,0:T(8,128)(2,1)} %get-tuple-element.44.w_ref), custom_call_target="tpu_custom_call" | custom-call | tf_op jit(solution)/shard_map/pallas_call | solution.py:896
  120.3 82.0 %shard_map.214 = (bf16[1024,1024]{1,0:T(8,128)(2,1)}, bf16[16,1024,128]{2,1,0:T(8,128)(2,1)}, bf16[5,1024,1024]{2,1,0:T(8,128)(2,1)}) custom-call(bf16[1024,3072]{1,0:T(8,128)(2,1)} %get-tuple-element.45.q_ref.k_ref.v_ref, bf16[1024,3072]{1,0:T(8,128)(2,1)} %get-tuple-element.45.q_ref.k_ref.v_ref, bf16[1024,3072]{1,0:T(8,128)(2,1)} %get-tuple-element.45.q_ref.k_ref.v_ref, ...), custom_call_target="tpu_custom_call" | custom-call | tf_op jit(solution)/shard_map/pallas_call | solution.py:493
  202.4 8.9 %shard_map.215 = (f32[1024,1024]{1,0:T(8,128)}, bf16[1024,1024]{1,0:T(8,128)(2,1)}, bf16[1024,1024]{1,0:T(8,128)(2,1)}, f32[1,1024]{1,0:T(1,128)}) custom-call(bf16[1024,1024]{1,0:T(8,128)(2,1)} %get-tuple-element.46.attn_ref.out_ref, bf16[1024,1024]{1,0:T(8,128)(2,1)} %tok_ref.5, bf16[1024,1024]{1,0:T(8,128)(2,1)} %cot_ref.3, ...), custom_call_target="tpu_custom_call" | custom-call | tf_op jit(solution)/shard_map/pallas_call | solution.py:493
  211.3 114.7 %shard_map.216 = (f32[1024,1024]{1,0:T(8,128)}, f32[1024,1024]{1,0:T(8,128)}, f32[4,1,1024]{2,1,0:T(1,128)}, bf16[2,2,8,128,1024]{4,3,2,1,0:T(8,128)(2,1)}, bf16[4,128,1024]{2,1,0:T(8,128)(2,1)}) custom-call(bf16[1024,1024]{1,0:T(8,128)(2,1)} %get-tuple-element.49.hidden, bf16[1024,1024]{1,0:T(8,128)(2,1)} %get-tuple-element.50.two, ...), custom_call_target="tpu_custom_call" | custom-call | tf_op jit(solution)/shard_map/pallas_call | solution.py:493
  326.0 15.2 %shard_map.217 = (bf16[1024,1024]{1,0:T(8,128)(2,1)}, f32[1024,1024]{1,0:T(8,128)}, bf16[1024,1024]{1,0:T(8,128)(2,1)}, bf16[1,8,128,1024]{3,2,1,0:T(8,128)(2,1)...) custom-call(f32[1024,1024]{1,0:T(8,128)} %get-tuple-element.48.middle_ref, ...), custom_call_target="tpu_custom_call" | custom-call | tf_op jit(solution)/shard_map/pallas_call | solution.py:493
  341.3 1.3 select_maximum_fusion.refs_2_
  342.6 1.8 convolution_convert_fusion.refs_3_
  344.4 91.4 %shard_map.218 = (bf16[3,1024,1024]{2,1,0:T(8,128)(2,1)}, bf16[5,128,1024]{2,1,0:T(8,128)(2,1)}, f32[32,8,128]{2,1,0:T(8,128)}, bf16[64,2048]{1,0:T(8,128)(2,1)}, bf16[512,2048]{1,0:T(8,128)(2,1)}) custom-call(bf16[1024,3072]{1,0:T(8,128)(2,1)} %get-tuple-element.45.q_ref.k_ref.v_ref, bf16[1024,3072]{1,0:T(8,128)(2,1)} %get-tuple-element.45.q_ref.k_ref.v_ref, ...), custom_call_target="tpu_custom_call" | custom-call | tf_op jit(solution)/shard_map/pallas_call | solution.py:493
  435.9 88.3 %shard_map.219 = (bf16[3,128,1024]{2,1,0:T(8,128)(2,1)}, f32[1024,1024]{1,0:T(8,128)}, f32[16,1024]{1,0:T(8,128)}, f32[16,1024]{1,0:T(8,128)}, bf16[64,2048]{1,0:T(8,128)(2,1)}, /*index=5*/bf16[512,2048]{1,0:T(8,128)(2,1)}) custom-call(bf16[3,1024,1024]{2,1,0:T(8,128)(2,1)} %get-tuple-element.63.grad_ref, bf16[1024,1024]{1,0:T(8,128)(2,1)} %get-tuple-element.64.hidden_ref, ...), custom_call_target="tpu_custom_call" | custom-call | tf_op jit(solution)/shard_map/pallas_call | solution.py:493
  524.2 2.1 convert_reduce_fusion
  526.3 2.1 fusion.21
  528.4 0.5 fusion.22
  528.9 1.5 pad_maximum_fusion.1
  530.4 0.5 slice_bitcast_fusion.2
  530.9 0.6 slice_bitcast_fusion.1
  531.7 0.5 copy.41
  532.2 1.6 copy.43
  533.8 0.2 slice.87
  534.1 0.3 convert_element_type.70
  534.4 0.8 slice_bitcast_fusion
  535.3 0.2 convert_element_type.71
  535.5 0.6 pad_maximum_fusion
  536.1 1.7 fusion.19
  537.9 0.5 copy.44
  538.3 1.4 copy.47
  539.7 1.9 reshape.158
  541.5 4.8 copy.50
  (38 shorter events, 1.2 us)
Async XLA Ops:
  9.2 1.2 copy-start.3
  10.4 1.2 copy-start.5
  326.0 15.3 %copy-start.7 = (f32[4,1,1024]{2,1,0:T(1,128)S(1)}, f32[4,1,1024]{2,1,0:T(1,128)}, u32[]{:S(2)}) copy-start(f32[4,1,1024]{2,1,0:T(1,128)} %get-tuple-element.59) | copy-start | bytes 49156
  326.0 15.3 %copy-start.8 = (f32[1,1024]{1,0:T(1,128)S(1)}, f32[1,1024]{1,0:T(1,128)}, u32[]{:S(2)}) copy-start(f32[1,1024]{1,0:T(1,128)} %get-tuple-element.60) | copy-start | bytes 12292
  524.2 4.2 copy-start.1
  528.9 1.5 copy-start.6
  528.9 2.6 copy-start.4
  532.2 1.6 copy-start
  534.0 1.2 copy-start.2

commit v3 on v2

--- a/solution.py
+++ b/solution.py
@@ -18,10 +18,12 @@
 FF_BLOCKS = 4
 EARLY = 2
 LSE_LANE = 24
-GATHER_EVERY = 1
-REDUCE_EVERY = 1
-GATHER_START, GATHER_LAGS = 3, (0, 5, 10, 15, 18)
-REDUCE_START, REDUCE_LAGS = 3, (0, 3, 9, 16, 22, 26, 28)
+ATTEND_GATHER = (3, (0, 4, 8, 12, 15))
+MLP_GATHER = (3, (0, 5, 10, 15, 18))
+MLP_REDUCE = (20, 4, (0, 2, 6, 11, 16, 19, 21))
+BACK_REDUCE = (2.6, (0, 2, 5, 8, 11, 13, 15))
+BACK_FACTORS = (1, 4, 8, 12, 16, 19)
+TAIL_REDUCE = (0, 2, 5, 9, 13, 16, 18)
 VMEM_LIMIT = 62 * 2**20
 HIGHEST = lax.Precision.HIGHEST
 MESH = pl.DeviceIdType.MESH
@@ -106,8 +108,8 @@
         for hop in self.hops:
             if not hop.gone:
                 hop.left()
-        for near in self.ends:
-            near.arrived()
+        for end in self.ends:
+            end()
 
 
 def lanes(at, size):
@@ -126,46 +128,38 @@
     rows, width = shard.shape
     half = width // 2
     inner = half - 2 * outer
-
-    def own():
-        return lanes(core * half + x * outer, outer + inner)
-
-    def crossing():
-        return lanes(core * half + x * (outer + inner), outer)
-
-    def full():
-        return lanes(core * half, half)
-
-    def block(way, k):
-        return ((z - k + 4) % 4) * 2 + (y if way == "z" else 1 - y)
+    own = lanes(core * half + x * outer, outer + inner)
+    crossing = lanes(core * half + x * (outer + inner), outer)
+    full = lanes(core * half, half)
 
     def place_of(index):
         return lines(index * rows, rows) if at is None else lines(index * 128 + at, rows)
 
-    def part(index, columns):
-        return whole.at[place_of(index), columns]
-
-    def mine():
-        return z * 2 + y
+    mine = place_of(z * 2 + y)
+    blocks = {}
+    for k in range(4):
+        source = ((z - k + 4) % 4) * 2
+        blocks["z", k], blocks["y", k] = place_of(source + y), place_of(source + 1 - y)
+    to_z = {k: device(x, core, (z + k) % 4, y) for k in (1, 2, 3)}
+    to_y, to_x, to_core = device(x, core, z, 1 - y), device(1 - x, core, z, y), device(x, 1 - core, z, y)
 
     def from_shard(target):
-        return Hop(links, lambda: shard.at[:, own()], lambda: part(mine(), own()), target)
+        return Hop(links, lambda: shard.at[:, own], lambda: whole.at[mine, own], lambda: target)
 
     def pass_on(way, k, columns, target):
-        def at():
-            return part(block(way, k), columns())
-
-        return Hop(links, at, at, target)
-
-    to_y = lambda: device(x, core, z, 1 - y)
-    keep = Near(links, lambda: shard, lambda: whole.at[place_of(mine()), :])
-    along_z = {k: from_shard(lambda k=k: device(x, core, (z + k) % 4, y)) for k in (1, 2, 3)}
+        def ref():
+            return whole.at[blocks[way, k], columns]
+
+        return Hop(links, ref, ref, lambda: target)
+
+    keep = Near(links, lambda: shard, lambda: whole.at[mine, :])
+    along_z = {k: from_shard(to_z[k]) for k in (1, 2, 3)}
     along_y = {0: from_shard(to_y)}
     for k in (1, 2, 3):
         along_y[k] = pass_on("z", k, own, to_y)
     order = [("z", 1), ("y", 0), ("z", 2), ("y", 1), ("z", 3), ("y", 2), ("y", 3)]
-    crossed = [pass_on(way, k, crossing, lambda: device(1 - x, core, z, y)) for way, k in order] if outer else None
-    handed = [pass_on(way, k, full, lambda: device(x, 1 - core, z, y)) for way, k in order]
+    crossed = [pass_on(way, k, crossing, to_x) for way, k in order] if outer else None
+    handed = [pass_on(way, k, full, to_core) for way, k in order]
 
     def first():
         for k in (1, 2, 3):
@@ -222,36 +216,27 @@
     outer = half // 4
     wide = half - outer
 
-    def own():
-        return lanes(x * outer, wide)
-
-    def kept():
-        return lanes(x * wide, outer)
-
-    def given():
-        return lanes((1 - x) * wide, outer)
-
-    def owners(t, side):
-        return local.at[pl.ds(((z + t + 1) % 4) * 2, 2), pl.ds(at, rows), lanes(side * half, half)]
+    own, kept, given = lanes(x * outer, wide), lanes(x * wide, outer), lanes((1 - x) * wide, outer)
+    sides, here = {True: lanes(core * half, half), False: lanes((1 - core) * half, half)}, pl.ds(at, rows)
+    owners_of = [pl.ds(((z + t + 1) % 4) * 2, 2) for t in range(4)]
+    other = 1 - y
+    at_core, at_x, at_y = device(x, 1 - core, z, y), device(1 - x, core, z, y), device(x, core, z, other)
+    at_z = [device(x, core, (z + t + 1) % 4, y) for t in range(3)]
+
+    def owners(t, ours):
+        return local.at[owners_of[t], here, sides[ours]]
 
     turns4 = range(4)
-    load = [Near(links, lambda t=t: owners(t, core), lambda t=t: far.at[t]) for t in turns4] if far is not None else []
-    to_core = [Hop(links, lambda t=t: owners(t, 1 - core), lambda t=t: total.at[t], lambda: device(x, 1 - core, z, y)) for t in turns4]
-    to_x = [
-        Hop(links, lambda t=t: total.at[t, :, :, given()], lambda t=t: from_x.at[t], lambda: device(1 - x, core, z, y)) for t in turns4
-    ]
-    to_y = [
-        Hop(links, lambda t=t: total.at[t, 1 - y, :, own()], lambda t=t: from_y.at[t], lambda: device(x, core, z, 1 - y)) for t in turns4
-    ]
-    to_z = [
-        Hop(links, lambda t=t: total.at[t, y, :, own()], lambda t=t: from_z.at[t], lambda t=t: device(x, core, (z + t + 1) % 4, y))
-        for t in range(3)
-    ]
-    to_last = Hop(links, lambda: total.at[3, y, :, own()], lambda: from_last, lambda: device(1 - x, core, z, y))
-    mine = lambda: result.at[:, lanes(core * half, half)]
-    to_final = Hop(links, mine, mine, lambda: device(x, 1 - core, z, y))
+    load = [Near(links, lambda t=t: owners(t, True), lambda t=t: far.at[t]) for t in turns4] if far is not None else []
+    to_core = [Hop(links, lambda t=t: owners(t, False), lambda t=t: total.at[t], lambda: at_core) for t in turns4]
+    to_x = [Hop(links, lambda t=t: total.at[t, :, :, given], lambda t=t: from_x.at[t], lambda: at_x) for t in turns4]
+    to_y = [Hop(links, lambda t=t: total.at[t, other, :, own], lambda t=t: from_y.at[t], lambda: at_y) for t in turns4]
+    to_z = [Hop(links, lambda t=t: total.at[t, y, :, own], lambda t=t: from_z.at[t], lambda t=t: at_z[t]) for t in range(3)]
+    to_last = Hop(links, lambda: total.at[3, y, :, own], lambda: from_last, lambda: at_x)
+    mine = lambda: result.at[:, sides[True]]
+    to_final = Hop(links, mine, mine, lambda: at_core)
     store = Near(links, lambda: result, lambda: out)
-    links.ends.append(store)
+    links.ends.append(store.arrived)
 
     def add(index, landed):
         total[index] = (total[index].astype(jnp.float32) + landed.astype(jnp.float32)).astype(total.dtype)
@@ -267,7 +252,7 @@
             to_core[t].arrived()
             if far is None:
                 to_core[t].left()
-                add(t, owners(t, core)[...])
+                add(t, owners(t, True)[...])
             else:
                 load[t].arrived()
                 add(t, far[t])
@@ -276,22 +261,22 @@
     def x_turn():
         for t in turns4:
             to_x[t].arrived()
-            add((t, slice(None), slice(None), kept()), from_x[t])
+            add((t, slice(None), slice(None), kept), from_x[t])
             to_y[t].start()
 
     def y_turn():
         for t in range(3):
             to_y[t].arrived()
-            add((t, y, slice(None), own()), from_y[t])
+            add((t, y, slice(None), own), from_y[t])
             to_z[t].start()
 
     def z_turn():
         to_y[3].arrived()
-        everything = total[3, y, :, own()].astype(jnp.float32) + from_y[3].astype(jnp.float32)
+        everything = total[3, y, :, own].astype(jnp.float32) + from_y[3].astype(jnp.float32)
         for t in range(3):
             to_z[t].arrived()
             everything = everything + from_z[t].astype(jnp.float32)
-        total[3, y, :, own()] = everything.astype(total.dtype)
+        total[3, y, :, own] = everything.astype(total.dtype)
         to_last.start()
 
     def last_turn():
@@ -299,7 +284,7 @@
         middle = half - 2 * outer
         shared = total[3, y, :, lanes(outer, middle)].astype(jnp.float32) + from_last[:, lanes(x * outer, middle)].astype(jnp.float32)
         result[:, lanes(core * half + outer, middle)] = shared.astype(result.dtype)
-        result[:, lanes(core * half + x * wide, outer)] = total[3, y, :, kept()]
+        result[:, lanes(core * half + x * wide, outer)] = total[3, y, :, kept]
         result[:, lanes(core * half + (1 - x) * wide, outer)] = from_last[:, lanes((1 - x) * middle, outer)]
         to_final.start()
 
@@ -334,14 +319,14 @@
 
 def exchange_small(small, small_all, links, me):
     x, core, z, y = me
-    number = lambda: (x * 2 + core) * 8 + z * 2 + y
-    keep = Near(links, lambda: small.at[z * 2 + y], lambda: small_all.at[number()])
+    number = (x * 2 + core) * 8 + z * 2 + y
+    keep = Near(links, lambda: small.at[z * 2 + y], lambda: small_all.at[number])
     few = [
         Hop(
             links,
-            lambda k=k: small.at[(number() + k) % 8],
-            lambda: small_all.at[number()],
-            lambda k=k: (((number() + k) % 32) // 8, (number() + k) % 8),
+            lambda k=k: small.at[(number + k) % 8],
+            lambda: small_all.at[number],
+            lambda k=k: (((number + k) % 32) // 8, (number + k) % 8),
         )
         for k in range(1, 32)
     ]
@@ -455,11 +440,8 @@
             self.links.drain()
 
 
-def even(turns, hooks):
-    placed = {}
-    for t, turn in enumerate(turns):
-        placed.setdefault(t * hooks // len(turns), []).extend(turn)
-    return placed
+def timed(units, every, lags, first=0):
+    return [(int(first + every * i) + lag, turn) for i, unit in enumerate(units) for lag, turn in zip(lags, unit)]
 
 
 def placed(schedule):
@@ -478,6 +460,7 @@
 
 
 ANY = pl.BlockSpec(memory_space=pl.ANY)
+VMEM = pl.BlockSpec(memory_space=pltpu.VMEM)
 
 
 def call(kernel, grid, inputs, outputs, scratch=()):
@@ -493,35 +476,145 @@
     return made(*[array for array, _ in inputs])
 
 
-def gather_kernel(widths, *refs):
-    count = len(widths)
-    small, shards, refs = refs[0], refs[1 : 1 + count], refs[1 + count :]
-    small_all, wholes, sems = refs[0], refs[1 : 1 + count], refs[1 + count :]
+def exact(table, values):
+    sums = None
+    for _ in range(3):
+        part = values.astype(jnp.bfloat16)
+        values = values - part.astype(jnp.float32)
+        sums = nn(table, part) if sums is None else sums + nn(table, part)
+    return sums
+
+
+def modulation_turns(links, me, parts, from_y, from_z, columns):
+    x, core, z, y = me
+    block = lambda t, side: parts.at[((z + t + 1) % 4) * 2 + side, :, columns]
+    to_y = [Hop(links, lambda t=t: block(t, 1 - y), lambda t=t: from_y.at[t, :, columns], lambda: device(x, core, z, 1 - y)) for t in range(4)]
+    to_z = [
+        Hop(links, lambda t=t: block(t, y), lambda t=t: from_z.at[t, :, columns], lambda t=t: device(x, core, (z + t + 1) % 4, y))
+        for t in range(3)
+    ]
+
+    def begin():
+        for hop in to_y:
+            hop.start()
+
+    def middle():
+        for t in range(3):
+            to_y[t].arrived()
+            block(t, y)[...] = (block(t, y)[...].astype(jnp.float32) + from_y[t, :, columns].astype(jnp.float32)).astype(parts.dtype)
+            to_z[t].start()
+
+    def end():
+        to_y[3].arrived()
+        total = block(3, y)[...].astype(jnp.float32) + from_y[3, :, columns].astype(jnp.float32)
+        for t in range(3):
+            to_z[t].arrived()
+            total = total + from_z[t, :, columns].astype(jnp.float32)
+        return total
+
+    return begin, middle, end
+
+
+def first_kernel(small, wmod_ref, wqkv, tok_ref, table_ref, small_all, wholes, hidden_ref, out_ref, unit_ref, landed, held, normed, *refs):
+    parts, from_y, from_z, sems = refs[:2], refs[2:4], refs[4:6], refs[6:]
     me, links = place(), Links(*sems)
-    begin, end = exchange_small(small, small_all, links, me)
-    units = []
-    for shard, whole, width in zip(shards, wholes, widths):
-        for first in range(0, width, 1024):
-            columns = pl.ds(first, 1024)
-            units.append(gather_turns(links, me, shard.at[:, columns], whole.at[:, columns], 128 if len(units) % 2 else 256))
+    x, core, z, y = me
+    group = (x * 2 + core) * 8
+    rows = tok_ref.shape[0]
+    begin, end = exchange_small(small, landed, links, me)
+    units = [
+        gather_turns(links, me, wqkv.at[half, pl.ds(i * D, D)], held.at[i], 128 if half.start else 256, half.start)
+        for i in range(3)
+        for half in HALVES
+    ]
+    gather = merged(units, 1)
+    halves = [modulation_turns(links, me, parts[i], from_y[i], from_z[i], pl.ds(0, 2 * D)) for i in (0, 1)]
+    keep = [Near(links, lambda i=i: held.at[i], lambda i=i: wholes.at[i]) for i in range(3)]
+    save = Near(links, lambda: landed, lambda: small_all)
+    links.ends += [near.arrived for near in keep + [save]]
+
+    def norm(first):
+        def unit(u):
+            at = pl.ds(pl.multiple_of(u * UNIT, UNIT), UNIT)
+            normed[at, :] = normalize(tok_ref[at, :].astype(jnp.float32))[0]
+
+        loop(rows // UNIT // 2, lambda i: unit(first + i))
+
+    def settle(half):
+        total = halves[half][2]()
+        table = table_ref[...].astype(jnp.bfloat16)
+        for f in range(4):
+            bias = landed[group + 4 * half + f, :16, :].astype(jnp.float32)
+            for i in range(4):
+                at = (4 * f + i) * 128
+                value = total[:, at : at + 128] + bias[i : i + 1, :]
+                unit_ref[:, 2 * half * D + at : 2 * half * D + at + 128] = exact(table, value)
+
+    def project(i):
+        def block(r):
+            here = pl.ds(pl.multiple_of(r * 256, 256), 256)
+            out_ref[here, i * D : (i + 1) * D] = nn(hidden_ref[here, :], held[i]).astype(jnp.bfloat16)
+
+        loop(rows // 256, block)
+
     begin()
-    for turn in merged(units, GATHER_EVERY):
-        run(turn)
+    run(gather[0])
+    norm(0)
+    run(gather[1])
+    norm(rows // UNIT // 2)
     end()
+    save.start()
+    for f in range(8):
+        part = nn(landed[group + f, 16:, :], wmod_ref[...])
+        for half in (0, 1):
+            parts[half][f] = part[:, half * 2 * D : (half + 1) * 2 * D].astype(parts[half].dtype)
+    halves[0][0]()
+    run(gather[2])
+    halves[0][1]()
+    halves[1][0]()
+    run(gather[3])
+    settle(0)
+    halves[1][1]()
+
+    def shape(u):
+        at = pl.ds(pl.multiple_of(u * UNIT, UNIT), UNIT)
+        hidden_ref[at, :] = (normed[at, :] * (1.0 + unit_ref[pl.ds(u, 1), :D]) + unit_ref[pl.ds(u, 1), D : 2 * D]).astype(jnp.bfloat16)
+
+    run(gather[4])
+    loop(rows // UNIT, shape)
+    run(gather[5])
+    keep[0].start()
+    project(0)
+    run(gather[6])
+    settle(1)
+    run(gather[7])
+    keep[1].start()
+    project(1)
+    run(gather[8])
+    run(gather[9])
+    keep[2].start()
+    project(2)
     links.drain()
 
 
-def gather_all(small, shards):
-    widths = [s.shape[1] for s in shards]
-    units = sum(widths) // 1024
-    out = call(
-        functools.partial(gather_kernel, widths),
+def first_all(small, w_mod, w_qkv, tokens, table):
+    rows, (units, slots) = tokens.shape[0], table.shape
+    b16, f32 = jnp.bfloat16, jnp.float32
+    hops = 31 + 6 * GATHER_HOPS + 14
+    return call(
+        first_kernel,
         (),
-        [(small, ANY)] + [(s, ANY) for s in shards],
-        [((32,) + small.shape[1:], small.dtype, ANY)] + [((8 * s.shape[0], s.shape[1]), s.dtype, ANY) for s in shards],
-        semaphores(31 + GATHER_HOPS * units, 1 + GATHER_NEAR * units),
+        [(small, ANY), (w_mod, VMEM), (w_qkv, ANY), (tokens, VMEM), (table, VMEM)],
+        [
+            ((32,) + small.shape[1:], b16, ANY), ((3, D, D), b16, ANY), ((rows, D), b16, VMEM), ((rows, 3 * D), b16, VMEM),
+            ((units, 4 * D), f32, VMEM),
+        ],
+        [
+            pltpu.VMEM((32,) + small.shape[1:], b16), pltpu.VMEM((3, D, D), b16), pltpu.VMEM((rows, D), f32),
+        ]
+        + [pltpu.VMEM((count, slots, 2 * D), kind) for count in (8, 4, 3) for kind in (f32, b16)]
+        + semaphores(hops, 1 + 6 * GATHER_NEAR + 4),
     )
-    return out[0], out[1:]
 
 
 def attend_kernel(shared, q_ref, k_ref, v_ref, ql_ref, kl_ref, *refs):
@@ -533,7 +626,7 @@
             for i in range(shared)
             for half in HALVES
         ]
-        host = Host(links, even(merged(units, GATHER_EVERY), D // 32), D // 128, 4)
+        host = Host(links, placed(timed(units, *ATTEND_GATHER)), D // 128, 4)
     else:
         (out_ref, qa_ref), host = refs, Idle()
     rows = q_ref.shape[0]
@@ -602,11 +695,10 @@
             )
             for i in range(2 * units)
         ]
-        plans.append(factors_turns(links, me, factors, factor_group, factor_all))
-        turns = merged(plans, REDUCE_EVERY, 2)
-        turns[0].append(begin)
-        turns[-1].append(end)
-        host = Host(links, even(turns, D // 32), D // 128, 4)
+        schedule = list(zip(BACK_FACTORS, factors_turns(links, me, factors, factor_group, factor_all)))
+        schedule = [(0, begin)] + schedule + timed(plans, *BACK_REDUCE)
+        links.ends += [end]
+        host = Host(links, placed(schedule), D // 128, 4)
     else:
         (grad_ref, kt_ref, dqt_ref), host = refs, Idle()
     rows = k_ref.shape[0]
@@ -640,9 +732,6 @@
     host.finish()
 
 
-VMEM = pl.BlockSpec(memory_space=pltpu.VMEM)
-
-
 def attend_back(projected, key_lanes, asked, attn_out, grad_attn, groups=(), small=None, factors=None):
     rows, pairs = projected.shape[0], D // 128
     spec = lambda shift: pl.BlockSpec((rows, 128), lambda i: (0, i + shift))
@@ -714,17 +803,19 @@
     store = [Near(links, lambda b=b: made.at[b % slots], lambda b=b: grads_ref.at[b - FF_BLOCKS + grads_ref.shape[0]]) for b in range(FF_BLOCKS)]
     kept_blocks = range(FF_BLOCKS - grads_ref.shape[0], FF_BLOCKS)
     if late:
-        schedule = []
+        gathers, reduces = [], []
         for i in range(4 * late):
             b, w, half = early + i // 4, i // 2 % 2, HALVES[i % 2]
-            unit = gather_turns(links, me, shards.at[i // 2, half], held.at[b, w], 128 if i % 2 else 256, half.start)
-            schedule += [(GATHER_START * i + at, turn) for at, turn in zip(GATHER_LAGS, unit)]
+            gathers.append(gather_turns(links, me, shards.at[i // 2, half], held.at[b, w], 128 if i % 2 else 256, half.start))
         for i in range(4 * early):
             b, w, half = i // 4, i // 2 % 2, HALVES[i % 2]
-            unit = reduce_turns(
-                links, me, made.at[b % slots, w], half.start, summed.at[2 * b + w, half], results.at[2 * b + w, half], lands[5 * i : 5 * i + 5]
+            reduces.append(
+                reduce_turns(
+                    links, me, made.at[b % slots, w], half.start, summed.at[2 * b + w, half], results.at[2 * b + w, half], lands[5 * i : 5 * i + 5]
+                )
             )
-            schedule += [(16 * (b + 1) + REDUCE_START * (i % 4) + at, turn) for at, turn in zip(REDUCE_LAGS, unit)]
+        first, every, lags = MLP_REDUCE
+        schedule = timed(gathers, *MLP_GATHER) + timed(reduces, every, lags, first)
         host = Host(links, placed(schedule), FF_BLOCKS, 16)
     else:
         host = Idle()
@@ -885,7 +976,7 @@
 
     def block(r):
         here = pl.ds(pl.multiple_of(r * ROWS, ROWS), ROWS)
-        out_ref[here, :] = nn(hidden_ref[here, :], w_ref[...]).astype(jnp.bfloat16)
+        out_ref[here, :] = nn(hidden_ref[here, :], w_ref[0]).astype(jnp.bfloat16)
 
     loop(rows // ROWS, block)
 
@@ -897,7 +988,7 @@
         head_kernel,
         grid=(3,),
         out_shape=[jax.ShapeDtypeStruct((rows, D), jnp.bfloat16), jax.ShapeDtypeStruct((rows, 3 * D), jnp.bfloat16)],
-        in_specs=[whole((rows, D)), whole((rows // UNIT, D)), whole((rows // UNIT, D)), pl.BlockSpec((D, D), lambda j: (0, j))],
+        in_specs=[whole((rows, D)), whole((rows // UNIT, D)), whole((rows // UNIT, D)), pl.BlockSpec((1, D, D), lambda j: (j, 0, 0))],
         out_specs=[whole((rows, D)), pl.BlockSpec((rows, D), lambda j: (0, j))],
         compiler_params=pltpu.CompilerParams(vmem_limit_bytes=VMEM_LIMIT),
     )(tokens, scale, shift, w_qkv)
@@ -916,40 +1007,36 @@
             unit = reduce_turns(
                 links, me, gw.at[i // 2], half.start, summed.at[i // 2, half], results.at[i // 2, half], lands[5 * i : 5 * i + 5]
             )
-            schedule += [(2 * (i // 2) + 1 + i % 2 + k, turn) for k, turn in enumerate(unit)]
+            schedule += timed([unit], 0, TAIL_REDUCE, 4 * (i // 2 + 1) + 2 * (i % 2))
         turns = placed(schedule)
-        host = Host(links, {h: t for h, t in turns.items() if h < 12}, 6, 2)
-        rest = [turns[h] for h in sorted(turns) if h >= 12]
+        host = Host(links, {h: t for h, t in turns.items() if h < 24}, 6, 4)
+        rest = [turns[h] for h in sorted(turns) if h >= 24]
         spread = factors_turns(links, me, factors, factor_group, factor_all)
     else:
         gw, gtok_ref, gscale_ref, gshift_ref, back = refs
-        host = Idle()
-
-    host.turn(0)
-
-    @pl.when(p < 3)
-    def _():
-        for r in range(D // 256):
-            value = tn(hidden_ref[:, r * 256 : r * 256 + 256], grad_ref[0]).astype(jnp.bfloat16)
-            for half in (0, 1):
-                gw[p if shared else 0, 2 * r + half] = value[half * 128 : half * 128 + 128]
-
-    def way_back(first):
-        for r in range(2):
-            here = pl.ds(first + r * (rows // 4), rows // 4)
-            part = nt(grad_ref[0, here, :], w_ref[...])
-
-            @pl.when(p == 3)
-            def _():
-                back[here, :] = part
-
-            @pl.when(p > 3)
-            def _():
-                back[here, :] += part
-
-    pl.when(p >= 3)(functools.partial(way_back, 0))
-    host.turn(1)
-    pl.when(p >= 3)(functools.partial(way_back, rows // 2))
+        host, rest = Idle(), []
+
+    def products(r):
+        value = tn(hidden_ref[:, r * 256 : r * 256 + 256], grad_ref[0]).astype(jnp.bfloat16)
+        for half in (0, 1):
+            gw[p if shared else 0, 2 * r + half] = value[half * 128 : half * 128 + 128]
+
+    def way_back(r):
+        here = pl.ds(r * (rows // 4), rows // 4)
+        part = nt(grad_ref[0, here, :], w_ref[0])
+
+        @pl.when(p == 3)
+        def _():
+            back[here, :] = part
+
+        @pl.when(p > 3)
+        def _():
+            back[here, :] += part
+
+    for r in range(4):
+        host.turn(r)
+        pl.when(p < 3)(functools.partial(products, r))
+        pl.when(p >= 3)(functools.partial(way_back, r))
 
     @pl.when(p == pl.num_programs(0) - 1)
     def _():
@@ -961,21 +1048,20 @@
             gscale_ref[pl.ds(u, 1), :] = jnp.sum(grad * normed, axis=0, keepdims=True)
             gtok_ref[at, :] = mid_ref[at, :] + norm_back(grad * (1.0 + scale_ref[pl.ds(u, 1), :]), normed, inverse)
 
-        loop(rows // UNIT, unit)
+        for quarter in range(4):
+            if quarter < len(rest):
+                run(rest[quarter])
+            loop(rows // UNIT // 4, lambda i: unit(quarter * (rows // UNIT // 4) + i))
         if shared:
             table = table_ref[...].astype(jnp.bfloat16)
             for i, ref in enumerate((gscale_ref, gshift_ref)):
-                whole, sums = ref[...], None
-                for _ in range(3):
-                    part = whole.astype(jnp.bfloat16)
-                    whole = whole - part.astype(jnp.float32)
-                    sums = nn(table, part) if sums is None else sums + nn(table, part)
-                factors[:, i * D : (i + 1) * D] = sums.astype(jnp.bfloat16)
-            for i in range(max(len(rest), len(spread))):
+                factors[:, i * D : (i + 1) * D] = exact(table, ref[...]).astype(jnp.bfloat16)
+            left = rest[4:]
+            for i in range(max(len(left), len(spread))):
                 if i < len(spread):
                     spread[i]()
-                if i < len(rest):
-                    run(rest[i])
+                if i < len(left):
+                    run(left[i])
 
     host.finish()
 
@@ -987,7 +1073,7 @@
     f32, b16 = jnp.float32, jnp.bfloat16
     block = pl.BlockSpec((1, rows, D), lambda p: (lax.rem(p, 3), 0, 0))
     inputs = [
-        (grad_proj, block), (hidden, whole), (w_qkv, pl.BlockSpec((D, D), lambda p: (0, jnp.maximum(p - 3, 0)))), (tokens, whole), (grad_mid, whole), (scale, units),
+        (grad_proj, block), (hidden, whole), (w_qkv, pl.BlockSpec((1, D, D), lambda p: (jnp.maximum(p - 3, 0), 0, 0))), (tokens, whole), (grad_mid, whole), (scale, units),
     ]
     outputs = [((rows, D), f32, whole), ((rows // UNIT, D), f32, units), ((rows // UNIT, D), f32, units)]
     scratch = [pltpu.VMEM((rows, D), f32)]
@@ -1025,9 +1111,9 @@
         packed = jnp.pad(packed, ((0, 16 - packed.shape[0]), (0, 0)))
         by_owner = feats.reshape(slots, n, 128).transpose(1, 0, 2)
         small = jnp.concatenate([jnp.broadcast_to(packed, (n, 16, 128)), by_owner], axis=1)
-        small_all, (full_mod, full_qkv) = gather_all(small, (w_mod, w_qkv))
+        small_all, full_qkv, hidden_attn, projected, per_unit = first_all(small, w_mod, w_qkv, tokens, unit_table)
         of_group = lax.dynamic_slice(small_all, (lax.axis_index("dp") * n, 0, 0), (n, 16, 128))
-        full_bmod, full_bout, full_bdown = of_group[:, :4].reshape(-1), of_group[:, 4].reshape(1, -1), of_group[:, 9].reshape(1, -1)
+        full_bout, full_bdown = of_group[:, 4].reshape(1, -1), of_group[:, 9].reshape(1, -1)
         full_bup = of_group[:, 5:9].transpose(1, 0, 2).reshape(FF_BLOCKS, 1, -1)
         every_feats = small_all[:, 16:].reshape(sizes[0], n, slots, 128).transpose(1, 0, 2, 3).reshape(-1, 128)
     else:
@@ -1035,11 +1121,12 @@
         full_bout, full_bdown, full_bup = full_bout[None], full_bdown[None], full_bup.reshape(FF_BLOCKS, 1, -1)
         every_feats = lax.all_gather(feats, ("dp", "fsdp"), axis=0, tiled=True)
         every_feats = lax.dynamic_slice(every_feats, (0, lax.axis_index("fsdp") * (D // n)), (every_feats.shape[0], D // n))
-    modulation = jnp.dot(feats, full_mod, preferred_element_type=jnp.float32) + full_bmod
-    per_unit = jnp.dot(unit_table, modulation, precision=HIGHEST)
-    scale_one, shift_one, scale_two, shift_two = [per_unit[:, i * D : (i + 1) * D] for i in range(4)]
+        modulation = jnp.dot(feats, full_mod, preferred_element_type=jnp.float32) + full_bmod
+        per_unit = jnp.dot(unit_table, modulation, precision=HIGHEST)
+        full_qkv = full_qkv.reshape(D, 3, D).transpose(1, 0, 2)
+        hidden_attn, projected = project_in(tokens, per_unit[:, :D], per_unit[:, D : 2 * D], full_qkv)
+    scale_one, _, scale_two, shift_two = [per_unit[:, i * D : (i + 1) * D] for i in range(4)]
     live_units = jnp.broadcast_to(live[:, None], (rows // UNIT, D))
-    hidden_attn, projected = project_in(tokens, scale_one, shift_one, full_qkv)
     query_lanes, key_lanes = attention_lanes(jnp.repeat(segment, UNIT), slots)
     if own:
         ups = w_up.reshape(-1, n, FF_BLOCKS, 128).transpose(2, 0, 1, 3).reshape(FF_BLOCKS, 1, -1, D)

time: 553 us -> 508 us (0.919)
  Pallas kernels: 499 us -> 457 us
    pallas_call x7, Pallas kernels: 483 us -> 457 us  [call(): return made(*[array for array, _ in inputs])]
    pallas_call x1 -> x0, Pallas kernels: 15.5 us -> none  [project_in(): pl.pallas_call(head_kernel, grid=(3,), out_shape=[jax.ShapeDtypeStruct((r...]
where the time goes in v3:
time: 508 us; the launch traced here: 501 us
  Pallas kernels  457 us (90%)
  local copies, waits for them, and re-layouts  23.6 us (5%)
  other arithmetic  14.3 us (3%)
    pallas_call x7, Pallas kernels, call(): return made(*[array for array, _ in inputs])  457 us

profile of v3, /device:TPU:0, one launch (start us, length us, event | category | flops | bytes accessed | tf_op | source)
XLA Modules:
  0.0 500.5 jit_solution(7642166173248048737)
XLA Ops:
  0.7 0.7 select_reduce_fusion
  1.4 0.7 convert_bitcast_fusion.1
  2.1 0.2 convert_reduce_fusion.1
  2.3 0.7 maximum_bitcast_fusion.1
  3.2 0.7 fusion.9
  3.9 0.2 fusion.6
  4.1 0.6 pad_maximum_fusion.4.small
  4.7 0.7 broadcast_in_dim.70.live_ref
  5.4 0.9 select_convert_fusion.kl_ref
  6.3 0.9 fusion.1.ql_ref
  7.2 1.8 reshape.137
  9.2 0.5 reshape.138
  9.7 0.6 copy-done.3
  10.3 1.2 pad_maximum_fusion.3
  11.4 1.2 pad_maximum_fusion.2.refs_0_
  12.6 79.6 %shard_map.212 = (bf16[32,32,128]{2,1,0:T(8,128)(2,1)}, bf16[3,1024,1024]{2,1,0:T(8,128)(2,1)}, bf16[1024,1024]{1,0:T(8,128)(2,1)}, bf16[1024,3072]{1,0:T(8,128)(2,1)}, f32[16,4096]{1,0:T(8,128)}) custom-call(bf16[8,32,128]{2,1,0:T(8,128)(2,1)} %pad_maximum_fusion.4.small, bf16[128,4096]{1,0:T(8,128)(2,1)} %wmod_ref.1, bf16[128,3072]{1,0:T(8,128)(2,1)} %wqkv.1, ...), custom_call_target="tpu_custom_call" | custom-call | tf_op jit(solution)/shard_map/pallas_call | solution.py:476
  92.2 1.6 fusion.13
  93.8 1.3 dynamic-slice_bitcast_fusion.1
  95.1 0.8 dynamic-slice_bitcast_fusion
  95.9 0.9 slice.64
  96.8 0.6 copy.38.bup_ref
  97.5 68.2 %shard_map.213 = (bf16[1024,1024]{1,0:T(8,128)(2,1)}, bf16[16,1024,128]{2,1,0:T(8,128)(2,1)}, bf16[5,1024,1024]{2,1,0:T(8,128)(2,1)}) custom-call(bf16[1024,3072]{1,0:T(8,128)(2,1)} %get-tuple-element.42.q_ref.k_ref.v_ref, bf16[1024,3072]{1,0:T(8,128)(2,1)} %get-tuple-element.42.q_ref.k_ref.v_ref, bf16[1024,3072]{1,0:T(8,128)(2,1)} %get-tuple-element.42.q_ref.k_ref.v_ref, ...), custom_call_target="tpu_custom_call" | custom-call | tf_op jit(solution)/shard_map/pallas_call | solution.py:476
  165.6 8.9 %shard_map.214 = (f32[1024,1024]{1,0:T(8,128)}, bf16[1024,1024]{1,0:T(8,128)(2,1)}, bf16[1024,1024]{1,0:T(8,128)(2,1)}, f32[1,1024]{1,0:T(1,128)}) custom-call(bf16[1024,1024]{1,0:T(8,128)(2,1)} %get-tuple-element.43.attn_ref.out_ref, bf16[1024,1024]{1,0:T(8,128)(2,1)} %tok_ref.5, bf16[1024,1024]{1,0:T(8,128)(2,1)} %cot_ref.3, ...), custom_call_target="tpu_custom_call" | custom-call | tf_op jit(solution)/shard_map/pallas_call | solution.py:476
  174.5 116.6 %shard_map.215 = (f32[1024,1024]{1,0:T(8,128)}, f32[1024,1024]{1,0:T(8,128)}, f32[4,1,1024]{2,1,0:T(1,128)}, bf16[2,2,8,128,1024]{4,3,2,1,0:T(8,128)(2,1)}, bf16[4,128,1024]{2,1,0:T(8,128)(2,1)}) custom-call(bf16[1024,1024]{1,0:T(8,128)(2,1)} %get-tuple-element.48.hidden, bf16[1024,1024]{1,0:T(8,128)(2,1)} %get-tuple-element.49.two, ...), custom_call_target="tpu_custom_call" | custom-call | tf_op jit(solution)/shard_map/pallas_call | solution.py:476
  291.1 15.2 %shard_map.216 = (bf16[1024,1024]{1,0:T(8,128)(2,1)}, f32[1024,1024]{1,0:T(8,128)}, bf16[1024,1024]{1,0:T(8,128)(2,1)}, bf16[1,8,128,1024]{3,2,1,0:T(8,128)(2,1)...) custom-call(f32[1024,1024]{1,0:T(8,128)} %get-tuple-element.47.middle_ref, ...), custom_call_target="tpu_custom_call" | custom-call | tf_op jit(solution)/shard_map/pallas_call | solution.py:476
  306.4 1.3 select_maximum_fusion.refs_2_
  307.7 1.8 convolution_convert_fusion.refs_3_
  309.5 86.8 %shard_map.217 = (bf16[3,1024,1024]{2,1,0:T(8,128)(2,1)}, bf16[5,128,1024]{2,1,0:T(8,128)(2,1)}, f32[32,8,128]{2,1,0:T(8,128)}, bf16[64,2048]{1,0:T(8,128)(2,1)}, bf16[512,2048]{1,0:T(8,128)(2,1)}) custom-call(bf16[1024,3072]{1,0:T(8,128)(2,1)} %get-tuple-element.42.q_ref.k_ref.v_ref, bf16[1024,3072]{1,0:T(8,128)(2,1)} %get-tuple-element.42.q_ref.k_ref.v_ref, ...), custom_call_target="tpu_custom_call" | custom-call | tf_op jit(solution)/shard_map/pallas_call | solution.py:476
  396.3 81.6 %shard_map.218 = (bf16[3,128,1024]{2,1,0:T(8,128)(2,1)}, f32[1024,1024]{1,0:T(8,128)}, f32[16,1024]{1,0:T(8,128)}, f32[16,1024]{1,0:T(8,128)}, bf16[64,2048]{1,0:T(8,128)(2,1)}, /*index=5*/bf16[512,2048]{1,0:T(8,128)(2,1)}) custom-call(bf16[3,1024,1024]{2,1,0:T(8,128)(2,1)} %get-tuple-element.62.grad_ref, bf16[1024,1024]{1,0:T(8,128)(2,1)} %get-tuple-element.63.hidden_ref, ...), custom_call_target="tpu_custom_call" | custom-call | tf_op jit(solution)/shard_map/pallas_call | solution.py:476
  478.0 2.1 convert_reduce_fusion
  480.1 2.1 fusion.14
  482.1 0.5 fusion.15
  482.6 1.5 pad_maximum_fusion.1
  484.2 0.5 slice_bitcast_fusion.2
  484.7 0.6 slice_bitcast_fusion.1
  485.3 0.2 convert_bitcast_fusion
  485.4 0.5 copy.41
  485.9 1.6 copy.43
  487.5 0.2 slice.75
  487.8 0.3 convert_element_type.60
  488.1 0.8 slice_bitcast_fusion
  489.0 0.2 convert_element_type.61
  489.3 0.6 pad_maximum_fusion
  489.8 1.7 fusion.12
  491.6 0.5 copy.44
  492.1 1.4 copy.47
  493.4 1.9 reshape.150
  495.3 4.8 copy.50
  (32 shorter events, 0.5 us)
Async XLA Ops:
  9.0 1.2 copy-start.3
  10.3 1.2 copy-start.5
  291.1 15.3 %copy-start.7 = (f32[4,1,1024]{2,1,0:T(1,128)S(1)}, f32[4,1,1024]{2,1,0:T(1,128)}, u32[]{:S(2)}) copy-start(f32[4,1,1024]{2,1,0:T(1,128)} %get-tuple-element.58) | copy-start | bytes 49156
  291.1 15.3 %copy-start.8 = (f32[1,1024]{1,0:T(1,128)S(1)}, f32[1,1024]{1,0:T(1,128)}, u32[]{:S(2)}) copy-start(f32[1,1024]{1,0:T(1,128)} %get-tuple-element.59) | copy-start | bytes 12292
  477.9 4.2 copy-start.1
  482.6 1.5 copy-start.6
  482.6 2.6 copy-start.4
  485.9 1.6 copy-start
  487.8 1.2 copy-start.2

commit v4 on v3

--- a/solution.py
+++ b/solution.py
@@ -19,11 +19,11 @@
 EARLY = 2
 LSE_LANE = 24
 ATTEND_GATHER = (3, (0, 4, 8, 12, 15))
-MLP_GATHER = (3, (0, 5, 10, 15, 18))
-MLP_REDUCE = (20, 4, (0, 2, 6, 11, 16, 19, 21))
+MLP_GATHER = ((0, 3, 6, 9, 12, 15, 19, 23), (0, 7, 13, 19, 22))
+MLP_REDUCE = ((18, 22, 26, 30, 34, 38, 42, 46), (0, 3, 8, 14, 20, 24, 26))
 BACK_REDUCE = (2.6, (0, 2, 5, 8, 11, 13, 15))
 BACK_FACTORS = (1, 4, 8, 12, 16, 19)
-TAIL_REDUCE = (0, 2, 5, 9, 13, 16, 18)
+TAIL_REDUCE = (0, 2, 6, 11, 16, 19, 21)
 VMEM_LIMIT = 62 * 2**20
 HIGHEST = lax.Precision.HIGHEST
 MESH = pl.DeviceIdType.MESH
@@ -441,7 +441,8 @@
 
 
 def timed(units, every, lags, first=0):
-    return [(int(first + every * i) + lag, turn) for i, unit in enumerate(units) for lag, turn in zip(lags, unit)]
+    starts = every if isinstance(every, tuple) else [int(first + every * i) for i in range(len(units))]
+    return [(start + lag, turn) for start, unit in zip(starts, units) for lag, turn in zip(lags, unit)]
 
 
 def placed(schedule):
@@ -814,8 +815,7 @@
                     links, me, made.at[b % slots, w], half.start, summed.at[2 * b + w, half], results.at[2 * b + w, half], lands[5 * i : 5 * i + 5]
                 )
             )
-        first, every, lags = MLP_REDUCE
-        schedule = timed(gathers, *MLP_GATHER) + timed(reduces, every, lags, first)
+        schedule = timed(gathers, *MLP_GATHER) + timed(reduces, *MLP_REDUCE)
         host = Host(links, placed(schedule), FF_BLOCKS, 16)
     else:
         host = Idle()
@@ -994,7 +994,7 @@
     )(tokens, scale, shift, w_qkv)
 
 
-def tail_kernel(shared, grad_ref, hidden_ref, w_ref, tok_ref, mid_ref, scale_ref, *refs):
+def tail_kernel(shared, grad_ref, hidden_ref, w_ref, tok_ref, scale_ref, *refs):
     p = pl.program_id(0)
     rows = tok_ref.shape[0]
     if shared:
@@ -1046,7 +1046,8 @@
             grad = back[at, :]
             gshift_ref[pl.ds(u, 1), :] = jnp.sum(grad, axis=0, keepdims=True)
             gscale_ref[pl.ds(u, 1), :] = jnp.sum(grad * normed, axis=0, keepdims=True)
-            gtok_ref[at, :] = mid_ref[at, :] + norm_back(grad * (1.0 + scale_ref[pl.ds(u, 1), :]), normed, inverse)
+            passed = norm_back(grad * (1.0 + scale_ref[pl.ds(u, 1), :]), normed, inverse)
+            gtok_ref[at, :] = passed.astype(jnp.bfloat16)
 
         for quarter in range(4):
             if quarter < len(rest):
@@ -1066,16 +1067,16 @@
     host.finish()
 
 
-def project_back(grad_proj, hidden, w_qkv, tokens, grad_mid, scale, table=None):
+def project_back(grad_proj, hidden, w_qkv, tokens, scale, table=None):
     rows = tokens.shape[0]
     once = lambda shape: pl.BlockSpec(shape, lambda p: (0, 0), pipeline_mode=pl.Buffered(1))
     units, whole = once((rows // UNIT, D)), once((rows, D))
     f32, b16 = jnp.float32, jnp.bfloat16
     block = pl.BlockSpec((1, rows, D), lambda p: (lax.rem(p, 3), 0, 0))
     inputs = [
-        (grad_proj, block), (hidden, whole), (w_qkv, pl.BlockSpec((1, D, D), lambda p: (jnp.maximum(p - 3, 0), 0, 0))), (tokens, whole), (grad_mid, whole), (scale, units),
+        (grad_proj, block), (hidden, whole), (w_qkv, pl.BlockSpec((1, D, D), lambda p: (jnp.maximum(p - 3, 0), 0, 0))), (tokens, whole), (scale, units),
     ]
-    outputs = [((rows, D), f32, whole), ((rows // UNIT, D), f32, units), ((rows // UNIT, D), f32, units)]
+    outputs = [((rows, D), b16, whole), ((rows // UNIT, D), f32, units), ((rows // UNIT, D), f32, units)]
     scratch = [pltpu.VMEM((rows, D), f32)]
     shared = table is not None
     if shared:
@@ -1160,9 +1161,10 @@
         sum_bout, sum_bup, sum_bdown = total[0], total[1:5].reshape(-1), total[5]
     else:
         grad_proj = attend_back(projected, key_lanes, asked, attn_out, grad_attn)[0]
-    qkv_grads, grad_tokens, grad_scale_one, grad_shift_one, *factors = project_back(
-        grad_proj, hidden_attn, full_qkv, tokens, grad_mid, scale_one, unit_table.T if own else None
+    qkv_grads, through_norm, grad_scale_one, grad_shift_one, *factors = project_back(
+        grad_proj, hidden_attn, full_qkv, tokens, scale_one, unit_table.T if own else None
     )
+    grad_tokens = grad_mid + through_norm.astype(jnp.float32)
     if own:
         mod_one = factors[1]
     else:

time: 508 us -> 498 us (0.980)
  Pallas kernels: 457 us -> 448 us
    pallas_call x7, Pallas kernels: 457 us -> 448 us  [call(): return made(*[array for array, _ in inputs])]
    add x0 -> x1, other arithmetic: none -> 6.08 us  [local(): grad_tokens = grad_mid + through_norm.astype(jnp.float32)]
where the time goes in v4:
time: 498 us; the launch traced here: 490 us
  Pallas kernels  448 us (90%)
  other arithmetic  19 us (4%)
  local copies, waits for them, and re-layouts  18.8 us (4%)
    pallas_call x7, Pallas kernels, call(): return made(*[array for array, _ in inputs])  448 us

profile of v4, /device:TPU:0, one launch (start us, length us, event | category | flops | bytes accessed | tf_op | source)
XLA Modules:
  0.0 489.8 jit_solution(10345255811049678135)
XLA Ops:
  0.7 0.7 select_reduce_fusion
  1.4 0.7 convert_bitcast_fusion.1
  2.1 0.2 convert_reduce_fusion.1
  2.3 0.7 maximum_bitcast_fusion.1
  3.2 0.7 fusion.9
  3.9 0.2 fusion.6
  4.1 0.6 pad_maximum_fusion.4.small
  4.7 0.7 broadcast_in_dim.70.live_ref
  5.4 0.9 select_convert_fusion.kl_ref
  6.3 0.9 fusion.1.ql_ref
  7.2 1.8 reshape.137
  9.2 0.5 reshape.138
  9.7 0.6 copy-done.4
  10.3 1.2 pad_maximum_fusion.3
  11.4 1.2 pad_maximum_fusion.2.refs_0_
  12.6 79.6 %shard_map.212 = (bf16[32,32,128]{2,1,0:T(8,128)(2,1)}, bf16[3,1024,1024]{2,1,0:T(8,128)(2,1)}, bf16[1024,1024]{1,0:T(8,128)(2,1)}, bf16[1024,3072]{1,0:T(8,128)(2,1)}, f32[16,4096]{1,0:T(8,128)}) custom-call(bf16[8,32,128]{2,1,0:T(8,128)(2,1)} %pad_maximum_fusion.4.small, bf16[128,4096]{1,0:T(8,128)(2,1)} %wmod_ref.1, bf16[128,3072]{1,0:T(8,128)(2,1)} %wqkv.1, ...), custom_call_target="tpu_custom_call" | custom-call | tf_op jit(solution)/shard_map/pallas_call | solution.py:477
  92.2 1.6 fusion.13
  93.8 1.3 dynamic-slice_bitcast_fusion.1
  95.1 0.8 dynamic-slice_bitcast_fusion
  95.9 0.9 slice.64
  96.8 0.6 copy.38.bup_ref
  97.4 68.2 %shard_map.213 = (bf16[1024,1024]{1,0:T(8,128)(2,1)}, bf16[16,1024,128]{2,1,0:T(8,128)(2,1)}, bf16[5,1024,1024]{2,1,0:T(8,128)(2,1)}) custom-call(bf16[1024,3072]{1,0:T(8,128)(2,1)} %get-tuple-element.42.q_ref.k_ref.v_ref, bf16[1024,3072]{1,0:T(8,128)(2,1)} %get-tuple-element.42.q_ref.k_ref.v_ref, bf16[1024,3072]{1,0:T(8,128)(2,1)} %get-tuple-element.42.q_ref.k_ref.v_ref, ...), custom_call_target="tpu_custom_call" | custom-call | tf_op jit(solution)/shard_map/pallas_call | solution.py:477
  165.6 8.9 %shard_map.214 = (f32[1024,1024]{1,0:T(8,128)}, bf16[1024,1024]{1,0:T(8,128)(2,1)}, bf16[1024,1024]{1,0:T(8,128)(2,1)}, f32[1,1024]{1,0:T(1,128)}) custom-call(bf16[1024,1024]{1,0:T(8,128)(2,1)} %get-tuple-element.43.attn_ref.out_ref, bf16[1024,1024]{1,0:T(8,128)(2,1)} %tok_ref.5, bf16[1024,1024]{1,0:T(8,128)(2,1)} %cot_ref.3, ...), custom_call_target="tpu_custom_call" | custom-call | tf_op jit(solution)/shard_map/pallas_call | solution.py:477
  174.5 111.8 %shard_map.215 = (f32[1024,1024]{1,0:T(8,128)}, f32[1024,1024]{1,0:T(8,128)}, f32[4,1,1024]{2,1,0:T(1,128)}, bf16[2,2,8,128,1024]{4,3,2,1,0:T(8,128)(2,1)}, bf16[4,128,1024]{2,1,0:T(8,128)(2,1)}) custom-call(bf16[1024,1024]{1,0:T(8,128)(2,1)} %get-tuple-element.48.hidden, bf16[1024,1024]{1,0:T(8,128)(2,1)} %get-tuple-element.49.two, ...), custom_call_target="tpu_custom_call" | custom-call | tf_op jit(solution)/shard_map/pallas_call | solution.py:477
  286.3 15.2 %shard_map.216 = (bf16[1024,1024]{1,0:T(8,128)(2,1)}, f32[1024,1024]{1,0:T(8,128)}, bf16[1024,1024]{1,0:T(8,128)(2,1)}, bf16[1,8,128,1024]{3,2,1,0:T(8,128)(2,1)...) custom-call(f32[1024,1024]{1,0:T(8,128)} %get-tuple-element.47.middle_ref, ...), custom_call_target="tpu_custom_call" | custom-call | tf_op jit(solution)/shard_map/pallas_call | solution.py:477
  301.6 1.3 select_maximum_fusion.refs_2_
  302.9 1.8 convolution_convert_fusion.refs_3_
  304.7 87.8 %shard_map.217 = (bf16[3,1024,1024]{2,1,0:T(8,128)(2,1)}, bf16[5,128,1024]{2,1,0:T(8,128)(2,1)}, f32[32,8,128]{2,1,0:T(8,128)}, bf16[64,2048]{1,0:T(8,128)(2,1)}, bf16[512,2048]{1,0:T(8,128)(2,1)}) custom-call(bf16[1024,3072]{1,0:T(8,128)(2,1)} %get-tuple-element.42.q_ref.k_ref.v_ref, bf16[1024,3072]{1,0:T(8,128)(2,1)} %get-tuple-element.42.q_ref.k_ref.v_ref, ...), custom_call_target="tpu_custom_call" | custom-call | tf_op jit(solution)/shard_map/pallas_call | solution.py:477
  392.6 76.3 %shard_map.218 = (bf16[3,128,1024]{2,1,0:T(8,128)(2,1)}, bf16[1024,1024]{1,0:T(8,128)(2,1)}, f32[16,1024]{1,0:T(8,128)}, f32[16,1024]{1,0:T(8,128)}, bf16[64,204...) custom-call(bf16[3,1024,1024]{2,1,0:T(8,128)(2,1)} %get-tuple-element.63.grad_ref, ...), custom_call_target="tpu_custom_call" | custom-call | tf_op jit(solution)/shard_map/pallas_call | solution.py:477
  468.9 6.1 %convert_add_fusion = f32[1024,1024]{1,0:T(8,128)} fusion(f32[1024,1024]{1,0:T(8,128)} %get-tuple-element.53, bf16[1024,1024]{1,0:T(8,128)(2,1)} %get-tuple-element.66), kind=kLoop, calls=%fused_computation.1 | loop fusion | flops 2097152 | bytes 10485760 | tf_op jit(solution)/shard_map/add | solution.py:1167
  475.0 0.8 convert_reduce_fusion
  475.7 0.5 fusion.14
  476.2 0.5 fusion.15
  476.7 1.5 pad_maximum_fusion.1
  478.2 0.5 slice_bitcast_fusion.2
  478.7 0.6 slice_bitcast_fusion.1
  479.3 0.2 convert_bitcast_fusion
  479.5 0.5 copy.41
  480.0 1.6 copy.43
  481.6 0.2 slice.75
  481.8 0.3 convert_element_type.64
  482.2 0.8 slice_bitcast_fusion
  483.1 0.2 convert_element_type.65
  483.3 0.6 pad_maximum_fusion
  483.9 1.7 fusion.12
  485.6 0.5 copy.44
  486.1 1.4 copy.47
  487.5 1.9 reshape.150
  (34 shorter events, 0.5 us)
Async XLA Ops:
  9.0 1.2 copy-start.4
  10.3 1.2 copy-start.6
  286.3 15.3 %copy-start.8 = (f32[4,1,1024]{2,1,0:T(1,128)S(1)}, f32[4,1,1024]{2,1,0:T(1,128)}, u32[]{:S(2)}) copy-start(f32[4,1,1024]{2,1,0:T(1,128)} %get-tuple-element.59) | copy-start | bytes 49156
  286.3 15.3 %copy-start.9 = (f32[1,1024]{1,0:T(1,128)S(1)}, f32[1,1024]{1,0:T(1,128)}, u32[]{:S(2)}) copy-start(f32[1,1024]{1,0:T(1,128)} %get-tuple-element.60) | copy-start | bytes 12292
  468.8 6.1 %copy-start.1 = (bf16[512,2048]{1,0:T(8,128)(2,1)S(1)}, bf16[512,2048]{1,0:T(8,128)(2,1)}, u32[]{:S(2)}) copy-start(bf16[512,2048]{1,0:T(8,128)(2,1)} %get-tuple-element.68) | copy-start | bytes 6291460
  468.9 6.1 %copy-start.2 = (bf16[512,2048]{1,0:T(8,128)(2,1)S(1)}, bf16[512,2048]{1,0:T(8,128)(2,1)}, u32[]{:S(2)}) copy-start(bf16[512,2048]{1,0:T(8,128)(2,1)} %get-tuple-element.67) | copy-start | bytes 6291460
  476.7 1.5 copy-start.7
  476.7 2.6 copy-start.5
  480.0 1.6 copy-start
  481.8 1.2 copy-start.3

commit v5 on v4

--- a/solution.py
+++ b/solution.py
@@ -18,7 +18,7 @@
 FF_BLOCKS = 4
 EARLY = 2
 LSE_LANE = 24
-ATTEND_GATHER = (3, (0, 4, 8, 12, 15))
+ATTEND_GATHER = (2.5, (0, 4, 8, 11, 13))
 MLP_GATHER = ((0, 3, 6, 9, 12, 15, 19, 23), (0, 7, 13, 19, 22))
 MLP_REDUCE = ((18, 22, 26, 30, 34, 38, 42, 46), (0, 3, 8, 14, 20, 24, 26))
 BACK_REDUCE = (2.6, (0, 2, 5, 8, 11, 13, 15))

time: 498 us -> 494 us (level)
  no operation moved by 1% of the time
where the time goes in v5:
time: 494 us; the launch traced here: 486 us
  Pallas kernels  444 us (90%)
  other arithmetic  19 us (4%)
  local copies, waits for them, and re-layouts  18.8 us (4%)
    pallas_call x7, Pallas kernels, call(): return made(*[array for array, _ in inputs])  444 us

profile of v5, /device:TPU:0, one launch (start us, length us, event | category | flops | bytes accessed | tf_op | source)
XLA Modules:
  0.0 486.1 jit_solution(12897857245578161897)
XLA Ops:
  0.7 0.7 select_reduce_fusion
  1.4 0.7 convert_bitcast_fusion.1
  2.1 0.2 convert_reduce_fusion.1
  2.3 0.7 maximum_bitcast_fusion.1
  3.2 0.7 fusion.9
  3.9 0.2 fusion.6
  4.1 0.6 pad_maximum_fusion.4.small
  4.7 0.7 broadcast_in_dim.70.live_ref
  5.4 0.9 select_convert_fusion.kl_ref
  6.3 0.9 fusion.1.ql_ref
  7.2 1.8 reshape.137
  9.2 0.5 reshape.138
  9.7 0.6 copy-done.4
  10.3 1.2 pad_maximum_fusion.3
  11.4 1.2 pad_maximum_fusion.2.refs_0_
  12.6 79.6 %shard_map.212 = (bf16[32,32,128]{2,1,0:T(8,128)(2,1)}, bf16[3,1024,1024]{2,1,0:T(8,128)(2,1)}, bf16[1024,1024]{1,0:T(8,128)(2,1)}, bf16[1024,3072]{1,0:T(8,128)(2,1)}, f32[16,4096]{1,0:T(8,128)}) custom-call(bf16[8,32,128]{2,1,0:T(8,128)(2,1)} %pad_maximum_fusion.4.small, bf16[128,4096]{1,0:T(8,128)(2,1)} %wmod_ref.1, bf16[128,3072]{1,0:T(8,128)(2,1)} %wqkv.1, ...), custom_call_target="tpu_custom_call" | custom-call | tf_op jit(solution)/shard_map/pallas_call | solution.py:477
  92.2 1.6 fusion.13
  93.8 1.3 dynamic-slice_bitcast_fusion.1
  95.1 0.8 dynamic-slice_bitcast_fusion
  95.9 0.9 slice.64
  96.8 0.6 copy.38.bup_ref
  97.4 63.5 %shard_map.213 = (bf16[1024,1024]{1,0:T(8,128)(2,1)}, bf16[16,1024,128]{2,1,0:T(8,128)(2,1)}, bf16[5,1024,1024]{2,1,0:T(8,128)(2,1)}) custom-call(bf16[1024,3072]{1,0:T(8,128)(2,1)} %get-tuple-element.42.q_ref.k_ref.v_ref, bf16[1024,3072]{1,0:T(8,128)(2,1)} %get-tuple-element.42.q_ref.k_ref.v_ref, bf16[1024,3072]{1,0:T(8,128)(2,1)} %get-tuple-element.42.q_ref.k_ref.v_ref, ...), custom_call_target="tpu_custom_call" | custom-call | tf_op jit(solution)/shard_map/pallas_call | solution.py:477
  161.0 8.9 %shard_map.214 = (f32[1024,1024]{1,0:T(8,128)}, bf16[1024,1024]{1,0:T(8,128)(2,1)}, bf16[1024,1024]{1,0:T(8,128)(2,1)}, f32[1,1024]{1,0:T(1,128)}) custom-call(bf16[1024,1024]{1,0:T(8,128)(2,1)} %get-tuple-element.43.attn_ref.out_ref, bf16[1024,1024]{1,0:T(8,128)(2,1)} %tok_ref.5, bf16[1024,1024]{1,0:T(8,128)(2,1)} %cot_ref.3, ...), custom_call_target="tpu_custom_call" | custom-call | tf_op jit(solution)/shard_map/pallas_call | solution.py:477
  169.9 112.8 %shard_map.215 = (f32[1024,1024]{1,0:T(8,128)}, f32[1024,1024]{1,0:T(8,128)}, f32[4,1,1024]{2,1,0:T(1,128)}, bf16[2,2,8,128,1024]{4,3,2,1,0:T(8,128)(2,1)}, bf16[4,128,1024]{2,1,0:T(8,128)(2,1)}) custom-call(bf16[1024,1024]{1,0:T(8,128)(2,1)} %get-tuple-element.48.hidden, bf16[1024,1024]{1,0:T(8,128)(2,1)} %get-tuple-element.49.two, ...), custom_call_target="tpu_custom_call" | custom-call | tf_op jit(solution)/shard_map/pallas_call | solution.py:477
  282.7 15.2 %shard_map.216 = (bf16[1024,1024]{1,0:T(8,128)(2,1)}, f32[1024,1024]{1,0:T(8,128)}, bf16[1024,1024]{1,0:T(8,128)(2,1)}, bf16[1,8,128,1024]{3,2,1,0:T(8,128)(2,1)...) custom-call(f32[1024,1024]{1,0:T(8,128)} %get-tuple-element.47.middle_ref, ...), custom_call_target="tpu_custom_call" | custom-call | tf_op jit(solution)/shard_map/pallas_call | solution.py:477
  298.0 1.3 select_maximum_fusion.refs_2_
  299.3 1.8 convolution_convert_fusion.refs_3_
  301.2 87.7 %shard_map.217 = (bf16[3,1024,1024]{2,1,0:T(8,128)(2,1)}, bf16[5,128,1024]{2,1,0:T(8,128)(2,1)}, f32[32,8,128]{2,1,0:T(8,128)}, bf16[64,2048]{1,0:T(8,128)(2,1)}, bf16[512,2048]{1,0:T(8,128)(2,1)}) custom-call(bf16[1024,3072]{1,0:T(8,128)(2,1)} %get-tuple-element.42.q_ref.k_ref.v_ref, bf16[1024,3072]{1,0:T(8,128)(2,1)} %get-tuple-element.42.q_ref.k_ref.v_ref, ...), custom_call_target="tpu_custom_call" | custom-call | tf_op jit(solution)/shard_map/pallas_call | solution.py:477
  388.9 76.3 %shard_map.218 = (bf16[3,128,1024]{2,1,0:T(8,128)(2,1)}, bf16[1024,1024]{1,0:T(8,128)(2,1)}, f32[16,1024]{1,0:T(8,128)}, f32[16,1024]{1,0:T(8,128)}, bf16[64,204...) custom-call(bf16[3,1024,1024]{2,1,0:T(8,128)(2,1)} %get-tuple-element.63.grad_ref, ...), custom_call_target="tpu_custom_call" | custom-call | tf_op jit(solution)/shard_map/pallas_call | solution.py:477
  465.2 6.1 %convert_add_fusion = f32[1024,1024]{1,0:T(8,128)} fusion(f32[1024,1024]{1,0:T(8,128)} %get-tuple-element.53, bf16[1024,1024]{1,0:T(8,128)(2,1)} %get-tuple-element.66), kind=kLoop, calls=%fused_computation.1 | loop fusion | flops 2097152 | bytes 10485760 | tf_op jit(solution)/shard_map/add | solution.py:1167
  471.3 0.8 convert_reduce_fusion
  472.1 0.5 fusion.14
  472.5 0.5 fusion.15
  473.0 1.5 pad_maximum_fusion.1
  474.5 0.5 slice_bitcast_fusion.2
  475.1 0.6 slice_bitcast_fusion.1
  475.6 0.2 convert_bitcast_fusion
  475.8 0.5 copy.41
  476.3 1.6 copy.43
  477.9 0.2 slice.75
  478.2 0.3 convert_element_type.64
  478.5 0.8 slice_bitcast_fusion
  479.4 0.2 convert_element_type.65
  479.6 0.6 pad_maximum_fusion
  480.2 1.7 fusion.12
  482.0 0.5 copy.44
  482.5 1.4 copy.47
  483.8 1.9 reshape.150
  (34 shorter events, 0.5 us)
Async XLA Ops:
  9.0 1.2 copy-start.4
  10.3 1.2 copy-start.6
  282.7 15.3 %copy-start.8 = (f32[4,1,1024]{2,1,0:T(1,128)S(1)}, f32[4,1,1024]{2,1,0:T(1,128)}, u32[]{:S(2)}) copy-start(f32[4,1,1024]{2,1,0:T(1,128)} %get-tuple-element.59) | copy-start | bytes 49156
  282.7 15.3 %copy-start.9 = (f32[1,1024]{1,0:T(1,128)S(1)}, f32[1,1024]{1,0:T(1,128)}, u32[]{:S(2)}) copy-start(f32[1,1024]{1,0:T(1,128)} %get-tuple-element.60) | copy-start | bytes 12292
  465.2 6.1 %copy-start.1 = (bf16[512,2048]{1,0:T(8,128)(2,1)S(1)}, bf16[512,2048]{1,0:T(8,128)(2,1)}, u32[]{:S(2)}) copy-start(bf16[512,2048]{1,0:T(8,128)(2,1)} %get-tuple-element.68) | copy-start | bytes 6291460
  465.2 6.1 %copy-start.2 = (bf16[512,2048]{1,0:T(8,128)(2,1)S(1)}, bf16[512,2048]{1,0:T(8,128)(2,1)}, u32[]{:S(2)}) copy-start(bf16[512,2048]{1,0:T(8,128)(2,1)} %get-tuple-element.67) | copy-start | bytes 6291460
  473.0 1.5 copy-start.7
  473.0 2.6 copy-start.5
  476.3 1.6 copy-start
  478.2 1.2 copy-start.3
